TPU v7x, 256 devices: a whole 4x4x8 slice. The times are simulated.
256 devices in a mesh: tm: 8 (over z_hi, core), row: 2 (over z_lo), col: 16 (over y, x).
Axes of the slice: x: 4, y: 4, z: 8 (z_hi: 4, z_lo: 2; z = z_hi * 2 + z_lo), core: 2. Of those that a mesh axis runs over, the one named last changes fastest.
Arguments:
- latent: bfloat16 [16, 16, 128, 384], P('tm', 'row', 'col'), may hold values from -6 to 6
- grad_out: bfloat16 [16, 16, 128, 384], P('tm', 'row', 'col'), may hold values from -6 to 6
- norm_gain: float32 [384], replicated, may hold values from 0.1 to 1.9
- w_query: bfloat16 [384, 384], replicated, may hold values from -0.3125 to 0.3125
- w_key: bfloat16 [384, 384], replicated, may hold values from -0.3125 to 0.3125
- w_value: bfloat16 [384, 384], replicated, may hold values from -0.3125 to 0.3125
- w_out: bfloat16 [384, 384], replicated, may hold values from -2.5 to 2.5
- gain_one: float32 [384], replicated, may hold values from 0.1 to 1.9
- gain_two: float32 [384], replicated, may hold values from 0.1 to 1.9
- kernel_one: bfloat16 [3, 3, 3, 384, 384], P(None, None, None, 'col'), may hold values from -0.0625 to 0.0625
- kernel_two: bfloat16 [3, 3, 3, 384, 384], P(None, None, None, 'col'), may hold values from -0.0625 to 0.0625
Outputs:
- grad_in: float32 [16, 16, 128, 384], P('tm', 'row', 'col')
All inputs are finite; a program needn't handle non-finite values.
Results may differ from a plain program's by a relative error of at most 0.017.
Values may be sent and summed in bfloat16 or wider, within the bound.
No kernel may reach another device: no remote copies, remote signals or barrier semaphores. Data moves between devices by JAX's collectives and lax.ppermute only.
A program may use at most 128 MiB of HBM per device.

v0:
```python
import math

import jax
import jax.numpy as jnp
from jax import lax
from jax.sharding import PartitionSpec as P

EPSILON = 1e-06


def extended_2(shard, sides, width):
    for axis, dim in sides:
        size, length = (lax.axis_size(axis), shard.shape[dim])
        up = [(i, (i + 1) % size) for i in range(size - 1)]
        down = [(j, i) for i, j in up]
        last = lax.slice_in_dim(shard, length - width, length, axis=dim)
        initial = lax.slice_in_dim(shard, 0, width, axis=dim)
        before = lax.ppermute(last, axis, up)
        after = lax.ppermute(initial, axis, down)
        shard = jnp.concatenate([before, shard, after], axis=dim)
    return shard


def shifted(value, axis, steps):
    count = lax.axis_size(axis)
    initial, last = (max(0, -steps), min(count, count - steps))
    return lax.ppermute(value, axis, [(source, source + steps) for source in range(initial, last)])


def norm_factor(field):
    return lax.rsqrt(jnp.mean(field * field, axis=-1, keepdims=True) + EPSILON)


def norm_backward(field, gain, upstream):
    factor = norm_factor(field)
    gained = gain * upstream
    return factor * gained - field * factor**3 * jnp.mean(field * gained, axis=-1, keepdims=True)


def silu_slope(pre):
    sig = jax.nn.sigmoid(pre)
    return sig * (1.0 + pre * (1.0 - sig))


def conv_taps(padded, kernel, frame_count, row_count, column_count, flipped):
    total = jnp.zeros((frame_count * row_count * column_count, kernel.shape[4]), jnp.float32)
    for depth in range(3):
        for down in range(3):
            for across in range(3):
                if flipped:
                    start_t, start_r, start_c = (2 - depth, 2 - down, 2 - across)
                    matrix = kernel[depth, down, across].T
                else:
                    start_t, start_r, start_c = (depth, down, across)
                    matrix = kernel[depth, down, across]
                window = padded[
                    start_t : start_t + frame_count,
                    start_r : start_r + row_count,
                    start_c : start_c + column_count,
                ]
                window = window.reshape(-1, padded.shape[3])
                total = total + jnp.dot(window, matrix, preferred_element_type=jnp.float32)
    return total.reshape(frame_count, row_count, column_count, -1)


def rim_padded(extended):
    return extended_2(extended, (("row", 1), ("col", 2)), 1)


def cached_input(field):
    cached = shifted(field, "tm", 1)
    return rim_padded(jnp.concatenate([cached, field], axis=0))


def later_input(field):
    later = shifted(field, "tm", -1)
    return rim_padded(jnp.concatenate([field, later], axis=0))


def project_back(gradient, weight):
    return jnp.einsum(
        "fkd,ed->fke", gradient, weight.astype(jnp.float32), precision=lax.Precision.HIGHEST
    )


def shards(
    latent,
    grad_out,
    norm_gain,
    w_query,
    w_key,
    w_value,
    w_out,
    gain_one,
    gain_two,
    kernel_one,
    kernel_two,
):
    kernel_one, kernel_two = (
        lax.all_gather(kernel_one, "col", axis=3, tiled=True),
        lax.all_gather(kernel_two, "col", axis=3, tiled=True),
    )
    frame_count, row_count, column_count, channels = latent.shape
    positions = row_count * column_count
    inverse_root = 1.0 / math.sqrt(channels)
    wide_latent = latent.astype(jnp.float32)
    normed = (
        (wide_latent * norm_factor(wide_latent) * norm_gain)
        .astype(jnp.bfloat16)
        .reshape(frame_count, positions, channels)
    )
    flat_normed = normed.reshape(-1, channels)
    queries = (
        jnp.dot(flat_normed, w_query, preferred_element_type=jnp.float32)
        .astype(jnp.bfloat16)
        .reshape(frame_count, positions, channels)
    )
    local_keys = (
        jnp.dot(flat_normed, w_key, preferred_element_type=jnp.float32)
        .astype(jnp.bfloat16)
        .reshape(frame_count, positions, channels)
    )
    local_values = (
        jnp.dot(flat_normed, w_value, preferred_element_type=jnp.float32)
        .astype(jnp.bfloat16)
        .reshape(frame_count, positions, channels)
    )
    keys, values = (
        lax.all_gather(local_keys, ("row", "col"), axis=1, tiled=True),
        lax.all_gather(local_values, ("row", "col"), axis=1, tiled=True),
    )
    scores = (
        jnp.einsum("fqd,fkd->fqk", queries, keys, preferred_element_type=jnp.float32) * inverse_root
    )
    prob = jax.nn.softmax(scores, axis=-1)
    prob_b = prob.astype(jnp.bfloat16)
    context = jnp.einsum("fqk,fkd->fqd", prob_b, values, preferred_element_type=jnp.float32).astype(
        jnp.bfloat16
    )
    mixed = wide_latent + jnp.dot(
        context.reshape(-1, channels), w_out, preferred_element_type=jnp.float32
    ).reshape(latent.shape)
    mixed = mixed.astype(jnp.bfloat16)
    wide_mixed = mixed.astype(jnp.float32)
    pre_one = wide_mixed * norm_factor(wide_mixed) * gain_one
    act_one = jax.nn.silu(pre_one).astype(jnp.bfloat16)
    conv_one = conv_taps(
        cached_input(act_one), kernel_one, frame_count, row_count, column_count, False
    ).astype(jnp.bfloat16)
    wide_conv = conv_one.astype(jnp.float32)
    pre_two = wide_conv * norm_factor(wide_conv) * gain_two
    g_act_two = conv_taps(
        later_input(grad_out), kernel_two, frame_count, row_count, column_count, True
    )
    g_conv = norm_backward(wide_conv, gain_two, g_act_two * silu_slope(pre_two)).astype(
        jnp.bfloat16
    )
    g_act_one = conv_taps(
        later_input(g_conv), kernel_one, frame_count, row_count, column_count, True
    )
    g_mixed = grad_out.astype(jnp.float32) + norm_backward(
        wide_mixed, gain_one, g_act_one * silu_slope(pre_one)
    )
    g_mixed = g_mixed.astype(jnp.bfloat16)
    g_context = jnp.dot(g_mixed.reshape(-1, channels), w_out.T, preferred_element_type=jnp.float32)
    g_context = g_context.astype(jnp.bfloat16).reshape(frame_count, positions, channels)
    g_prob = jnp.einsum("fqd,fkd->fqk", g_context, values, preferred_element_type=jnp.float32)
    row_delta = jnp.sum(prob * g_prob, axis=-1, keepdims=True)
    g_score = (prob * (g_prob - row_delta) * inverse_root).astype(jnp.bfloat16)
    g_query = jnp.einsum("fqk,fkd->fqd", g_score, keys, preferred_element_type=jnp.float32)
    local_term = project_back(g_query, w_query)
    key_part = jnp.einsum("fqk,fqd->fkd", g_score, queries, preferred_element_type=jnp.float32)
    value_part = jnp.einsum("fqk,fqd->fkd", prob_b, g_context, preferred_element_type=jnp.float32)
    g_key, g_value = (
        lax.psum_scatter(
            key_part.astype(jnp.bfloat16), ("row", "col"), scatter_dimension=1, tiled=True
        ).astype(jnp.float32),
        lax.psum_scatter(
            value_part.astype(jnp.bfloat16), ("row", "col"), scatter_dimension=1, tiled=True
        ).astype(jnp.float32),
    )
    g_normed = local_term + project_back(g_key, w_key) + project_back(g_value, w_value)
    g_normed = g_normed.reshape(latent.shape)
    return g_mixed.astype(jnp.float32) + norm_backward(wide_latent, norm_gain, g_normed)


def solution(mesh):
    placed = (
        P("tm", "row", "col", None),
        P("tm", "row", "col", None),
        P(),
        P(),
        P(),
        P(),
        P(),
        P(),
        P(),
        P(None, None, None, "col", None),
        P(None, None, None, "col", None),
    )
    return jax.shard_map(
        shards, mesh=mesh, in_specs=placed, out_specs=P("tm", "row", "col", None), check_vma=False
    )
```

profile of v0, /device:TPU:64, one launch (start us, length us, event | category | flops | bytes accessed | tf_op | source)
XLA Modules:
  0.0 899.7 jit_solution(10925578988999579039)
XLA Ops:
  8.6 1.8 convolution_convert_fusion.5
  10.5 1.8 convolution_convert_fusion.4
  13.7 1.9 collective-permute-start.5
  16.6 1.6 collective-permute-done.5
  18.2 1.3 collective-permute-start.7
  19.5 4.5 collective-permute-start.6
  25.6 1.3 collective-permute-start.8
  26.9 4.5 collective-permute-start.9
  32.4 1.5 collective-permute-done.9
  34.1 136.6 %all-gather.5.cloned.1.call-done = bf16[2,2048,384]{2,1,0:T(8,128)(2,1)} async-done(((bf16[2,64,384]{2,1,0:T(8,128)(2,1)}), bf16[2,2048,384]{2,1,0:T(8,128)(2,1)}) %all-gather.5.cloned.1.call-update) | async-done | bytes 3145744 | tf_op jit(solution)/shard_map/all_gather | solution.py:129
  170.7 3.0 convolution_multiply_fusion
  173.7 1.2 fusion.79
  174.9 156.0 %all-gather.7.cloned.1.call-done = bf16[2,2048,384]{2,1,0:T(8,128)(2,1)} async-done(((bf16[2,64,384]{2,1,0:T(8,128)(2,1)}), bf16[2,2048,384]{2,1,0:T(8,128)(2,1)}) %all-gather.7.cloned.1.call-update) | async-done | bytes 3145744 | tf_op jit(solution)/shard_map/all_gather | solution.py:130
  330.9 2.9 multiply_reduce_fusion.4
  334.0 1.9 collective-permute-start
  337.1 3.9 collective-permute-done
  341.0 1.3 collective-permute-start.2
  342.3 4.5 collective-permute-start.1
  348.4 3.1 collective-permute-start.3
  351.5 1.5 collective-permute-start.4
  354.1 4.2 collective-permute-done.4
  359.7 48.4 %all-gather.9.cloned.1.call-done = bf16[3,3,3,384,384]{4,3,2,1,0:T(8,128)(2,1)} async-done(((bf16[3,3,3,24,384]{4,3,2,1,0:T(8,128)(2,1)}), bf16[3,3,3,384,384]{4,3,2,1,0:T(8,128)(2,1)}) %all-gather.9.cloned.1.call-update) | async-done | bytes 7962640 | tf_op jit(solution)/shard_map/all_gather | solution.py:100
  408.2 1.3 fusion.48
  409.5 1.7 fusion.46
  411.2 1.2 fusion.44
  412.5 1.3 convolution_add_fusion.71
  413.7 1.2 convolution_add_fusion.70
  415.0 1.2 convolution_add_fusion.69
  416.2 1.2 fusion.17
  417.5 1.2 convolution_add_fusion.67
  418.7 1.2 convolution_add_fusion.66
  420.0 1.2 convolution_add_fusion.65
  421.2 1.2 convolution_add_fusion.64
  429.5 54.7 %all-gather.11.cloned.1.call-done = bf16[3,3,3,384,384]{4,3,2,1,0:T(8,128)(2,1)} async-done(((bf16[3,3,3,24,384]{4,3,2,1,0:T(8,128)(2,1)}), bf16[3,3,3,384,384]{4,3,2,1,0:T(8,128)(2,1)}) %all-gather.11.cloned.1.call-update) | async-done | bytes 7962640 | tf_op jit(solution)/shard_map/all_gather | solution.py:101
  484.1 1.3 fusion.30
  485.5 1.5 fusion.31
  487.0 1.2 fusion.32
  488.3 1.3 fusion.33
  489.6 1.2 fusion.34
  490.8 1.2 convolution_add_fusion.47
  492.1 1.2 convolution_add_fusion.46
  493.3 1.3 convolution_add_fusion.45
  494.6 1.2 fusion.15
  495.9 1.2 convolution_add_fusion.43
  497.1 1.2 convolution_add_fusion.42
  498.4 1.2 convolution_add_fusion.41
  507.3 2.2 collective-permute-start.10
  509.5 2.2 collective-permute-done.10
  511.7 1.3 collective-permute-start.12
  513.0 4.5 collective-permute-start.11
  517.6 1.5 collective-permute-done.11
  519.1 1.3 collective-permute-start.13
  520.4 4.8 collective-permute-start.14
  525.3 1.2 fusion.43
  527.3 1.3 fusion.47
  528.7 1.2 fusion.45
  533.5 1.2 fusion.11
  538.3 1.3 convolution_add_fusion.18
  545.4 4.8 convolution_convert_fusion.1
  550.4 2.8 convolution_convert_fusion
  553.3 4.0 fusion.23
  557.7 165.9 %reduce-scatter.3.cloned.1.call-done = bf16[2,64,384]{2,1,0:T(8,128)(2,1)} async-done(((bf16[2,2048,384]{2,1,0:T(8,128)(2,1)}), bf16[2,64,384]{2,1,0:T(8,128)(2,1)}) %reduce-scatter.3.cloned.1.call-update) | async-done | bytes 98320 | tf_op jit(solution)/shard_map/reduce_scatter | solution.py:175
  724.7 166.1 %reduce-scatter.5.cloned.1.call-done = bf16[2,64,384]{2,1,0:T(8,128)(2,1)} async-done(((bf16[2,2048,384]{2,1,0:T(8,128)(2,1)}), bf16[2,64,384]{2,1,0:T(8,128)(2,1)}) %reduce-scatter.5.cloned.1.call-update) | async-done | bytes 98320 | tf_op jit(solution)/shard_map/reduce_scatter | solution.py:178
  890.8 1.2 fusion.55
  (199 shorter events, 43.0 us)
Async XLA Ops:
  6.5 324.4 %copy-start = (bf16[384,384]{1,0:T(8,128)(2,1)S(1)}, bf16[384,384]{1,0:T(8,128)(2,1)}, u32[]{:S(2)}) copy-start(bf16[384,384]{1,0:T(8,128)(2,1)} %param.17) | copy-start | bytes 884740
  6.5 324.4 %copy-start.4 = (bf16[2,8,8,384]{3,2,1,0:T(8,128)(2,1)S(1)}, bf16[2,8,8,384]{3,2,1,0:T(8,128)(2,1)}, u32[]{:S(2)}) copy-start(bf16[2,8,8,384]{3,2,1,0:T(8,128)(2,1)} %param.11) | copy-start | bytes 294916
  6.5 164.2 %all-gather.5.cloned.1.call-start = ((), (), s32[]{:S(2)}) async-start(), calls=%async_computation.2 | async-start | bytes 3244032 | tf_op jit(solution)/shard_map/all_gather | solution.py:129
  10.4 320.5 %all-gather.7.cloned.1.call-start = ((), (), s32[]{:S(2)}) async-start(), calls=%async_computation.3 | async-start | bytes 3244032 | tf_op jit(solution)/shard_map/all_gather | solution.py:130
  12.4 395.8 %all-gather.9.cloned.1.call-start = ((), (), s32[]{:S(2)}) async-start(), calls=%async_computation.4 | async-start | bytes 8460288 | tf_op jit(solution)/shard_map/all_gather | solution.py:100
  13.1 471.0 %all-gather.11.cloned.1.call-start = ((), (), s32[]{:S(2)}) async-start(), calls=%async_computation.5 | async-start | bytes 8460288 | tf_op jit(solution)/shard_map/all_gather | solution.py:101
  13.7 709.9 %reduce-scatter.3.cloned.1.call-start = ((), (), s32[]{:S(2)}) async-start(), calls=%async_computation.6 | async-start | bytes 3244032 | tf_op jit(solution)/shard_map/reduce_scatter | solution.py:175
  13.7 4.4 collective-permute-start.5
  18.2 152.5 %copy-start.24 = (bf16[2,8,8,384]{3,2,1,0:T(8,128)(2,1)}, bf16[2,8,8,384]{3,2,1,0:T(8,128)(2,1)S(1)}, u32[]{:S(2)}) copy-start(bf16[2,8,8,384]{3,2,1,0:T(8,128)(2,1)S(1)} %collective-permute-done.5) | copy-start | bytes 294916
  18.2 7.0 collective-permute-start.7
  19.5 6.1 collective-permute-start.6
  25.2 308.6 %copy-start.25 = (bf16[128,384]{1,0:T(8,128)(2,1)}, bf16[128,384]{1,0:T(8,128)(2,1)S(1)}, u32[]{:S(2)}) copy-start(bf16[128,384]{1,0:T(8,128)(2,1)S(1)} %convolution_convert_fusion.6) | copy-start | bytes 294916
  25.6 308.2 %copy-start.29 = (f32[384]{0:T(512)S(1)}, f32[384]{0:T(512)}, u32[]{:S(2)}) copy-start(f32[384]{0:T(512)} %param.18) | copy-start | bytes 4612
  25.6 6.7 collective-permute-start.8
  26.9 6.9 collective-permute-start.9
  174.9 158.9 %copy-start.32 = (f32[2,64]{1,0:T(2,128)}, f32[2,64]{1,0:T(2,128)S(1)}, u32[]{:S(2)}) copy-start(f32[2,64]{1,0:T(2,128)S(1)} %get-tuple-element.109) | copy-start | bytes 1540
  334.0 6.9 collective-permute-start
  341.0 6.5 collective-permute-start.2
  342.3 6.1 collective-permute-start.1
  348.4 5.7 collective-permute-start.3
  351.5 6.7 collective-permute-start.4
  408.1 14.3 %copy-start.1 = (bf16[3,3,3,384,384]{4,3,2,1,0:T(8,128)(2,1)S(1)}, bf16[3,3,3,384,384]{4,3,2,1,0:T(8,128)(2,1)}, u32[]{:S(2)}) copy-start(bf16[3,3,3,384,384]{4,3,2,1,0:T(8,128)(2,1)} %all-gather.9.cloned.1.call-done) | copy-start | bytes 23887876
  408.1 15.5 %copy-start.20 = (bf16[2,8,8,384]{3,2,1,0:T(8,128)(2,1)S(1)}, bf16[2,8,8,384]{3,2,1,0:T(8,128)(2,1)}, u32[]{:S(2)}) copy-start(bf16[2,8,8,384]{3,2,1,0:T(8,128)(2,1)} %get-tuple-element.46) | copy-start | bytes 294916
  408.1 15.7 %copy-start.19 = (bf16[2,8,8,384]{3,2,1,0:T(8,128)(2,1)S(1)}, bf16[2,8,8,384]{3,2,1,0:T(8,128)(2,1)}, u32[]{:S(2)}) copy-start(bf16[2,8,8,384]{3,2,1,0:T(8,128)(2,1)} %get-tuple-element.123) | copy-start | bytes 294916
  408.1 17.0 %copy-start.18 = (bf16[2,8,8,384]{3,2,1,0:T(8,128)(2,1)S(1)}, bf16[2,8,8,384]{3,2,1,0:T(8,128)(2,1)}, u32[]{:S(2)}) copy-start(bf16[2,8,8,384]{3,2,1,0:T(8,128)(2,1)} %get-tuple-element.124) | copy-start | bytes 294916
  408.1 18.4 %copy-start.17 = (bf16[2,8,8,384]{3,2,1,0:T(8,128)(2,1)S(1)}, bf16[2,8,8,384]{3,2,1,0:T(8,128)(2,1)}, u32[]{:S(2)}) copy-start(bf16[2,8,8,384]{3,2,1,0:T(8,128)(2,1)} %get-tuple-element.44) | copy-start | bytes 294916
  408.1 18.8 %copy-start.23 = (bf16[2,8,8,384]{3,2,1,0:T(8,128)(2,1)S(1)}, bf16[2,8,8,384]{3,2,1,0:T(8,128)(2,1)}, u32[]{:S(2)}) copy-start(bf16[2,8,8,384]{3,2,1,0:T(8,128)(2,1)} %get-tuple-element.130) | copy-start | bytes 294916
  408.2 19.0 %copy-start.16 = (bf16[2,8,8,384]{3,2,1,0:T(8,128)(2,1)S(1)}, bf16[2,8,8,384]{3,2,1,0:T(8,128)(2,1)}, u32[]{:S(2)}) copy-start(bf16[2,8,8,384]{3,2,1,0:T(8,128)(2,1)} %get-tuple-element.43) | copy-start | bytes 294916
  409.5 17.9 %copy-start.15 = (bf16[2,8,8,384]{3,2,1,0:T(8,128)(2,1)S(1)}, bf16[2,8,8,384]{3,2,1,0:T(8,128)(2,1)}, u32[]{:S(2)}) copy-start(bf16[2,8,8,384]{3,2,1,0:T(8,128)(2,1)} %get-tuple-element.126) | copy-start | bytes 294916
  412.5 15.4 %copy-start.14 = (bf16[2,8,8,384]{3,2,1,0:T(8,128)(2,1)S(1)}, bf16[2,8,8,384]{3,2,1,0:T(8,128)(2,1)}, u32[]{:S(2)}) copy-start(bf16[2,8,8,384]{3,2,1,0:T(8,128)(2,1)} %get-tuple-element.42) | copy-start | bytes 294916
  413.7 14.4 %copy-start.13 = (bf16[2,8,8,384]{3,2,1,0:T(8,128)(2,1)S(1)}, bf16[2,8,8,384]{3,2,1,0:T(8,128)(2,1)}, u32[]{:S(2)}) copy-start(bf16[2,8,8,384]{3,2,1,0:T(8,128)(2,1)} %get-tuple-element.127) | copy-start | bytes 294916
  415.0 13.3 %copy-start.22 = (bf16[2,8,8,384]{3,2,1,0:T(8,128)(2,1)S(1)}, bf16[2,8,8,384]{3,2,1,0:T(8,128)(2,1)}, u32[]{:S(2)}) copy-start(bf16[2,8,8,384]{3,2,1,0:T(8,128)(2,1)} %get-tuple-element.83) | copy-start | bytes 294916
  416.2 12.3 %copy-start.21 = (bf16[2,8,8,384]{3,2,1,0:T(8,128)(2,1)S(1)}, bf16[2,8,8,384]{3,2,1,0:T(8,128)(2,1)}, u32[]{:S(2)}) copy-start(bf16[2,8,8,384]{3,2,1,0:T(8,128)(2,1)} %get-tuple-element.41) | copy-start | bytes 294916
  417.4 66.7 %copy-start.12 = (bf16[2,8,8,384]{3,2,1,0:T(8,128)(2,1)S(1)}, bf16[2,8,8,384]{3,2,1,0:T(8,128)(2,1)}, u32[]{:S(2)}) copy-start(bf16[2,8,8,384]{3,2,1,0:T(8,128)(2,1)} %get-tuple-element.138) | copy-start | bytes 294916
  418.7 66.8 %copy-start.11 = (bf16[2,8,8,384]{3,2,1,0:T(8,128)(2,1)S(1)}, bf16[2,8,8,384]{3,2,1,0:T(8,128)(2,1)}, u32[]{:S(2)}) copy-start(bf16[2,8,8,384]{3,2,1,0:T(8,128)(2,1)} %get-tuple-element.137) | copy-start | bytes 294916
  427.2 74.7 %copy-start.10 = (bf16[2,8,8,384]{3,2,1,0:T(8,128)(2,1)S(1)}, bf16[2,8,8,384]{3,2,1,0:T(8,128)(2,1)}, u32[]{:S(2)}) copy-start(bf16[2,8,8,384]{3,2,1,0:T(8,128)(2,1)} %get-tuple-element.134) | copy-start | bytes 294916
  429.4 58.9 %copy-start.34 = (f32[128]{0:T(128)}, f32[128]{0:T(128)S(1)}, u32[]{:S(2)}) copy-start(f32[128]{0:T(128)S(1)} %get-tuple-element.108) | copy-start | bytes 1540
  484.1 15.5 %copy-start.2 = (bf16[3,3,3,384,384]{4,3,2,1,0:T(8,128)(2,1)S(1)}, bf16[3,3,3,384,384]{4,3,2,1,0:T(8,128)(2,1)}, u32[]{:S(2)}) copy-start(bf16[3,3,3,384,384]{4,3,2,1,0:T(8,128)(2,1)} %all-gather.11.cloned.1.call-done) | copy-start | bytes 23887876
  484.1 21.2 %copy-start.27 = (bf16[2,8,8,384]{3,2,1,0:T(8,128)(2,1)S(1)}, bf16[2,8,8,384]{3,2,1,0:T(8,128)(2,1)}, u32[]{:S(2)}) copy-start(bf16[2,8,8,384]{3,2,1,0:T(8,128)(2,1)} %get-tuple-element.95) | copy-start | bytes 294916
  488.3 17.6 %copy-start.9 = (bf16[2,8,8,384]{3,2,1,0:T(8,128)(2,1)S(1)}, bf16[2,8,8,384]{3,2,1,0:T(8,128)(2,1)}, u32[]{:S(2)}) copy-start(bf16[2,8,8,384]{3,2,1,0:T(8,128)(2,1)} %param.12) | copy-start | bytes 294916
  493.3 13.3 %copy-start.28 = (bf16[2,8,8,384]{3,2,1,0:T(8,128)(2,1)S(1)}, bf16[2,8,8,384]{3,2,1,0:T(8,128)(2,1)}, u32[]{:S(2)}) copy-start(bf16[2,8,8,384]{3,2,1,0:T(8,128)(2,1)} %get-tuple-element.77) | copy-start | bytes 294916
  493.3 13.3 %copy-start.31 = (f32[384]{0:T(512)S(1)}, f32[384]{0:T(512)}, u32[]{:S(2)}) copy-start(f32[384]{0:T(512)} %param.19) | copy-start | bytes 4612
  493.3 13.3 %copy-start.35 = (f32[128]{0:T(128)S(1)}, f32[128]{0:T(128)}, u32[]{:S(2)}) copy-start(f32[128]{0:T(128)} %copy-done.34) | copy-start | bytes 1540
  507.3 32.4 %slice-start = ((s8[7962624]{0:T(1024)(128)(4,1)}), s8[4194304]{0:T(1024)(128)(4,1)S(1)}, s32[]{:S(2)}) async-start(s8[7962624]{0:T(1024)(128)(4,1)} %bitcast.413), calls=%async_computation.8 | async-start | bytes 8388608
  507.3 4.4 collective-permute-start.10
  511.7 5.9 collective-permute-start.12
  513.0 6.1 collective-permute-start.11
  519.1 7.4 collective-permute-start.13
  520.4 6.4 collective-permute-start.14
  527.2 12.4 %slice-start.1 = ((s8[7962624]{0:T(1024)(128)(4,1)}), s8[3768320]{0:T(1024)(128)(4,1)S(1)}, s32[]{:S(2)}) async-start(s8[7962624]{0:T(1024)(128)(4,1)} %bitcast.413), calls=%async_computation.9 | async-start | bytes 7536640
  528.7 13.6 %copy-start.36 = (f32[128]{0:T(128)S(1)}, f32[128]{0:T(128)}, u32[]{:S(2)}) copy-start(f32[128]{0:T(128)} %copy-done.34) | copy-start | bytes 1540
  528.7 13.6 %copy-start.37 = (f32[128]{0:T(128)S(1)}, f32[128]{0:T(128)}, u32[]{:S(2)}) copy-start(f32[128]{0:T(128)} %get-tuple-element.107) | copy-start | bytes 1540
  538.3 6.0 copy-start.3
  540.8 4.6 copy-start.26
  540.8 4.6 copy-start.33
  545.4 4.9 copy-start.8
  550.3 7.0 copy-start.7
  550.3 173.3 %copy-start.5 = (bf16[384,384]{1,0:T(8,128)(2,1)S(1)}, bf16[384,384]{1,0:T(8,128)(2,1)}, u32[]{:S(2)}) copy-start(bf16[384,384]{1,0:T(8,128)(2,1)} %param.15) | copy-start | bytes 884740
  550.3 340.5 %copy-start.6 = (bf16[384,384]{1,0:T(8,128)(2,1)S(1)}, bf16[384,384]{1,0:T(8,128)(2,1)}, u32[]{:S(2)}) copy-start(bf16[384,384]{1,0:T(8,128)(2,1)} %param.16) | copy-start | bytes 884740
  550.4 340.4 %copy-start.30 = (f32[384]{0:T(512)S(1)}, f32[384]{0:T(512)}, u32[]{:S(2)}) copy-start(f32[384]{0:T(512)} %param.13) | copy-start | bytes 4612
  550.4 340.4 %reduce-scatter.5.cloned.1.call-start = ((), (), s32[]{:S(2)}) async-start(), calls=%async_computation.7 | async-start | bytes 3244032 | tf_op jit(solution)/shard_map/reduce_scatter | solution.py:178
Sparse Core Ops, SparseCore 0:
  10.6 160.0 all-gather.4
  172.5 158.3 all-gather.6
  333.4 74.6 all-gather.8
  410.5 73.6 all-gather.10
  550.4 173.1 reduce-scatter.2
  726.2 164.5 reduce-scatter.4
where the time goes:
time: 901 us; the launch traced here: 900 us
  waiting for transfers between devices  745 us (83%)
  matrix products  86.4 us (10%)
  starting transfers between devices  40.2 us (4%)
  between operations  14.9 us (2%)
    reduce_scatter x1, waiting for transfers between devices, shards(): lax.psum_scatter(value_part.astype(jnp.bfloat16), ('row', 'col'), scatter...  166 us
    reduce_scatter x1, waiting for transfers between devices, shards(): lax.psum_scatter(key_part.astype(jnp.bfloat16), ('row', 'col'), scatter_d...  166 us
    all_gather x1, waiting for transfers between devices, shards(): lax.all_gather(local_values, ('row', 'col'), axis=1, tiled=True)  156 us
    all_gather x1, waiting for transfers between devices, shards(): lax.all_gather(local_keys, ('row', 'col'), axis=1, tiled=True)  137 us
    dot_general x81, matrix products, conv_taps(): total = total + jnp.dot(window, matrix, preferred_element_type=jnp.float32)  60 us
    all_gather x1, waiting for transfers between devices, shards(): lax.all_gather(kernel_two, 'col', axis=3, tiled=True)  54.7 us
    all_gather x1, waiting for transfers between devices, shards(): lax.all_gather(kernel_one, 'col', axis=3, tiled=True)  48.4 us
    ppermute x6, starting transfers between devices, extended_2(): before = lax.ppermute(last, axis, up)  26.1 us
  transfers between devices with their start and end apart: 21, of which 16 were waited for; matrix products, arithmetic and copies ran while one was open for 5% of the time, Pallas kernels for 0%

commit v1 on v0

v1 whole, which is shorter than its diff:
```python
import math

import jax
import jax.numpy as jnp
from jax import lax
from jax.experimental import pallas as pl
from jax.experimental.pallas import tpu as pltpu
from jax.sharding import PartitionSpec as P

EPSILON = 1e-06
F32, BF16 = jnp.float32, jnp.bfloat16
C = 384
ROWS, SLOTS = 16, 16
SPAN = ROWS * SLOTS
VMEM = 50 * 1024 * 1024
NT = (((1,), (1,)), ((), ()))


def norm_factor(field):
    return lax.rsqrt(jnp.mean(field * field, axis=-1, keepdims=True) + EPSILON)


def norm_backward(field, gain, upstream):
    factor = norm_factor(field)
    gained = gain * upstream
    return factor * gained - field * factor**3 * jnp.mean(field * gained, axis=-1, keepdims=True)


def silu_slope(pre):
    sig = jax.nn.sigmoid(pre)
    return sig * (1.0 + pre * (1.0 - sig))


def stage_shifts(x_ref, s_ref):
    length = x_ref.shape[1]
    for frame in range(3):
        wide = x_ref[frame].astype(F32)
        s_ref[frame, :, :C] = pltpu.roll(wide, 1, 0).astype(BF16)
        s_ref[frame, :, C : 2 * C] = x_ref[frame]
        s_ref[frame, :, 2 * C :] = pltpu.roll(wide, length - 1, 0).astype(BF16)


def flipped_taps(s_ref, w_ref, step, pitch, span):
    depth, down = step // 3, lax.rem(step, 3)
    start = pl.multiple_of((2 - down) * pitch, pitch)
    total = None
    for across in range(3):
        lane = (2 - across) * C
        window = s_ref[2 - depth, pl.ds(start, span), lane : lane + C]
        term = lax.dot_general(window, w_ref[across], NT, preferred_element_type=F32)
        total = term if total is None else total + term
    return total


def pair_kernel(core_ref, x_ref, w_ref, out_ref, s_ref):
    step = pl.program_id(0)
    pitch, span = 2 * SLOTS, 2 * SPAN

    @pl.when(step == 0)
    def _():
        stage_shifts(x_ref, s_ref)
        out_ref[...] = jnp.zeros_like(out_ref)

    @pl.when(core_ref[0] == 0)
    def _():
        start = pl.multiple_of(lax.rem(step, 3) * pitch, pitch)
        window = s_ref[step // 3, pl.ds(start, span), :]
        out_ref[...] += jnp.dot(
            window, w_ref[...].reshape(3 * C, C), preferred_element_type=F32
        )

    @pl.when(core_ref[0] != 0)
    def _():
        out_ref[...] += flipped_taps(s_ref, w_ref, step, pitch, span)


def pair_conv(core, x, weights):
    return pl.pallas_call(
        pair_kernel,
        out_shape=jax.ShapeDtypeStruct((2 * SPAN, C), F32),
        grid_spec=pltpu.PrefetchScalarGridSpec(
            num_scalar_prefetch=1,
            grid=(9,),
            in_specs=[
                pl.BlockSpec(x.shape, lambda i, core: (0, 0, 0)),
                pl.BlockSpec((3, C, C), lambda i, core: (i, 0, 0)),
            ],
            out_specs=pl.BlockSpec((2 * SPAN, C), lambda i, core: (0, 0)),
            scratch_shapes=[pltpu.VMEM((3, x.shape[1], 3 * C), BF16)],
        ),
        compiler_params=pltpu.CompilerParams(vmem_limit_bytes=VMEM),
        cost_estimate=pl.CostEstimate(
            flops=2 * 27 * 2 * SPAN * C * C, bytes_accessed=27 * C * C * 2, transcendentals=0
        ),
        name="pair_conv",
    )(core, x, weights)


def own_slots(shape):
    slot = lax.rem(lax.broadcasted_iota(jnp.int32, shape, 0), SLOTS)
    return (slot >= 2) & (slot < 10)


def back_kernel(core_ref, x_ref, mine_ref, other_ref, grad_ref, mixed_ref, gain_ref, out_ref, s_ref, sum_ref):
    step = pl.program_id(0)

    @pl.when(step == 0)
    def _():
        stage_shifts(x_ref, s_ref)
        sum_ref[...] = jnp.zeros_like(sum_ref)

    @pl.when(core_ref[0] == 0)
    def _():
        sum_ref[...] += flipped_taps(s_ref, mine_ref, step, SLOTS, SPAN)

    @pl.when(core_ref[0] != 0)
    def _():
        sum_ref[...] += flipped_taps(s_ref, other_ref, step, SLOTS, SPAN)

    @pl.when(step == 8)
    def _():
        mixed = mixed_ref[...].astype(F32)
        gain = gain_ref[...]
        slope = silu_slope(mixed * norm_factor(mixed) * gain)
        total = grad_ref[...].astype(F32) + norm_backward(mixed, gain, sum_ref[...] * slope)
        out_ref[...] = jnp.where(own_slots(total.shape), total, 0.0).astype(BF16)


def back_conv(core, x, mine, other, grad, mixed, gain):
    whole = lambda i, core: (0, 0)
    return pl.pallas_call(
        back_kernel,
        out_shape=jax.ShapeDtypeStruct((SPAN, C), BF16),
        grid_spec=pltpu.PrefetchScalarGridSpec(
            num_scalar_prefetch=1,
            grid=(9,),
            in_specs=[
                pl.BlockSpec(x.shape, lambda i, core: (0, 0, 0)),
                pl.BlockSpec((3, C, C), lambda i, core: (i * (1 - core[0]), 0, 0)),
                pl.BlockSpec((3, C, C), lambda i, core: (i * core[0], 0, 0)),
                pl.BlockSpec((SPAN, C), whole),
                pl.BlockSpec((SPAN, C), whole),
                pl.BlockSpec((1, C), whole),
            ],
            out_specs=pl.BlockSpec((SPAN, C), whole),
            scratch_shapes=[pltpu.VMEM((3, x.shape[1], 3 * C), BF16), pltpu.VMEM((SPAN, C), F32)],
        ),
        compiler_params=pltpu.CompilerParams(vmem_limit_bytes=VMEM),
        cost_estimate=pl.CostEstimate(
            flops=2 * 27 * SPAN * C * C, bytes_accessed=27 * C * C * 2, transcendentals=0
        ),
        name="back_conv",
    )(core, x, mine, other, grad, mixed, gain)


CHUNK = 512


def attend_back_kernel(
    col_ref, gm_ref, prob_ref, keys_ref, values_ref, qk_ref, w_out_ref, w_value_ref, w_query_ref,
    out_ref, gp_ref, sum_ref, mix_ref, right_ref,
):
    positions = keys_ref.shape[0]
    count = positions // CHUNK
    inverse_root = 1.0 / math.sqrt(C)
    g_context = lax.dot_general(
        gm_ref[...], w_out_ref[...], NT, preferred_element_type=F32
    ).astype(BF16)
    right_ref[:SPAN, :] = qk_ref[...]
    right_ref[SPAN:, :] = lax.dot_general(
        g_context, w_value_ref[...], NT, preferred_element_type=F32
    ).astype(BF16)
    delta = jnp.zeros((1, SPAN), F32)
    for c in range(count):
        part = pl.ds(c * CHUNK, CHUNK)
        g_prob = lax.dot_general(values_ref[part, :], g_context, NT, preferred_element_type=F32)
        gp_ref[part, :] = g_prob
        delta = delta + jnp.sum(prob_ref[part, :] * g_prob, axis=0, keepdims=True)
    g_query = jnp.zeros((SPAN, C), F32)
    for c in range(count):
        part = pl.ds(c * CHUNK, CHUNK)
        prob = prob_ref[part, :]
        g_score = (prob * (gp_ref[part, :] - delta) * inverse_root).astype(BF16)
        mix_ref[:, :SPAN] = g_score
        mix_ref[:, SPAN:] = prob.astype(BF16)
        sum_ref[part, :] = jnp.dot(mix_ref[...], right_ref[...], preferred_element_type=F32)
        g_query += lax.dot_general(
            g_score, keys_ref[part, :], (((0,), (0,)), ((), ())), preferred_element_type=F32
        )
    high = g_query.astype(BF16)
    low = (g_query - high.astype(F32)).astype(BF16)
    local = lax.dot_general(high, w_query_ref[...], NT, preferred_element_type=F32)
    local += lax.dot_general(low, w_query_ref[...], NT, preferred_element_type=F32)
    local = pltpu.roll(local, SPAN - 2, 0)
    for r in range(ROWS):
        start = pl.multiple_of((r // 8) * (positions // 2) + col_ref[0] * 64 + (r % 8) * 8, 8)
        sum_ref[pl.ds(start, 8), :] += local[r * SLOTS : r * SLOTS + 8]
    out_ref[...] = sum_ref[...].astype(BF16)


def attend_back(col, gm, prob, keys, values, qk, w_out, w_value, w_query):
    positions = keys.shape[0]
    return pl.pallas_call(
        attend_back_kernel,
        out_shape=jax.ShapeDtypeStruct((positions, C), BF16),
        in_specs=[pl.BlockSpec(memory_space=pltpu.SMEM)] + [pl.BlockSpec(memory_space=pltpu.VMEM)] * 8,
        out_specs=pl.BlockSpec(memory_space=pltpu.VMEM),
        scratch_shapes=[
            pltpu.VMEM((positions, SPAN), F32),
            pltpu.VMEM((positions, C), F32),
            pltpu.VMEM((CHUNK, 2 * SPAN), BF16),
            pltpu.VMEM((2 * SPAN, C), BF16),
        ],
        compiler_params=pltpu.CompilerParams(vmem_limit_bytes=VMEM),
        name="attend_back",
    )(col, gm, prob, keys, values, qk, w_out, w_value, w_query)


def shards(
    latent,
    grad_out,
    norm_gain,
    w_query,
    w_key,
    w_value,
    w_out,
    gain_one,
    gain_two,
    kernel_one,
    kernel_two,
):
    time_row = ("tm", "row")
    tm, row, col = lax.axis_index("tm"), lax.axis_index("row"), lax.axis_index("col")
    groups, cols = lax.axis_size("tm"), lax.axis_size("col")
    frames = groups * 2
    core = lax.rem(tm, 2)
    core_arg, col_arg = core.reshape(1), col.reshape(1)
    inverse_root = 1.0 / math.sqrt(C)
    swap_core = [(i, i ^ 1) for i in range(groups)]
    swap_row = [(0, 1), (1, 0)]

    def moved(value, steps):
        pairs = [(s, s + steps) for s in range(frames) if 0 <= s + steps < frames]
        return lax.ppermute(value, time_row, pairs)

    mine = lax.all_gather(
        jnp.where(core == 0, kernel_one, kernel_two), "col", axis=3, tiled=True
    ).reshape(27, C, C)
    other = lax.ppermute(mine, "tm", swap_core)

    spread = jnp.broadcast_to(latent.reshape(2, 1, 64, C), (2, cols, 64, C)).reshape(-1, 64, C)
    frame = lax.all_to_all(spread, ("row", "col"), 0, 0, tiled=True)
    tiles = frame.reshape(2, cols, 8, 8, C)
    pick = lambda index: lax.dynamic_index_in_dim(tiles, index, 1, keepdims=False)
    before, own, after = (
        pick(jnp.maximum(col - 1, 0)),
        pick(col),
        pick(jnp.minimum(col + 1, cols - 1)),
    )
    empty = jnp.zeros((2, 8, 4, C), BF16)
    window = jnp.concatenate([before[:, :, 6:], own, after[:, :, :2], empty], axis=2)
    window = window.reshape(SPAN, C)
    slot = lax.rem(lax.broadcasted_iota(jnp.int32, (SPAN, 1), 0), SLOTS)
    column = col * 8 + slot - 2
    inside = (column >= 0) & (column < cols * 8)
    wide_frame = frame.reshape(-1, C).astype(F32)
    normed = (wide_frame * norm_factor(wide_frame) * norm_gain).astype(BF16)
    keys = jnp.dot(normed, w_key, preferred_element_type=F32).astype(BF16)
    values = jnp.dot(normed, w_value, preferred_element_type=F32).astype(BF16)
    wide_window = window.astype(F32)
    normed_window = (wide_window * norm_factor(wide_window) * norm_gain).astype(BF16)
    queries = jnp.dot(normed_window, w_query, preferred_element_type=F32).astype(BF16)
    scores = jnp.einsum("kd,qd->kq", keys, queries, preferred_element_type=F32) * inverse_root
    prob = jax.nn.softmax(scores, axis=0)
    context = jnp.einsum(
        "kq,kd->qd", prob.astype(BF16), values, preferred_element_type=F32
    ).astype(BF16)
    mixed = (wide_window + jnp.dot(context, w_out, preferred_element_type=F32)).astype(BF16)
    wide_mixed = mixed.astype(F32)
    act_one = jax.nn.silu(wide_mixed * norm_factor(wide_mixed) * gain_one)
    act_one = jnp.where(inside & (slot < 12), act_one, 0.0).astype(BF16)
    query_key = lax.dot_general(queries, w_key, NT, preferred_element_type=F32).astype(BF16)

    def framed(f0, f1, f2):
        stacked = jnp.stack([f.reshape(ROWS, SLOTS, C) for f in (f0, f1, f2)])
        return jnp.pad(stacked, ((0, 0), (1, 1), (0, 0), (0, 0)))

    act_frames = framed(moved(act_one, 2), moved(act_one, 1), act_one)

    keep = lax.dynamic_index_in_dim(grad_out, row, 0, keepdims=False)
    give = lax.dynamic_index_in_dim(grad_out, 1 - row, 0, keepdims=False)
    got = lax.ppermute(give, "row", swap_row)
    tile = jnp.concatenate([jnp.where(row == 0, keep, got), jnp.where(row == 0, got, keep)], axis=0)
    to_right = [(i, i + 1) for i in range(cols - 1)]
    to_left = [(i + 1, i) for i in range(cols - 1)]
    grad = jnp.concatenate(
        [
            lax.ppermute(tile[:, 6:], "col", to_right),
            tile,
            lax.ppermute(tile[:, :2], "col", to_left),
            jnp.zeros((ROWS, 4, C), BF16),
        ],
        axis=1,
    ).reshape(SPAN, C)
    grad_frames = framed(grad, moved(grad, -1), moved(grad, -2))

    ours = jnp.where(core == 0, act_frames, grad_frames)
    theirs = lax.ppermute(jnp.where(core == 0, grad_frames, act_frames), "tm", swap_core)
    both = jnp.stack([ours, theirs], axis=2).reshape(3, (ROWS + 2) * 2 * SLOTS, C)
    sums = pair_conv(core_arg, both, mine).reshape(ROWS, 2, SLOTS, C)
    kept = sums[:, 0].reshape(SPAN, C)
    given = lax.ppermute(sums[:, 1].reshape(SPAN, C), "tm", swap_core)
    conv_one = jnp.where(core == 0, kept, given).astype(BF16)
    g_act_two = jnp.where(core == 0, given, kept)
    wide_conv = conv_one.astype(F32)
    pre_two = wide_conv * norm_factor(wide_conv) * gain_two
    g_conv = norm_backward(wide_conv, gain_two, g_act_two * silu_slope(pre_two))
    g_conv = jnp.where(inside & (slot >= 1) & (slot < 11), g_conv, 0.0).astype(BF16)
    conv_frames = framed(g_conv, moved(g_conv, -1), moved(g_conv, -2))
    g_mixed = back_conv(
        core_arg,
        conv_frames.reshape(3, (ROWS + 2) * SLOTS, C),
        mine,
        other,
        grad,
        mixed,
        gain_one.reshape(1, C),
    )
    partial = attend_back(
        col_arg, g_mixed, prob, keys, values, query_key, w_out, w_value, w_query
    )
    parts = lax.all_to_all(partial.reshape(-1, 64, C), ("row", "col"), 0, 0, tiled=True)
    g_normed = jnp.sum(parts.reshape(2, cols, 64, C).astype(F32), axis=1).reshape(latent.shape)

    halves = g_mixed.reshape(2, 8, SLOTS, C)[:, :, 2:10]
    stay = lax.dynamic_index_in_dim(halves, row, 0, keepdims=False)
    leave = lax.dynamic_index_in_dim(halves, 1 - row, 0, keepdims=False)
    come = lax.ppermute(leave, "row", swap_row)
    g_tile = jnp.stack([jnp.where(row == 0, stay, come), jnp.where(row == 0, come, stay)])
    wide_latent = latent.astype(F32)
    return g_tile.astype(F32) + norm_backward(wide_latent, norm_gain, g_normed)


def solution(mesh):
    placed = (
        P("tm", "row", "col", None),
        P("tm", "row", "col", None),
        P(),
        P(),
        P(),
        P(),
        P(),
        P(),
        P(),
        P(None, None, None, "col", None),
        P(None, None, None, "col", None),
    )
    return jax.shard_map(
        shards, mesh=mesh, in_specs=placed, out_specs=P("tm", "row", "col", None), check_vma=False
    )
```

time: 901 us -> 205 us (0.23)
  the two profiles are of different devices: /device:TPU:64 before, /device:TPU:1 now
where the time goes in v1:
time: 205 us; the launch traced here: 202 us
  waiting for transfers between devices  95.8 us (47%)
  starting transfers between devices  43 us (21%)
  Pallas kernels  28.1 us (14%)
  between operations  14 us (7%)
  other arithmetic  11.1 us (5%)
  matrix products  6.18 us (3%)
  local copies, waits for them, and re-layouts  3.77 us (2%)
    all_gather x1, waiting for transfers between devices, shards(): lax.all_gather(jnp.where(core == 0, kernel_one, kernel_two), 'col', axis=...  41.4 us
    ppermute x6, starting transfers between devices, moved(): return lax.ppermute(value, time_row, pairs)  19.8 us
    ppermute x1, waiting for transfers between devices, shards(): come = lax.ppermute(leave, 'row', swap_row)  19.3 us
    ppermute x1, waiting for transfers between devices, shards(): got = lax.ppermute(give, 'row', swap_row)  17.9 us
    pallas_call x1, Pallas kernels, pair_conv(): pl.pallas_call(pair_kernel, out_shape=jax.ShapeDtypeStruct((2 * SPAN, C),...  11.1 us
    pallas_call x1, Pallas kernels, back_conv(): pl.pallas_call(back_kernel, out_shape=jax.ShapeDtypeStruct((SPAN, C), BF1...  9.72 us
    all_to_all x1, starting transfers between devices, shards(): frame = lax.all_to_all(spread, ('row', 'col'), 0, 0, tiled=True)  9.35 us
    ppermute x6, waiting for transfers between devices, moved(): return lax.ppermute(value, time_row, pairs)  8.88 us
  transfers between devices with their start and end apart: 16, of which 10 were waited for; matrix products, arithmetic and copies ran while one was open for 8% of the time, Pallas kernels for 6%

profile of v1, /device:TPU:1, one launch (start us, length us, event | category | flops | bytes accessed | tf_op | source)
XLA Modules:
  0.0 202.0 jit_solution(277811022509984205)
XLA Ops:
  6.5 2.0 broadcast_select_fusion.1
  8.5 1.5 broadcast_in_dim.52
  10.0 9.4 %all-to-all-start = ((bf16[32,64,384]{2,1,0:T(8,128)(2,1)}), bf16[32,64,384]{2,1,0:T(8,128)(2,1)S(1)}, u32[]{:S(2)}, u32[]{:S(2)}) async-start(bf16[32,64,384]{2,1,0:T(8,128)(2,1)} %bitcast.107), calls=%async_computation | async-start | bytes 3145728 | tf_op jit(solution)/shard_map/all_to_all | solution.py:252
  19.4 1.3 collective-permute-start.2
  20.8 17.9 %collective-permute-done.2 = bf16[8,8,384]{2,1,0:T(8,128)(2,1)S(1)} collective-permute-done((bf16[8,8,384]{2,1,0:T(8,128)(2,1)S(1)}, bf16[8,8,384]{2,1,0:T(8,128)(2,1)S(1)}, u32[]{:S(2)}, u32[]{:S(2)}) %collective-permute-start.2) | collective-permute-done | bytes 49184 | tf_op jit(solution)/shard_map/ppermute | solution.py:292
  38.7 3.0 %collective-permute-start.3 = (bf16[16,2,384]{2,1,0:T(2,128)(2,1)S(1)}, bf16[16,2,384]{2,1,0:T(2,128)(2,1)S(1)}, u32[]{:S(2)}, u32[]{:S(2)}) collective-permute-start(bf16[16,2,384]{2,1,0:T(2,128)(2,1)S(1)} %get-tuple-element.22), channel_id=1, source_target_pairs={{0,1},{1,2},{2,3},{3,4},{4,5},{5,6},{6,7},{7,8},{8,9},{9,10},{10,1... | collective-permute-start | bytes 73736 | tf_op jit(solution)/shard_map/ppermute | solution.py:298
  41.7 1.3 collective-permute-start.4
  43.0 0.6 compare_and_fusion
  43.6 0.1 pad.36.clone
  43.7 3.2 %collective-permute-done.4 = bf16[16,2,384]{2,1,0:T(2,128)(2,1)S(1)} collective-permute-done((bf16[16,2,384]{2,1,0:T(2,128)(2,1)S(1)}, bf16[16,2,384]{2,1,0:T(2,128)(2,1)S(1)}, u32[]{:S(2)}, u32[]{:S(2)}) %collective-permute-start.4) | collective-permute-done | bytes 24608 | tf_op jit(solution)/shard_map/ppermute | solution.py:300
  46.9 0.1 maximum_maximum_fusion
  47.1 0.4 copy-done.14
  47.5 4.8 %collective-permute-start.6 = (bf16[256,384]{1,0:T(8,128)(2,1)S(1)}, bf16[256,384]{1,0:T(8,128)(2,1)}, u32[]{:S(2)}, u32[]{:S(2)}) collective-permute-start(bf16[256,384]{1,0:T(8,128)(2,1)S(1)} %bitcast.99), channel_id=1, source_target_pairs={{32,0},{48,16},{64,32},{80,48},{96,64},{112,80},{128,96},{144,112}... | collective-permute-start | bytes 589832 | tf_op jit(solution)/shard_map/ppermute | solution.py:244
  52.3 1.9 collective-permute-start.5
  54.3 0.4 multiply_reduce_fusion
  54.7 0.1 rsqrt.54
  54.8 41.4 %all-gather.2.cloned.1.call-done = bf16[3,3,3,384,384]{4,3,2,1,0:T(8,128)(2,1)} async-done(((bf16[3,3,3,24,384]{4,3,2,1,0:T(8,128)(2,1)}), bf16[3,3,3,384,384]{4,3,2,1,0:T(8,128)(2,1)}) %all-gather.2.cloned.1.call-update) | async-done | bytes 7962640 | tf_op jit(solution)/shard_map/all_gather | solution.py:246
  96.3 0.7 collective-permute-start.11
  96.9 0.2 multiply_reduce_fusion.1
  97.2 0.1 rsqrt.56
  97.2 0.1 maximum_convert_fusion
  97.4 0.1 fusion.45
  97.5 0.3 convolution_convert_fusion.4
  97.8 0.4 fusion.1
  98.2 1.1 convolution_convert_fusion.1.keys_ref
  99.4 0.7 fusion.56
  100.1 0.4 copy-done.5
  100.5 0.4 fusion.3
  100.9 0.6 copy-done.2
  101.5 1.1 convolution_convert_fusion.values_ref
  102.7 1.6 fusion.2.prob_ref
  104.3 0.2 copy-done.4
  104.5 2.6 %fusion.18 = (f32[256]{0:T(256)S(1)}, bf16[256,384]{1,0:T(8,128)(2,1)S(1)}) fusion(f32[256,384]{1,0:T(8,128)S(1)} %bitcast.108, bf16[384,384]{1,0:T(8,128)(2,1)S(1)} %copy-done.1, bf16[2048,384]{1,0:T(8,128)(2,1)S(1)} %convolution_convert_fusion.values_ref, f32[2048,256]{1,0:T(8,128)} %fusion.2.prob_ref), kind=kOutput, calls=%fused_computation.42 | convolution fusion | flops 479264512 | bytes 4555776 | tf_op jit(solution)/shard_map/dot_general | solution.py:278
  107.1 0.8 fusion.26
  108.0 3.2 %collective-permute-start.1 = (bf16[256,384]{1,0:T(8,128)(2,1)S(1)}, bf16[256,384]{1,0:T(8,128)(2,1)S(1)}, u32[]{:S(2)}, u32[]{:S(2)}) collective-permute-start(bf16[256,384]{1,0:T(8,128)(2,1)S(1)} %fusion.26), channel_id=1, source_target_pairs={{0,16},{16,32},{32,48},{48,64},{64,80},{80,96},{96,112},{112,128},... | collective-permute-start | bytes 589832 | tf_op jit(solution)/shard_map/ppermute | solution.py:244
  111.2 4.3 %collective-permute-start = (bf16[256,384]{1,0:T(8,128)(2,1)S(1)}, bf16[256,384]{1,0:T(8,128)(2,1)S(1)}, u32[]{:S(2)}, u32[]{:S(2)}) collective-permute-start(bf16[256,384]{1,0:T(8,128)(2,1)S(1)} %fusion.26), channel_id=1, source_target_pairs={{0,32},{16,48},{32,64},{48,80},{64,96},{80,112},{96,128},{112,144}... | collective-permute-start | bytes 589832 | tf_op jit(solution)/shard_map/ppermute | solution.py:244
  115.5 1.0 fusion.71
  116.5 1.6 collective-permute-done
  118.1 1.2 select_bitcast_fusion
  119.4 0.3 collective-permute-start.7
  119.7 2.1 %collective-permute-done.7 = bf16[3,18,16,384]{3,2,1,0:T(8,128)(2,1)S(1)} collective-permute-done((bf16[3,18,16,384]{3,2,1,0:T(8,128)(2,1)S(1)}, bf16[3,18,16,384]{3,2,1,0:T(8,128)(2,1)S(1)}, u32[]{:S(2)}, u32[]{:S(2)}) %collective-permute-start.7) | collective-permute-done | bytes 663584 | tf_op jit(solution)/shard_map/ppermute | solution.py:308
  121.8 0.2 pad_maximum_fusion
  121.9 0.2 copy.15
  122.1 11.1 %pair_conv.1 = f32[512,384]{1,0:T(8,128)S(1)} custom-call(s32[1]{0:T(128)} %bitcast.core_ref, bf16[3,576,384]{2,1,0:T(8,128)(2,1)S(1)} %bitcast.97, bf16[27,384,384]{2,1,0:T(8,128)(2,1)} %bitcast.105), custom_call_target="tpu_custom_call" | custom-call | flops 4076863488 | bytes 7962624 | tf_op jit(solution)/shard_map/pair_conv/pallas_call | solution.py:78
  133.3 0.1 collective-permute-start.8
  133.4 1.7 collective-permute-done.8
  135.1 0.1 fusion.27
  135.3 0.4 fusion.42
  135.7 0.2 fusion.41
  135.9 2.0 %collective-permute-start.10 = (bf16[256,384]{1,0:T(8,128)(2,1)S(1)}, bf16[256,384]{1,0:T(8,128)(2,1)S(1)}, u32[]{:S(2)}, u32[]{:S(2)}) collective-permute-start(bf16[256,384]{1,0:T(8,128)(2,1)S(1)} %fusion.41), channel_id=1, source_target_pairs={{32,0},{48,16},{64,32},{80,48},{96,64},{112,80},{128,96},{144,112}... | collective-permute-start | bytes 589832 | tf_op jit(solution)/shard_map/ppermute | solution.py:244
  137.9 3.5 %collective-permute-start.9 = (bf16[256,384]{1,0:T(8,128)(2,1)S(1)}, bf16[256,384]{1,0:T(8,128)(2,1)S(1)}, u32[]{:S(2)}, u32[]{:S(2)}) collective-permute-start(bf16[256,384]{1,0:T(8,128)(2,1)S(1)} %fusion.41), channel_id=1, source_target_pairs={{16,0},{32,16},{48,32},{64,48},{80,64},{96,80},{112,96},{128,112},... | collective-permute-start | bytes 589832 | tf_op jit(solution)/shard_map/ppermute | solution.py:244
  141.5 0.3 convolution_convert_fusion.2.qk_ref
  141.8 5.8 %collective-permute-done.10 = bf16[256,384]{1,0:T(8,128)(2,1)S(1)} collective-permute-done((bf16[256,384]{1,0:T(8,128)(2,1)S(1)}, bf16[256,384]{1,0:T(8,128)(2,1)S(1)}, u32[]{:S(2)}, u32[]{:S(2)}) %collective-permute-start.10) | collective-permute-done | bytes 196640 | tf_op jit(solution)/shard_map/ppermute | solution.py:244
  147.6 1.4 collective-permute-done.9
  149.1 0.1 select_maximum_fusion
  149.1 9.7 %back_conv.1.gm_ref = bf16[256,384]{1,0:T(8,128)(2,1)S(1)} custom-call(s32[1]{0:T(128)} %bitcast.core_ref, bf16[3,288,384]{2,1,0:T(8,128)(2,1)S(1)} %bitcast.96, bf16[27,384,384]{2,1,0:T(8,128)(2,1)} %bitcast.106, bf16[27,384,384]{2,1,0:T(8,128)(2,1)} %collective-permute-done.11.other_ref, bf16[256,384]{1,0:T(8,128)(2,1)S(1)} %bitcast.101, ...), custom_call_target="tpu_custom_call" | custom-call | flops 2038431744 | bytes 7962624 | tf_op jit(solution)/shard_map/back_conv/pallas_call | solution.py:131
  158.9 7.2 %attend_back.1 = bf16[2048,384]{1,0:T(8,128)(2,1)} custom-call(s32[1]{0:T(128)} %bitcast.34.col_ref, bf16[256,384]{1,0:T(8,128)(2,1)S(1)} %back_conv.1.gm_ref, f32[2048,256]{1,0:T(8,128)} %fusion.2.prob_ref, bf16[2048,384]{1,0:T(8,128)(2,1)} %copy-done.5, bf16[2048,384]{1,0:T(8,128)(2,1)} %copy-done.4, ...), custom_call_target="tpu_custom_call" | custom-call | tf_op jit(solution)/shard_map/attend_back/pallas_call | solution.py:203
  166.1 5.8 %all-to-all-start.1 = ((bf16[32,64,384]{2,1,0:T(8,128)(2,1)}), bf16[32,64,384]{2,1,0:T(8,128)(2,1)S(1)}, u32[]{:S(2)}, u32[]{:S(2)}) async-start(bf16[32,64,384]{2,1,0:T(8,128)(2,1)} %bitcast.35), calls=%async_computation.1 | async-start | bytes 3145728 | tf_op jit(solution)/shard_map/all_to_all | solution.py:332
  172.0 1.3 collective-permute-start.12
  173.3 19.3 %collective-permute-done.12 = bf16[8,8,384]{2,1,0:T(8,128)(2,1)S(1)} collective-permute-done((bf16[8,8,384]{2,1,0:T(8,128)(2,1)S(1)}, bf16[8,8,384]{2,1,0:T(8,128)(2,1)S(1)}, u32[]{:S(2)}, u32[]{:S(2)}) %collective-permute-start.12) | collective-permute-done | bytes 49184 | tf_op jit(solution)/shard_map/ppermute | solution.py:338
  192.6 1.3 all-to-all-done.1
  194.0 0.2 convert_reduce_fusion
  194.2 0.1 fusion.46
  194.3 0.8 fusion.49
  (59 shorter events, 0.4 us)
Async XLA Ops:
  6.5 91.7 %copy-start = (bf16[384,384]{1,0:T(8,128)(2,1)S(1)}, bf16[384,384]{1,0:T(8,128)(2,1)}, u32[]{:S(2)}) copy-start(bf16[384,384]{1,0:T(8,128)(2,1)} %param.15) | copy-start | bytes 884740
  6.5 2.0 copy-start.8
  6.5 89.7 %all-gather.2.cloned.1.call-start = ((), (), s32[]{:S(2)}) async-start(), calls=%async_computation.2 | async-start | bytes 8460288 | tf_op jit(solution)/shard_map/all_gather | solution.py:246
  10.0 9.4 %copy-start.12 = (bf16[2,8,8,384]{3,2,1,0:T(8,128)(2,1)S(1)}, bf16[2,8,8,384]{3,2,1,0:T(8,128)(2,1)}, u32[]{:S(2)}) copy-start(bf16[2,8,8,384]{3,2,1,0:T(8,128)(2,1)} %param.12) | copy-start | bytes 294916
  10.0 44.2 %all-to-all-start = ((bf16[32,64,384]{2,1,0:T(8,128)(2,1)}), bf16[32,64,384]{2,1,0:T(8,128)(2,1)S(1)}, u32[]{:S(2)}, u32[]{:S(2)}) async-start(bf16[32,64,384]{2,1,0:T(8,128)(2,1)} %bitcast.107), calls=%async_computation | async-start | bytes 3145728 | tf_op jit(solution)/shard_map/all_to_all | solution.py:252
  19.4 19.2 %collective-permute-start.2 = (bf16[8,8,384]{2,1,0:T(8,128)(2,1)S(1)}, bf16[8,8,384]{2,1,0:T(8,128)(2,1)S(1)}, u32[]{:S(2)}, u32[]{:S(2)}) collective-permute-start(bf16[8,8,384]{2,1,0:T(8,128)(2,1)S(1)} %dynamic-slice_bitcast_fusion.4), channel_id=1, source_target_pairs={{0,16},{16,0},{1,17},{17,1},{2,18},{18,2},{3,19},{19,3},{4,20},{20... | collective-permute-start | bytes 147464 | tf_op jit(solution)/shard_map/ppermute | solution.py:292
  38.6 8.4 %copy-start.10 = (bf16[8,8,384]{2,1,0:T(8,128)(2,1)}, bf16[8,8,384]{2,1,0:T(8,128)(2,1)S(1)}, u32[]{:S(2)}) copy-start(bf16[8,8,384]{2,1,0:T(8,128)(2,1)S(1)} %get-tuple-element.20) | copy-start | bytes 147460
  38.6 8.4 %copy-start.11 = (bf16[8,8,384]{2,1,0:T(8,128)(2,1)}, bf16[8,8,384]{2,1,0:T(8,128)(2,1)S(1)}, u32[]{:S(2)}) copy-start(bf16[8,8,384]{2,1,0:T(8,128)(2,1)S(1)} %get-tuple-element.21) | copy-start | bytes 147460
  38.7 5.0 %collective-permute-start.3 = (bf16[16,2,384]{2,1,0:T(2,128)(2,1)S(1)}, bf16[16,2,384]{2,1,0:T(2,128)(2,1)S(1)}, u32[]{:S(2)}, u32[]{:S(2)}) collective-permute-start(bf16[16,2,384]{2,1,0:T(2,128)(2,1)S(1)} %get-tuple-element.22), channel_id=1, source_target_pairs={{0,1},{1,2},{2,3},{3,4},{4,5},{5,6},{6,7},{7,8},{8,9},{9,10},{10,1... | collective-permute-start | bytes 73736 | tf_op jit(solution)/shard_map/ppermute | solution.py:298
  41.7 5.2 %collective-permute-start.4 = (bf16[16,2,384]{2,1,0:T(2,128)(2,1)S(1)}, bf16[16,2,384]{2,1,0:T(2,128)(2,1)S(1)}, u32[]{:S(2)}, u32[]{:S(2)}) collective-permute-start(bf16[16,2,384]{2,1,0:T(2,128)(2,1)S(1)} %get-tuple-element.23), channel_id=1, source_target_pairs={{1,0},{2,1},{3,2},{4,3},{5,4},{6,5},{7,6},{8,7},{9,8},{10,9},{11,1... | collective-permute-start | bytes 73736 | tf_op jit(solution)/shard_map/ppermute | solution.py:300
  43.7 3.4 %copy-start.13 = (bf16[16,2,384]{2,1,0:T(2,128)(2,1)}, bf16[16,2,384]{2,1,0:T(2,128)(2,1)S(1)}, u32[]{:S(2)}) copy-start(bf16[16,2,384]{2,1,0:T(2,128)(2,1)S(1)} %collective-permute-done.3) | copy-start | bytes 73732
  46.9 0.6 copy-start.14
  47.5 49.8 %copy-start.15 = (f32[384]{0:T(512)S(1)}, f32[384]{0:T(512)}, u32[]{:S(2)}) copy-start(f32[384]{0:T(512)} %param.13) | copy-start | bytes 4612
  47.5 50.0 %copy-start.3 = (bf16[384,384]{1,0:T(8,128)(2,1)S(1)}, bf16[384,384]{1,0:T(8,128)(2,1)}, u32[]{:S(2)}) copy-start(bf16[384,384]{1,0:T(8,128)(2,1)} %w_query_ref.1) | copy-start | bytes 884740
  47.5 69.0 %collective-permute-start.6 = (bf16[256,384]{1,0:T(8,128)(2,1)S(1)}, bf16[256,384]{1,0:T(8,128)(2,1)}, u32[]{:S(2)}, u32[]{:S(2)}) collective-permute-start(bf16[256,384]{1,0:T(8,128)(2,1)S(1)} %bitcast.99), channel_id=1, source_target_pairs={{32,0},{48,16},{64,32},{80,48},{96,64},{112,80},{128,96},{144,112}... | collective-permute-start | bytes 589832 | tf_op jit(solution)/shard_map/ppermute | solution.py:244
  52.3 64.2 %collective-permute-start.5 = (bf16[256,384]{1,0:T(8,128)(2,1)S(1)}, bf16[256,384]{1,0:T(8,128)(2,1)}, u32[]{:S(2)}, u32[]{:S(2)}) collective-permute-start(bf16[256,384]{1,0:T(8,128)(2,1)S(1)} %bitcast.100), channel_id=1, source_target_pairs={{16,0},{32,16},{48,32},{64,48},{80,64},{96,80},{112,96},{128,112},... | collective-permute-start | bytes 589832 | tf_op jit(solution)/shard_map/ppermute | solution.py:244
  96.3 52.9 %collective-permute-start.11 = (bf16[27,384,384]{2,1,0:T(8,128)(2,1)}, bf16[27,384,384]{2,1,0:T(8,128)(2,1)}, u32[]{:S(2)}, u32[]{:S(2)}) collective-permute-start(bf16[27,384,384]{2,1,0:T(8,128)(2,1)} %bitcast.104), channel_id=1, source_target_pairs={{0,32},{32,0},{64,96},{96,64},{128,160},{160,128},{192,224},{224,1... | collective-permute-start | bytes 23887880 | tf_op jit(solution)/shard_map/ppermute | solution.py:249
  97.8 1.6 copy-start.6
  99.4 1.2 copy-start.5
  100.5 1.0 copy-start.2
  102.6 1.8 copy-start.4
  102.6 1.8 copy-start.1
  104.5 2.6 %copy-start.16 = (f32[384]{0:T(512)S(1)}, f32[384]{0:T(512)}, u32[]{:S(2)}) copy-start(f32[384]{0:T(512)} %param.18) | copy-start | bytes 4612
  108.0 8.5 %collective-permute-start.1 = (bf16[256,384]{1,0:T(8,128)(2,1)S(1)}, bf16[256,384]{1,0:T(8,128)(2,1)S(1)}, u32[]{:S(2)}, u32[]{:S(2)}) collective-permute-start(bf16[256,384]{1,0:T(8,128)(2,1)S(1)} %fusion.26), channel_id=1, source_target_pairs={{0,16},{16,32},{32,48},{48,64},{64,80},{80,96},{96,112},{112,128},... | collective-permute-start | bytes 589832 | tf_op jit(solution)/shard_map/ppermute | solution.py:244
  111.2 7.0 %collective-permute-start = (bf16[256,384]{1,0:T(8,128)(2,1)S(1)}, bf16[256,384]{1,0:T(8,128)(2,1)S(1)}, u32[]{:S(2)}, u32[]{:S(2)}) collective-permute-start(bf16[256,384]{1,0:T(8,128)(2,1)S(1)} %fusion.26), channel_id=1, source_target_pairs={{0,32},{16,48},{32,64},{48,80},{64,96},{80,112},{96,128},{112,144}... | collective-permute-start | bytes 589832 | tf_op jit(solution)/shard_map/ppermute | solution.py:244
  119.4 2.4 %collective-permute-start.7 = (bf16[3,18,16,384]{3,2,1,0:T(8,128)(2,1)S(1)}, bf16[3,18,16,384]{3,2,1,0:T(8,128)(2,1)S(1)}, u32[]{:S(2)}, u32[]{:S(2)}) collective-permute-start(bf16[3,18,16,384]{3,2,1,0:T(8,128)(2,1)S(1)} %get-tuple-element.15), channel_id=1, source_target_pairs={{0,32},{32,0},{64,96},{96,64},{128,160},{160,128},{192,224},{224,1... | collective-permute-start | bytes 1990664 | tf_op jit(solution)/shard_map/ppermute | solution.py:308
  133.2 2.0 %copy-start.17 = (f32[384]{0:T(512)S(1)}, f32[384]{0:T(512)}, u32[]{:S(2)}) copy-start(f32[384]{0:T(512)} %param.19) | copy-start | bytes 4612
  133.3 1.8 collective-permute-start.8
  135.1 6.4 %copy-start.7 = (bf16[256,384]{1,0:T(8,128)(2,1)S(1)}, bf16[256,384]{1,0:T(8,128)(2,1)}, u32[]{:S(2)}) copy-start(bf16[256,384]{1,0:T(8,128)(2,1)} %copy-done.6) | copy-start | bytes 589828
  135.9 11.7 %collective-permute-start.10 = (bf16[256,384]{1,0:T(8,128)(2,1)S(1)}, bf16[256,384]{1,0:T(8,128)(2,1)S(1)}, u32[]{:S(2)}, u32[]{:S(2)}) collective-permute-start(bf16[256,384]{1,0:T(8,128)(2,1)S(1)} %fusion.41), channel_id=1, source_target_pairs={{32,0},{48,16},{64,32},{80,48},{96,64},{112,80},{128,96},{144,112}... | collective-permute-start | bytes 589832 | tf_op jit(solution)/shard_map/ppermute | solution.py:244
  137.9 11.1 %collective-permute-start.9 = (bf16[256,384]{1,0:T(8,128)(2,1)S(1)}, bf16[256,384]{1,0:T(8,128)(2,1)S(1)}, u32[]{:S(2)}, u32[]{:S(2)}) collective-permute-start(bf16[256,384]{1,0:T(8,128)(2,1)S(1)} %fusion.41), channel_id=1, source_target_pairs={{16,0},{32,16},{48,32},{64,48},{80,64},{96,80},{112,96},{128,112},... | collective-permute-start | bytes 589832 | tf_op jit(solution)/shard_map/ppermute | solution.py:244
  166.1 27.9 %all-to-all-start.1 = ((bf16[32,64,384]{2,1,0:T(8,128)(2,1)}), bf16[32,64,384]{2,1,0:T(8,128)(2,1)S(1)}, u32[]{:S(2)}, u32[]{:S(2)}) async-start(bf16[32,64,384]{2,1,0:T(8,128)(2,1)} %bitcast.35), calls=%async_computation.1 | async-start | bytes 3145728 | tf_op jit(solution)/shard_map/all_to_all | solution.py:332
  171.9 22.2 %copy-start.9 = (bf16[2,8,8,384]{3,2,1,0:T(8,128)(2,1)S(1)}, bf16[2,8,8,384]{3,2,1,0:T(8,128)(2,1)}, u32[]{:S(2)}) copy-start(bf16[2,8,8,384]{3,2,1,0:T(8,128)(2,1)} %param.11) | copy-start | bytes 294916
  172.0 20.6 %collective-permute-start.12 = (bf16[8,8,384]{2,1,0:T(8,128)(2,1)S(1)}, bf16[8,8,384]{2,1,0:T(8,128)(2,1)S(1)}, u32[]{:S(2)}, u32[]{:S(2)}) collective-permute-start(bf16[8,8,384]{2,1,0:T(8,128)(2,1)S(1)} %dynamic-slice_bitcast_fusion.3), channel_id=1, source_target_pairs={{0,16},{16,0},{1,17},{17,1},{2,18},{18,2},{3,19},{19,3},{4,20},{20... | collective-permute-start | bytes 147464 | tf_op jit(solution)/shard_map/ppermute | solution.py:338
Sparse Core Ops, SparseCore 0:
  9.8 86.3 all-gather.1

commit v2 on v1

v2 whole, which is shorter than its diff:
```python
import math

import jax
import jax.numpy as jnp
from jax import lax
from jax.experimental import pallas as pl
from jax.experimental.pallas import tpu as pltpu
from jax.sharding import PartitionSpec as P

EPSILON = 1e-06
F32, BF16 = jnp.float32, jnp.bfloat16
C = 384
ROWS, SLOTS = 16, 16
SPAN = ROWS * SLOTS
TILE = ROWS * 8
VMEM = 50 * 1024 * 1024
NT = (((1,), (1,)), ((), ()))


def norm_factor(field):
    return lax.rsqrt(jnp.mean(field * field, axis=-1, keepdims=True) + EPSILON)


def norm_backward(field, gain, upstream):
    factor = norm_factor(field)
    gained = gain * upstream
    return factor * gained - field * factor**3 * jnp.mean(field * gained, axis=-1, keepdims=True)


def silu_slope(pre):
    sig = jax.nn.sigmoid(pre)
    return sig * (1.0 + pre * (1.0 - sig))


def stage_shifts(x_ref, s_ref):
    length = x_ref.shape[1]
    for frame in range(3):
        wide = x_ref[frame].astype(F32)
        s_ref[frame, :, :C] = pltpu.roll(wide, 1, 0).astype(BF16)
        s_ref[frame, :, C : 2 * C] = x_ref[frame]
        s_ref[frame, :, 2 * C :] = pltpu.roll(wide, length - 1, 0).astype(BF16)


def fetch(core, mine_ref, other_ref, w_ref, sem, begin):
    count = w_ref.shape[0] // 3

    def copy(source, triple):
        return pltpu.make_async_copy(
            source.at[pl.ds(3 * (begin + triple), 3)], w_ref.at[pl.ds(3 * triple, 3)], sem.at[triple]
        )

    for triple in range(count):
        if other_ref is None:
            copy(mine_ref, triple).start()
        else:
            pl.when(core == 0)(lambda triple=triple: copy(mine_ref, triple).start())
            pl.when(core != 0)(lambda triple=triple: copy(other_ref, triple).start())
    return lambda triple: copy(mine_ref, triple).wait()


def pair_kernel(core_ref, x_ref, mine_ref, out_ref, s_ref, w_ref, sem):
    pitch, span = 2 * SLOTS, 2 * SPAN
    arrived = fetch(None, mine_ref, None, w_ref, sem, 0)
    stage_shifts(x_ref, s_ref)
    out_ref[...] = jnp.zeros_like(out_ref)
    for triple in range(9):
        arrived(triple)
        depth, down = triple // 3, triple % 3

        @pl.when(core_ref[0] == 0)
        def _():
            window = s_ref[depth, down * pitch : down * pitch + span, :]
            matrix = w_ref[3 * triple : 3 * triple + 3].reshape(3 * C, C)
            out_ref[...] += jnp.dot(window, matrix, preferred_element_type=F32)

        @pl.when(core_ref[0] != 0)
        def _():
            start = (2 - down) * pitch
            total = out_ref[...]
            for across in range(3):
                lane = (2 - across) * C
                window = s_ref[2 - depth, start : start + span, lane : lane + C]
                total += lax.dot_general(
                    window, w_ref[3 * triple + across], NT, preferred_element_type=F32
                )
            out_ref[...] = total


def pair_conv(core, x, mine):
    vmem = pl.BlockSpec(memory_space=pltpu.VMEM)
    return pl.pallas_call(
        pair_kernel,
        out_shape=jax.ShapeDtypeStruct((2 * SPAN, C), F32),
        in_specs=[pl.BlockSpec(memory_space=pltpu.SMEM), vmem, pl.BlockSpec(memory_space=pl.ANY)],
        out_specs=vmem,
        scratch_shapes=[
            pltpu.VMEM((3, x.shape[1], 3 * C), BF16),
            pltpu.VMEM((27, C, C), BF16),
            pltpu.SemaphoreType.DMA((9,)),
        ],
        compiler_params=pltpu.CompilerParams(vmem_limit_bytes=VMEM),
        cost_estimate=pl.CostEstimate(
            flops=2 * 27 * 2 * SPAN * C * C, bytes_accessed=27 * C * C * 2, transcendentals=0
        ),
        name="pair_conv",
    )(core, x, mine)


def back_kernel(depths, core_ref, *refs):
    count = len(depths)
    frame_refs, (mine_ref, other_ref), rest = refs[:count], refs[count : count + 2], refs[count + 2 :]
    if count == 2:
        start_ref, grad_ref, mixed_ref, gain_ref, out_ref, s_ref, wide_ref, tile_ref, w_ref, sem = rest
    else:
        out_ref, s_ref, wide_ref, tile_ref, w_ref, sem = rest
    arrived = fetch(core_ref[0], mine_ref, other_ref, w_ref, sem, 3 * depths[0])
    tile_ref[:, :8, :] = jnp.zeros((3, 8, C), F32)
    tile_ref[:, 8 + TILE :, :] = jnp.zeros((3, 8, C), F32)
    for place, frame_ref in enumerate(frame_refs):
        wide_ref[...] = frame_ref[...].astype(F32)
        for shift in range(3):
            for r in range(ROWS):
                tile_ref[shift, 8 + r * 8 : 16 + r * 8, :] = wide_ref[
                    r * 10 + shift : r * 10 + shift + 8, :
                ]
            for down in range(3):
                s_ref[place, down, :, shift * C : (shift + 1) * C] = tile_ref[
                    shift, down * 8 : down * 8 + TILE, :
                ].astype(BF16)
    total = start_ref[...] if count == 2 else jnp.zeros((TILE, C), F32)
    for triple in range(3 * count):
        arrived(triple)
        place, down = triple // 3, triple % 3
        for across in range(3):
            lane = (2 - across) * C
            window = s_ref[place, 2 - down, :, lane : lane + C]
            total += lax.dot_general(
                window, w_ref[3 * triple + across], NT, preferred_element_type=F32
            )
    if count == 2:
        mixed = mixed_ref[...].astype(F32)
        gain = gain_ref[...]
        slope = silu_slope(mixed * norm_factor(mixed) * gain)
        total = grad_ref[...].astype(F32) + norm_backward(mixed, gain, total * slope)
    out_ref[...] = total.astype(out_ref.dtype)


def back_conv(depths, core, frames, weights, rest=()):
    count = len(depths)
    vmem, remain = pl.BlockSpec(memory_space=pltpu.VMEM), pl.BlockSpec(memory_space=pl.ANY)
    return pl.pallas_call(
        lambda *refs: back_kernel(depths, *refs),
        out_shape=jax.ShapeDtypeStruct((TILE, C), BF16 if rest else F32),
        in_specs=[pl.BlockSpec(memory_space=pltpu.SMEM)]
        + [vmem] * count
        + [remain] * 2
        + [vmem] * len(rest),
        out_specs=vmem,
        scratch_shapes=[
            pltpu.VMEM((count, 3, TILE, 3 * C), BF16),
            pltpu.VMEM((ROWS * 10, C), F32),
            pltpu.VMEM((3, TILE + 16, C), F32),
            pltpu.VMEM((9 * count, C, C), BF16),
            pltpu.SemaphoreType.DMA((3 * count,)),
        ],
        compiler_params=pltpu.CompilerParams(vmem_limit_bytes=VMEM),
        cost_estimate=pl.CostEstimate(
            flops=2 * 9 * count * TILE * C * C, bytes_accessed=9 * count * C * C * 2, transcendentals=0
        ),
        name="back_conv",
    )(core, *frames, *weights, *rest)


CHUNK = 512


def attend_back_kernel(
    col_ref, gm_ref, prob_ref, keys_ref, values_ref, qk_ref, w_out_ref, w_value_ref, w_query_ref,
    out_ref, gp_ref, sum_ref, mix_ref, right_ref,
):
    positions = keys_ref.shape[0]
    count = positions // CHUNK
    inverse_root = 1.0 / math.sqrt(C)
    g_context = lax.dot_general(
        gm_ref[...], w_out_ref[...], NT, preferred_element_type=F32
    ).astype(BF16)
    right_ref[:TILE, :] = qk_ref[...]
    right_ref[TILE:, :] = lax.dot_general(
        g_context, w_value_ref[...], NT, preferred_element_type=F32
    ).astype(BF16)
    delta = jnp.zeros((1, TILE), F32)
    for c in range(count):
        part = pl.ds(c * CHUNK, CHUNK)
        g_prob = lax.dot_general(values_ref[part, :], g_context, NT, preferred_element_type=F32)
        gp_ref[part, :] = g_prob
        delta = delta + jnp.sum(prob_ref[part, :] * g_prob, axis=0, keepdims=True)
    g_query = jnp.zeros((TILE, C), F32)
    for c in range(count):
        part = pl.ds(c * CHUNK, CHUNK)
        prob = prob_ref[part, :]
        g_score = (prob * (gp_ref[part, :] - delta) * inverse_root).astype(BF16)
        mix_ref[:, :TILE] = g_score
        mix_ref[:, TILE:] = prob.astype(BF16)
        sum_ref[part, :] = jnp.dot(mix_ref[...], right_ref[...], preferred_element_type=F32)
        g_query += lax.dot_general(
            g_score, keys_ref[part, :], (((0,), (0,)), ((), ())), preferred_element_type=F32
        )
    high = g_query.astype(BF16)
    low = (g_query - high.astype(F32)).astype(BF16)
    local = lax.dot_general(high, w_query_ref[...], NT, preferred_element_type=F32)
    local += lax.dot_general(low, w_query_ref[...], NT, preferred_element_type=F32)
    for half in range(2):
        start = pl.multiple_of(half * (positions // 2) + col_ref[0] * 64, 64)
        sum_ref[pl.ds(start, 64), :] += local[half * 64 : half * 64 + 64]
    out_ref[...] = sum_ref[...].astype(BF16)


def attend_back(col, gm, prob, keys, values, qk, w_out, w_value, w_query):
    positions = keys.shape[0]
    return pl.pallas_call(
        attend_back_kernel,
        out_shape=jax.ShapeDtypeStruct((positions, C), BF16),
        in_specs=[pl.BlockSpec(memory_space=pltpu.SMEM)] + [pl.BlockSpec(memory_space=pltpu.VMEM)] * 8,
        out_specs=pl.BlockSpec(memory_space=pltpu.VMEM),
        scratch_shapes=[
            pltpu.VMEM((positions, TILE), F32),
            pltpu.VMEM((positions, C), F32),
            pltpu.VMEM((CHUNK, 2 * TILE), BF16),
            pltpu.VMEM((2 * TILE, C), BF16),
        ],
        compiler_params=pltpu.CompilerParams(vmem_limit_bytes=VMEM),
        cost_estimate=pl.CostEstimate(
            flops=10 * positions * TILE * C, bytes_accessed=8 * positions * C, transcendentals=0
        ),
        name="attend_back",
    )(col, gm, prob, keys, values, qk, w_out, w_value, w_query)


def shards(
    latent,
    grad_out,
    norm_gain,
    w_query,
    w_key,
    w_value,
    w_out,
    gain_one,
    gain_two,
    kernel_one,
    kernel_two,
):
    time_row = ("tm", "row")
    tm, row, col = lax.axis_index("tm"), lax.axis_index("row"), lax.axis_index("col")
    groups, cols = lax.axis_size("tm"), lax.axis_size("col")
    frames = groups * 2
    core = lax.rem(tm, 2)
    core_arg, col_arg = core.reshape(1), col.reshape(1)
    inverse_root = 1.0 / math.sqrt(C)
    swap_core = [(i, i ^ 1) for i in range(groups)]
    swap_row = [(0, 1), (1, 0)]

    def moved(value, steps):
        pairs = [(s, s + steps) for s in range(frames) if 0 <= s + steps < frames]
        return lax.ppermute(value, time_row, pairs)

    mine = lax.all_gather(
        jnp.where(core == 0, kernel_one, kernel_two), "col", axis=3, tiled=True
    ).reshape(27, C, C)

    spread = jnp.broadcast_to(latent.reshape(2, 1, 64, C), (2, cols, 64, C)).reshape(-1, 64, C)
    frame = lax.all_to_all(spread, ("row", "col"), 0, 0, tiled=True)
    tiles = frame.reshape(2, cols, 8, 8, C)
    pick = lambda index: lax.dynamic_index_in_dim(tiles, index, 1, keepdims=False)
    before, own, after = (
        pick(jnp.maximum(col - 1, 0)),
        pick(col),
        pick(jnp.minimum(col + 1, cols - 1)),
    )
    empty = jnp.zeros((2, 8, 4, C), BF16)
    window = jnp.concatenate([before[:, :, 6:], own, after[:, :, :2], empty], axis=2)
    window = window.reshape(SPAN, C)
    slot = lax.rem(lax.broadcasted_iota(jnp.int32, (SPAN, 1), 0), SLOTS)
    column = col * 8 + slot - 2
    inside = (column >= 0) & (column < cols * 8)
    wide_frame = frame.reshape(-1, C).astype(F32)
    normed = (wide_frame * norm_factor(wide_frame) * norm_gain).astype(BF16)
    keys = jnp.dot(normed, w_key, preferred_element_type=F32).astype(BF16)
    values = jnp.dot(normed, w_value, preferred_element_type=F32).astype(BF16)
    wide_window = window.astype(F32)
    normed_window = (wide_window * norm_factor(wide_window) * norm_gain).astype(BF16)
    queries = jnp.dot(normed_window, w_query, preferred_element_type=F32).astype(BF16)
    scores = jnp.einsum("kd,qd->kq", keys, queries, preferred_element_type=F32) * inverse_root
    prob = jax.nn.softmax(scores, axis=0)
    context = jnp.einsum(
        "kq,kd->qd", prob.astype(BF16), values, preferred_element_type=F32
    ).astype(BF16)
    mixed = (wide_window + jnp.dot(context, w_out, preferred_element_type=F32)).astype(BF16)
    wide_mixed = mixed.astype(F32)
    act_one = jax.nn.silu(wide_mixed * norm_factor(wide_mixed) * gain_one)
    act_one = jnp.where(inside & (slot < 12), act_one, 0.0).astype(BF16)

    def own_columns(value):
        return value.reshape(ROWS, SLOTS, C)[:, 2:10].reshape(TILE, C)

    own_queries = own_columns(queries)
    own_scores = jnp.einsum("kd,qd->kq", keys, own_queries, preferred_element_type=F32)
    own_prob = jax.nn.softmax(own_scores * inverse_root, axis=0)
    query_key = lax.dot_general(own_queries, w_key, NT, preferred_element_type=F32).astype(BF16)

    def framed(f0, f1, f2):
        stacked = jnp.stack([f.reshape(ROWS, SLOTS, C) for f in (f0, f1, f2)])
        return jnp.pad(stacked, ((0, 0), (1, 1), (0, 0), (0, 0)))

    act_frames = framed(moved(act_one, 2), moved(act_one, 1), act_one)

    keep = lax.dynamic_index_in_dim(grad_out, row, 0, keepdims=False)
    give = lax.dynamic_index_in_dim(grad_out, 1 - row, 0, keepdims=False)
    got = lax.ppermute(give, "row", swap_row)
    tile = jnp.concatenate([jnp.where(row == 0, keep, got), jnp.where(row == 0, got, keep)], axis=0)
    to_right = [(i, i + 1) for i in range(cols - 1)]
    to_left = [(i + 1, i) for i in range(cols - 1)]
    grad = jnp.concatenate(
        [
            lax.ppermute(tile[:, 6:], "col", to_right),
            tile,
            lax.ppermute(tile[:, :2], "col", to_left),
            jnp.zeros((ROWS, 4, C), BF16),
        ],
        axis=1,
    ).reshape(SPAN, C)
    grad_frames = framed(grad, moved(grad, -1), moved(grad, -2))

    ours = jnp.where(core == 0, act_frames, grad_frames)
    theirs = lax.ppermute(jnp.where(core == 0, grad_frames, act_frames), "tm", swap_core)
    both = jnp.stack([ours, theirs], axis=2).reshape(3, (ROWS + 2) * 2 * SLOTS, C)
    both, mine, own_prob, query_key = lax.optimization_barrier((both, mine, own_prob, query_key))
    other = lax.ppermute(mine, "tm", swap_core)
    sums = pair_conv(core_arg, both, mine).reshape(ROWS, 2, SLOTS, C)
    kept = sums[:, 0].reshape(SPAN, C)
    given = lax.ppermute(sums[:, 1].reshape(SPAN, C), "tm", swap_core)
    conv_one = jnp.where(core == 0, kept, given).astype(BF16)
    g_act_two = jnp.where(core == 0, given, kept)
    wide_conv = conv_one.astype(F32)
    pre_two = wide_conv * norm_factor(wide_conv) * gain_two
    g_conv = norm_backward(wide_conv, gain_two, g_act_two * silu_slope(pre_two))
    g_conv = jnp.where(inside, g_conv, 0.0).astype(BF16)
    g_conv = g_conv.reshape(ROWS, SLOTS, C)[:, 1:11].reshape(ROWS * 10, C)
    later = [moved(g_conv, -2), moved(g_conv, -1)]
    weights = (mine, other)
    own_part = back_conv((2,), core_arg, [g_conv], weights)
    rest = (own_part, own_columns(grad), own_columns(mixed), gain_one.reshape(1, C))
    g_mixed = back_conv((0, 1), core_arg, later, weights, rest)

    halves = g_mixed.reshape(2, 8, 8, C)
    stay = lax.dynamic_index_in_dim(halves, row, 0, keepdims=False)
    leave = lax.dynamic_index_in_dim(halves, 1 - row, 0, keepdims=False)
    come = lax.ppermute(leave, "row", swap_row)
    g_tile = jnp.stack([jnp.where(row == 0, stay, come), jnp.where(row == 0, come, stay)])
    partial = attend_back(
        col_arg, g_mixed, own_prob, keys, values, query_key, w_out, w_value, w_query
    )
    partial, g_tile = lax.optimization_barrier((partial, g_tile))
    parts = lax.all_to_all(partial.reshape(-1, 64, C), ("row", "col"), 0, 0, tiled=True)
    g_normed = jnp.sum(parts.reshape(2, cols, 64, C).astype(F32), axis=1).reshape(latent.shape)

    wide_latent = latent.astype(F32)
    return g_tile.astype(F32) + norm_backward(wide_latent, norm_gain, g_normed)


def solution(mesh):
    placed = (
        P("tm", "row", "col", None),
        P("tm", "row", "col", None),
        P(),
        P(),
        P(),
        P(),
        P(),
        P(),
        P(),
        P(None, None, None, "col", None),
        P(None, None, None, "col", None),
    )
    return jax.shard_map(
        shards, mesh=mesh, in_specs=placed, out_specs=P("tm", "row", "col", None), check_vma=False
    )
```

time: 205 us -> 166 us (0.81); the launches traced: 202 us -> 166 us
  waiting for transfers between devices: 95.8 us -> 44 us
  blocking collectives: 0 us -> 26.4 us
  Pallas kernels: 28.1 us -> 20.3 us
  starting transfers between devices: 43 us -> 36.5 us
  matrix products: 6.18 us -> 8.97 us
    all_gather x1, waiting for transfers between devices: 41.4 us -> 13.3 us  [shards(): lax.all_gather(jnp.where(core == 0, kernel_one, kernel_two), 'col', axis=...]
    all_to_all x0 -> x1, blocking collectives: none -> 26.4 us  [shards(): lax.all_to_all(partial.reshape(-1, 64, C), ('row', 'col'), 0, 0, tiled=True)]
    ppermute x1, waiting for transfers between devices: 19.3 us -> 0.01 us  [shards(): come = lax.ppermute(leave, 'row', swap_row)]
    all_to_all x1 -> x0, starting transfers between devices: 5.83 us -> none  [shards(): lax.all_to_all(partial.reshape(-1, 64, C), ('row', 'col'), 0, 0, tiled=True)]
    pallas_call x1 -> x2, Pallas kernels: 9.72 us -> 6.47 us  [back_conv(): pl.pallas_call(lambda *refs: back_kernel(depths, *refs), out_shape=jax.Sh...]
    ppermute x6, waiting for transfers between devices: 8.88 us -> 5.65 us  [moved(): return lax.ppermute(value, time_row, pairs)]
    pallas_call x1, Pallas kernels: 7.23 us -> 4.33 us  [attend_back(): pl.pallas_call(attend_back_kernel, out_shape=jax.ShapeDtypeStruct((positi...]
  transfers between devices with their start and end apart: 16 -> 15, of which waited for: 10 -> 7; matrix products, arithmetic and copies ran while one was open for 8% -> 11% of each run, Pallas kernels for 6% -> 10%
where the time goes in v2:
time: 166 us
  waiting for transfers between devices  44 us (27%)
  starting transfers between devices  36.5 us (22%)
  blocking collectives  26.4 us (16%)
  Pallas kernels  20.3 us (12%)
  between operations  14 us (8%)
  other arithmetic  10.8 us (7%)
  matrix products  8.97 us (5%)
  local copies, waits for them, and re-layouts  4.56 us (3%)
    all_to_all x1, blocking collectives, shards(): lax.all_to_all(partial.reshape(-1, 64, C), ('row', 'col'), 0, 0, tiled=True)  26.4 us
    ppermute x6, starting transfers between devices, moved(): return lax.ppermute(value, time_row, pairs)  20.6 us
    ppermute x1, waiting for transfers between devices, shards(): got = lax.ppermute(give, 'row', swap_row)  17.9 us
    all_gather x1, waiting for transfers between devices, shards(): lax.all_gather(jnp.where(core == 0, kernel_one, kernel_two), 'col', axis=...  13.3 us
    pallas_call x1, Pallas kernels, pair_conv(): pl.pallas_call(pair_kernel, out_shape=jax.ShapeDtypeStruct((2 * SPAN, C),...  9.53 us
    all_to_all x1, starting transfers between devices, shards(): frame = lax.all_to_all(spread, ('row', 'col'), 0, 0, tiled=True)  9.35 us
    pallas_call x2, Pallas kernels, back_conv(): pl.pallas_call(lambda *refs: back_kernel(depths, *refs), out_shape=jax.Sh...  6.47 us
    ppermute x6, waiting for transfers between devices, moved(): return lax.ppermute(value, time_row, pairs)  5.65 us
  transfers between devices with their start and end apart: 15, of which 7 were waited for; matrix products, arithmetic and copies ran while one was open for 11% of the time, Pallas kernels for 10%

profile of v2, /device:TPU:1, one launch (start us, length us, event | category | flops | bytes accessed | tf_op | source)
XLA Modules:
  0.0 165.5 jit_solution(13411854999481761248)
XLA Ops:
  6.5 2.0 %broadcast_select_fusion.1 = bf16[3,3,3,24,384]{4,3,2,1,0:T(8,128)(2,1)} fusion(bf16[3,3,3,24,384]{4,3,2,1,0:T(8,128)(2,1)} %param.20, bf16[3,3,3,24,384]{4,3,2,1,0:T(8,128)(2,1)} %param.21, pred[]{:T(512)S(6)} %eq.4), kind=kLoop, calls=%fused_computation.36 | loop fusion | flops 248832 | bytes 1492993 | tf_op jit(solution)/shard_map/jit(_where)/select_n | solution.py:267
  8.6 1.5 broadcast_in_dim.54
  10.0 9.4 %all-to-all-start = ((bf16[32,64,384]{2,1,0:T(8,128)(2,1)}), bf16[32,64,384]{2,1,0:T(8,128)(2,1)S(1)}, u32[]{:S(2)}, u32[]{:S(2)}) async-start(bf16[32,64,384]{2,1,0:T(8,128)(2,1)} %bitcast.111), calls=%async_computation | async-start | bytes 3145728 | tf_op jit(solution)/shard_map/all_to_all | solution.py:271
  19.4 1.3 collective-permute-start.2
  20.8 17.9 %collective-permute-done.2 = bf16[8,8,384]{2,1,0:T(8,128)(2,1)S(1)} collective-permute-done((bf16[8,8,384]{2,1,0:T(8,128)(2,1)S(1)}, bf16[8,8,384]{2,1,0:T(8,128)(2,1)S(1)}, u32[]{:S(2)}, u32[]{:S(2)}) %collective-permute-start.2) | collective-permute-done | bytes 49184 | tf_op jit(solution)/shard_map/ppermute | solution.py:318
  38.6 0.1 fusion.46
  38.7 3.0 %collective-permute-start.3 = (bf16[16,2,384]{2,1,0:T(2,128)(2,1)S(1)}, bf16[16,2,384]{2,1,0:T(2,128)(2,1)S(1)}, u32[]{:S(2)}, u32[]{:S(2)}) collective-permute-start(bf16[16,2,384]{2,1,0:T(2,128)(2,1)S(1)} %get-tuple-element.34), channel_id=1, source_target_pairs={{0,1},{1,2},{2,3},{3,4},{4,5},{5,6},{6,7},{7,8},{8,9},{9,10},{10,1... | collective-permute-start | bytes 73736 | tf_op jit(solution)/shard_map/ppermute | solution.py:324
  41.8 1.3 collective-permute-start.4
  43.1 0.5 compare_and_fusion
  43.6 0.1 pad.29.clone
  43.7 3.3 %collective-permute-done.4 = bf16[16,2,384]{2,1,0:T(2,128)(2,1)S(1)} collective-permute-done((bf16[16,2,384]{2,1,0:T(2,128)(2,1)S(1)}, bf16[16,2,384]{2,1,0:T(2,128)(2,1)S(1)}, u32[]{:S(2)}, u32[]{:S(2)}) %collective-permute-start.4) | collective-permute-done | bytes 24608 | tf_op jit(solution)/shard_map/ppermute | solution.py:326
  46.9 0.8 maximum_maximum_fusion
  47.7 4.7 %collective-permute-start.6 = (bf16[256,384]{1,0:T(8,128)(2,1)}, bf16[256,384]{1,0:T(8,128)(2,1)}, u32[]{:S(2)}, u32[]{:S(2)}) collective-permute-start(bf16[256,384]{1,0:T(8,128)(2,1)} %bitcast.16), channel_id=1, source_target_pairs={{32,0},{48,16},{64,32},{80,48},{96,64},{112,80},{128,96},{144,112}... | collective-permute-start | bytes 589832 | tf_op jit(solution)/shard_map/ppermute | solution.py:264
  52.4 1.9 %collective-permute-start.5 = (bf16[256,384]{1,0:T(8,128)(2,1)}, bf16[256,384]{1,0:T(8,128)(2,1)}, u32[]{:S(2)}, u32[]{:S(2)}) collective-permute-start(bf16[256,384]{1,0:T(8,128)(2,1)} %bitcast.16), channel_id=1, source_target_pairs={{16,0},{32,16},{48,32},{64,48},{80,64},{96,80},{112,96},{128,112},... | collective-permute-start | bytes 589832 | tf_op jit(solution)/shard_map/ppermute | solution.py:264
  54.3 0.8 fusion.65
  55.1 0.4 multiply_reduce_fusion
  55.5 0.1 rsqrt.54
  55.7 0.2 multiply_reduce_fusion.1
  55.9 0.1 rsqrt.56
  56.0 0.1 maximum_convert_fusion
  56.1 0.1 fusion.37
  56.3 0.3 convolution_convert_fusion.3
  56.5 0.4 fusion.1
  57.0 1.1 convolution_convert_fusion.1.keys_ref
  58.1 0.7 fusion.51
  58.9 1.4 copy-done.6
  60.3 0.4 fusion.2
  60.7 2.3 %convolution_convert_fusion.values_ref = bf16[2048,384]{1,0:T(8,128)(2,1)} fusion(bf16[2048,384]{1,0:T(8,128)(2,1)S(1)} %fusion.1, bf16[384,384]{1,0:T(8,128)(2,1)S(1)} %copy-done.1), kind=kOutput, calls=%fused_computation.5 | convolution fusion | flops 604766208 | bytes 3440640 | tf_op jit(solution)/shard_map/dot_general | solution.py:288
  63.0 3.7 %fusion.10 = (f32[256]{0:T(256)S(1)}, bf16[256,384]{1,0:T(8,128)(2,1)}) fusion(f32[256,384]{1,0:T(8,128)S(1)} %bitcast.114, bf16[384,384]{1,0:T(8,128)(2,1)S(1)} %copy-done.3, bf16[2048,384]{1,0:T(8,128)(2,1)} %convolution_convert_fusion.values_ref, f32[2048,256]{1,0:T(8,128)} %copy-done.6, f32[256]{0:T(256)S(1)} %fusion.2, f32[256]{0:T(256)S(1)} %get-tuple-element.40), kind=kOutput, calls=%fused_computation.39 | convolution fusion | flops 480313088 | bytes 4557824 | tf_op jit(solution)/shard_map/dot_general | solution.py:297
  66.7 1.2 fusion.18
  67.9 3.4 %collective-permute-start.1 = (bf16[256,384]{1,0:T(8,128)(2,1)S(1)}, bf16[256,384]{1,0:T(8,128)(2,1)S(1)}, u32[]{:S(2)}, u32[]{:S(2)}) collective-permute-start(bf16[256,384]{1,0:T(8,128)(2,1)S(1)} %fusion.18), channel_id=1, source_target_pairs={{0,16},{16,32},{32,48},{48,64},{64,80},{80,96},{96,112},{112,128},... | collective-permute-start | bytes 589832 | tf_op jit(solution)/shard_map/ppermute | solution.py:264
  71.3 5.3 %collective-permute-start = (bf16[256,384]{1,0:T(8,128)(2,1)S(1)}, bf16[256,384]{1,0:T(8,128)(2,1)S(1)}, u32[]{:S(2)}, u32[]{:S(2)}) collective-permute-start(bf16[256,384]{1,0:T(8,128)(2,1)S(1)} %fusion.18), channel_id=1, source_target_pairs={{0,32},{16,48},{32,64},{48,80},{64,96},{80,112},{96,128},{112,144}... | collective-permute-start | bytes 589832 | tf_op jit(solution)/shard_map/ppermute | solution.py:264
  76.5 0.6 fusion.52
  77.2 2.0 %collective-permute-done = bf16[256,384]{1,0:T(8,128)(2,1)S(1)} collective-permute-done((bf16[256,384]{1,0:T(8,128)(2,1)S(1)}, bf16[256,384]{1,0:T(8,128)(2,1)S(1)}, u32[]{:S(2)}, u32[]{:S(2)}) %collective-permute-start) | collective-permute-done | bytes 196640 | tf_op jit(solution)/shard_map/ppermute | solution.py:264
  79.2 1.3 select_bitcast_fusion
  80.4 0.1 collective-permute-start.7
  80.5 0.2 convolution_convert_fusion.4.qk_ref
  80.8 0.3 fusion.8
  81.1 0.1 fusion.7.prob_ref
  81.2 1.4 collective-permute-done.7
  82.6 0.2 pad_maximum_fusion
  82.8 0.2 copy.13
  83.0 13.3 %all-gather.2.cloned.1.call-done = bf16[3,3,3,384,384]{4,3,2,1,0:T(8,128)(2,1)} async-done(((bf16[3,3,3,24,384]{4,3,2,1,0:T(8,128)(2,1)}), bf16[3,3,3,384,384]{4,3,2,1,0:T(8,128)(2,1)}) %all-gather.2.cloned.1.call-update) | async-done | bytes 7962640 | tf_op jit(solution)/shard_map/all_gather | solution.py:266
  96.3 0.7 collective-permute-start.11
  96.9 9.5 %pair_conv.1 = f32[512,384]{1,0:T(8,128)S(1)} custom-call(s32[1]{0:T(128)} %bitcast.1.core_ref.refs_0_, bf16[3,576,384]{2,1,0:T(8,128)(2,1)S(1)} %bitcast.102, bf16[27,384,384]{2,1,0:T(8,128)(2,1)} %bitcast.107), custom_call_target="tpu_custom_call" | custom-call | flops 4076863488 | bytes 7962624 | tf_op jit(solution)/shard_map/pair_conv/pallas_call | solution.py:91
  106.5 0.1 fusion.50
  106.6 0.1 collective-permute-start.8
  106.7 0.5 copy-done.14
  107.2 2.5 %collective-permute-done.8 = f32[256,384]{1,0:T(8,128)S(1)} collective-permute-done((f32[256,384]{1,0:T(8,128)S(1)}, f32[256,384]{1,0:T(8,128)S(1)}, u32[]{:S(2)}, u32[]{:S(2)}) %collective-permute-start.8) | collective-permute-done | bytes 393248 | tf_op jit(solution)/shard_map/ppermute | solution.py:340
  109.7 0.1 fusion.19
  109.8 0.4 fusion.34
  110.2 0.2 fusion.33
  110.6 3.4 %collective-permute-start.10 = (bf16[160,384]{1,0:T(8,128)(2,1)S(1)}, bf16[160,384]{1,0:T(8,128)(2,1)S(1)}, u32[]{:S(2)}, u32[]{:S(2)}) collective-permute-start(bf16[160,384]{1,0:T(8,128)(2,1)S(1)} %reshape.183.refs_1_), channel_id=1, source_target_pairs={{16,0},{32,16},{48,32},{64,48},{80,64},{96,80},{112,96},{128,112},... | collective-permute-start | bytes 368648 | tf_op jit(solution)/shard_map/ppermute | solution.py:264
  114.0 1.9 %collective-permute-start.9 = (bf16[160,384]{1,0:T(8,128)(2,1)S(1)}, bf16[160,384]{1,0:T(8,128)(2,1)S(1)}, u32[]{:S(2)}, u32[]{:S(2)}) collective-permute-start(bf16[160,384]{1,0:T(8,128)(2,1)S(1)} %reshape.183.refs_1_), channel_id=1, source_target_pairs={{32,0},{48,16},{64,32},{80,48},{96,64},{112,80},{128,96},{144,112}... | collective-permute-start | bytes 368648 | tf_op jit(solution)/shard_map/ppermute | solution.py:264
  116.0 2.6 %back_conv.2.refs_5_ = f32[128,384]{1,0:T(8,128)S(1)} custom-call(s32[1]{0:T(128)} %bitcast.1.core_ref.refs_0_, bf16[160,384]{1,0:T(8,128)(2,1)S(1)} %reshape.183.refs_1_, bf16[27,384,384]{2,1,0:T(8,128)(2,1)} %bitcast.108, bf16[27,384,384]{2,1,0:T(8,128)(2,1)} %collective-permute-done.11.refs_3_.refs_4_), custom_call_target="tpu_custom_call" | custom-call | flops 339738624 | bytes 2654208 | tf_op jit(solution)/shard_map/back_conv/pallas_call | solution.py:151
  118.6 3.6 %collective-permute-done.9.refs_1_ = bf16[160,384]{1,0:T(8,128)(2,1)S(1)} collective-permute-done((bf16[160,384]{1,0:T(8,128)(2,1)S(1)}, bf16[160,384]{1,0:T(8,128)(2,1)S(1)}, u32[]{:S(2)}, u32[]{:S(2)}) %collective-permute-start.9) | collective-permute-done | bytes 122912 | tf_op jit(solution)/shard_map/ppermute | solution.py:264
  122.3 3.9 %back_conv.3.gm_ref = bf16[128,384]{1,0:T(8,128)(2,1)S(1)} custom-call(s32[1]{0:T(128)} %bitcast.1.core_ref.refs_0_, bf16[160,384]{1,0:T(8,128)(2,1)S(1)} %collective-permute-done.9.refs_1_, bf16[160,384]{1,0:T(8,128)(2,1)S(1)} %collective-permute-done.10.refs_2_, bf16[27,384,384]{2,1,0:T(8,128)(2,1)} %bitcast.109, ...), custom_call_target="tpu_custom_call" | custom-call | flops 679477248 | bytes 5308416 | tf_op jit(solution)/shard_map/back_conv/pallas_call | solution.py:151
  126.2 0.1 collective-permute-start.12
  126.3 4.3 %attend_back.1 = bf16[2048,384]{1,0:T(8,128)(2,1)S(1)} custom-call(s32[1]{0:T(128)} %bitcast.col_ref, bf16[128,384]{1,0:T(8,128)(2,1)S(1)} %back_conv.3.gm_ref, f32[2048,128]{1,0:T(8,128)S(1)} %fusion.7.prob_ref, bf16[2048,384]{1,0:T(8,128)(2,1)} %copy-done.5, bf16[2048,384]{1,0:T(8,128)(2,1)} %convolution_convert_fusion.values_ref, ...), custom_call_target="tpu_custom_call" | custom-call | flops 1006632960 | bytes 6291456 | tf_op jit(solution)/shard_map/attend_back/pallas_call | solution.py:220
  130.7 26.4 %all_to_all.10 = bf16[32,64,384]{2,1,0:T(8,128)(2,1)S(1)} all-to-all(bf16[32,64,384]{2,1,0:T(8,128)(2,1)S(1)} %bitcast.101), channel_id=1, replica_groups=mesh['tm'=8,'row'=2,'col'=16] {'row','col'}, dimensions={0} | all-to-all | bytes 3145728 | tf_op jit(solution)/shard_map/all_to_all | solution.py:363
  157.0 0.2 convert_reduce_fusion
  157.3 0.5 copy-done.12
  157.7 0.1 fusion.38
  157.9 0.8 fusion.41
  (60 shorter events, 0.5 us)
Async XLA Ops:
  6.5 50.5 %copy-start = (bf16[384,384]{1,0:T(8,128)(2,1)S(1)}, bf16[384,384]{1,0:T(8,128)(2,1)}, u32[]{:S(2)}) copy-start(bf16[384,384]{1,0:T(8,128)(2,1)} %param.15) | copy-start | bytes 884740
  6.5 2.0 %copy-start.7 = (bf16[2,8,8,384]{3,2,1,0:T(8,128)(2,1)S(1)}, bf16[2,8,8,384]{3,2,1,0:T(8,128)(2,1)}, u32[]{:S(2)}) copy-start(bf16[2,8,8,384]{3,2,1,0:T(8,128)(2,1)} %param.11) | copy-start | bytes 294916
  6.5 89.7 %all-gather.2.cloned.1.call-start = ((), (), s32[]{:S(2)}) async-start(), calls=%async_computation.2 | async-start | bytes 8460288 | tf_op jit(solution)/shard_map/all_gather | solution.py:266
  10.0 9.4 %copy-start.10 = (bf16[2,8,8,384]{3,2,1,0:T(8,128)(2,1)S(1)}, bf16[2,8,8,384]{3,2,1,0:T(8,128)(2,1)}, u32[]{:S(2)}) copy-start(bf16[2,8,8,384]{3,2,1,0:T(8,128)(2,1)} %param.12) | copy-start | bytes 294916
  10.0 45.1 %all-to-all-start = ((bf16[32,64,384]{2,1,0:T(8,128)(2,1)}), bf16[32,64,384]{2,1,0:T(8,128)(2,1)S(1)}, u32[]{:S(2)}, u32[]{:S(2)}) async-start(bf16[32,64,384]{2,1,0:T(8,128)(2,1)} %bitcast.111), calls=%async_computation | async-start | bytes 3145728 | tf_op jit(solution)/shard_map/all_to_all | solution.py:271
  19.4 19.2 %collective-permute-start.2 = (bf16[8,8,384]{2,1,0:T(8,128)(2,1)S(1)}, bf16[8,8,384]{2,1,0:T(8,128)(2,1)S(1)}, u32[]{:S(2)}, u32[]{:S(2)}) collective-permute-start(bf16[8,8,384]{2,1,0:T(8,128)(2,1)S(1)} %dynamic-slice_bitcast_fusion.4), channel_id=1, source_target_pairs={{0,16},{16,0},{1,17},{17,1},{2,18},{18,2},{3,19},{19,3},{4,20},{20... | collective-permute-start | bytes 147464 | tf_op jit(solution)/shard_map/ppermute | solution.py:318
  38.7 5.0 %collective-permute-start.3 = (bf16[16,2,384]{2,1,0:T(2,128)(2,1)S(1)}, bf16[16,2,384]{2,1,0:T(2,128)(2,1)S(1)}, u32[]{:S(2)}, u32[]{:S(2)}) collective-permute-start(bf16[16,2,384]{2,1,0:T(2,128)(2,1)S(1)} %get-tuple-element.34), channel_id=1, source_target_pairs={{0,1},{1,2},{2,3},{3,4},{4,5},{5,6},{6,7},{7,8},{8,9},{9,10},{10,1... | collective-permute-start | bytes 73736 | tf_op jit(solution)/shard_map/ppermute | solution.py:324
  41.8 5.2 %collective-permute-start.4 = (bf16[16,2,384]{2,1,0:T(2,128)(2,1)S(1)}, bf16[16,2,384]{2,1,0:T(2,128)(2,1)S(1)}, u32[]{:S(2)}, u32[]{:S(2)}) collective-permute-start(bf16[16,2,384]{2,1,0:T(2,128)(2,1)S(1)} %get-tuple-element.35), channel_id=1, source_target_pairs={{1,0},{2,1},{3,2},{4,3},{5,4},{6,5},{7,6},{8,7},{9,8},{10,9},{11,1... | collective-permute-start | bytes 73736 | tf_op jit(solution)/shard_map/ppermute | solution.py:326
  47.7 29.4 %collective-permute-start.6 = (bf16[256,384]{1,0:T(8,128)(2,1)}, bf16[256,384]{1,0:T(8,128)(2,1)}, u32[]{:S(2)}, u32[]{:S(2)}) collective-permute-start(bf16[256,384]{1,0:T(8,128)(2,1)} %bitcast.16), channel_id=1, source_target_pairs={{32,0},{48,16},{64,32},{80,48},{96,64},{112,80},{128,96},{144,112}... | collective-permute-start | bytes 589832 | tf_op jit(solution)/shard_map/ppermute | solution.py:264
  52.4 24.8 %collective-permute-start.5 = (bf16[256,384]{1,0:T(8,128)(2,1)}, bf16[256,384]{1,0:T(8,128)(2,1)}, u32[]{:S(2)}, u32[]{:S(2)}) collective-permute-start(bf16[256,384]{1,0:T(8,128)(2,1)} %bitcast.16), channel_id=1, source_target_pairs={{16,0},{32,16},{48,32},{64,48},{80,64},{96,80},{112,96},{128,112},... | collective-permute-start | bytes 589832 | tf_op jit(solution)/shard_map/ppermute | solution.py:264
  55.1 1.0 copy-start.11
  55.1 1.1 copy-start.2
  58.1 18.4 %copy-start.5 = (bf16[2048,384]{1,0:T(8,128)(2,1)}, bf16[2048,384]{1,0:T(8,128)(2,1)S(1)}, u32[]{:S(2)}) copy-start(bf16[2048,384]{1,0:T(8,128)(2,1)S(1)} %convolution_convert_fusion.1.keys_ref) | copy-start | bytes 4718596
  58.9 1.4 copy-start.6
  58.9 1.8 %copy-start.1 = (bf16[384,384]{1,0:T(8,128)(2,1)S(1)}, bf16[384,384]{1,0:T(8,128)(2,1)}, u32[]{:S(2)}) copy-start(bf16[384,384]{1,0:T(8,128)(2,1)} %w_value_ref.1) | copy-start | bytes 884740
  60.7 2.3 %copy-start.3 = (bf16[384,384]{1,0:T(8,128)(2,1)S(1)}, bf16[384,384]{1,0:T(8,128)(2,1)}, u32[]{:S(2)}) copy-start(bf16[384,384]{1,0:T(8,128)(2,1)} %w_out_ref.1) | copy-start | bytes 884740
  63.0 3.7 %copy-start.13 = (f32[384]{0:T(512)S(1)}, f32[384]{0:T(512)}, u32[]{:S(2)}) copy-start(f32[384]{0:T(512)} %param.18) | copy-start | bytes 4612
  66.7 12.5 %copy-start.8 = (bf16[1,16,16,384]{3,2,1,0:T(8,128)(2,1)S(1)}, bf16[1,16,16,384]{3,2,1,0:T(8,128)(2,1)}, u32[]{:S(2)}) copy-start(bf16[1,16,16,384]{3,2,1,0:T(8,128)(2,1)} %fusion.65) | copy-start | bytes 589828
  67.9 9.3 %collective-permute-start.1 = (bf16[256,384]{1,0:T(8,128)(2,1)S(1)}, bf16[256,384]{1,0:T(8,128)(2,1)S(1)}, u32[]{:S(2)}, u32[]{:S(2)}) collective-permute-start(bf16[256,384]{1,0:T(8,128)(2,1)S(1)} %fusion.18), channel_id=1, source_target_pairs={{0,16},{16,32},{32,48},{48,64},{64,80},{80,96},{96,112},{112,128},... | collective-permute-start | bytes 589832 | tf_op jit(solution)/shard_map/ppermute | solution.py:264
  71.3 7.9 %collective-permute-start = (bf16[256,384]{1,0:T(8,128)(2,1)S(1)}, bf16[256,384]{1,0:T(8,128)(2,1)S(1)}, u32[]{:S(2)}, u32[]{:S(2)}) collective-permute-start(bf16[256,384]{1,0:T(8,128)(2,1)S(1)} %fusion.18), channel_id=1, source_target_pairs={{0,32},{16,48},{32,64},{48,80},{64,96},{80,112},{96,128},{112,144}... | collective-permute-start | bytes 589832 | tf_op jit(solution)/shard_map/ppermute | solution.py:264
  80.4 2.2 %collective-permute-start.7 = (bf16[3,18,16,384]{3,2,1,0:T(8,128)(2,1)S(1)}, bf16[3,18,16,384]{3,2,1,0:T(8,128)(2,1)S(1)}, u32[]{:S(2)}, u32[]{:S(2)}) collective-permute-start(bf16[3,18,16,384]{3,2,1,0:T(8,128)(2,1)S(1)} %get-tuple-element.27), channel_id=1, source_target_pairs={{0,32},{32,0},{64,96},{96,64},{128,160},{160,128},{192,224},{224,1... | collective-permute-start | bytes 1990664 | tf_op jit(solution)/shard_map/ppermute | solution.py:334
  96.3 19.7 %collective-permute-start.11 = (bf16[27,384,384]{2,1,0:T(8,128)(2,1)}, bf16[27,384,384]{2,1,0:T(8,128)(2,1)}, u32[]{:S(2)}, u32[]{:S(2)}) collective-permute-start(bf16[27,384,384]{2,1,0:T(8,128)(2,1)} %bitcast.106), channel_id=1, source_target_pairs={{0,32},{32,0},{64,96},{96,64},{128,160},{160,128},{192,224},{224,1... | collective-permute-start | bytes 23887880 | tf_op jit(solution)/shard_map/ppermute | solution.py:337
  106.5 0.7 copy-start.14
  106.5 3.3 %copy-start.15 = (f32[384]{0:T(512)S(1)}, f32[384]{0:T(512)}, u32[]{:S(2)}) copy-start(f32[384]{0:T(512)} %param.19) | copy-start | bytes 4612
  106.6 3.1 %collective-permute-start.8 = (f32[256,384]{1,0:T(8,128)S(1)}, f32[256,384]{1,0:T(8,128)S(1)}, u32[]{:S(2)}, u32[]{:S(2)}) collective-permute-start(f32[256,384]{1,0:T(8,128)S(1)} %bitcast.120), channel_id=1, source_target_pairs={{0,32},{32,0},{64,96},{96,64},{128,160},{160,128},{192,224},{224,1... | collective-permute-start | bytes 1179656 | tf_op jit(solution)/shard_map/ppermute | solution.py:340
  109.8 6.1 %copy-start.9 = (bf16[256,384]{1,0:T(8,128)(2,1)S(1)}, bf16[256,384]{1,0:T(8,128)(2,1)}, u32[]{:S(2)}) copy-start(bf16[256,384]{1,0:T(8,128)(2,1)} %get-tuple-element.43) | copy-start | bytes 589828
  110.6 8.0 %collective-permute-start.10 = (bf16[160,384]{1,0:T(8,128)(2,1)S(1)}, bf16[160,384]{1,0:T(8,128)(2,1)S(1)}, u32[]{:S(2)}, u32[]{:S(2)}) collective-permute-start(bf16[160,384]{1,0:T(8,128)(2,1)S(1)} %reshape.183.refs_1_), channel_id=1, source_target_pairs={{16,0},{32,16},{48,32},{64,48},{80,64},{96,80},{112,96},{128,112},... | collective-permute-start | bytes 368648 | tf_op jit(solution)/shard_map/ppermute | solution.py:264
  114.0 8.2 %collective-permute-start.9 = (bf16[160,384]{1,0:T(8,128)(2,1)S(1)}, bf16[160,384]{1,0:T(8,128)(2,1)S(1)}, u32[]{:S(2)}, u32[]{:S(2)}) collective-permute-start(bf16[160,384]{1,0:T(8,128)(2,1)S(1)} %reshape.183.refs_1_), channel_id=1, source_target_pairs={{32,0},{48,16},{64,32},{80,48},{96,64},{112,80},{128,96},{144,112}... | collective-permute-start | bytes 368648 | tf_op jit(solution)/shard_map/ppermute | solution.py:264
  118.6 7.7 %copy-start.4 = (bf16[384,384]{1,0:T(8,128)(2,1)S(1)}, bf16[384,384]{1,0:T(8,128)(2,1)}, u32[]{:S(2)}) copy-start(bf16[384,384]{1,0:T(8,128)(2,1)} %w_out_ref.1) | copy-start | bytes 884740
  126.2 4.4 %collective-permute-start.12 = (bf16[8,8,384]{2,1,0:T(8,128)(2,1)S(1)}, bf16[8,8,384]{2,1,0:T(8,128)(2,1)S(1)}, u32[]{:S(2)}, u32[]{:S(2)}) collective-permute-start(bf16[8,8,384]{2,1,0:T(8,128)(2,1)S(1)} %dynamic-slice_bitcast_fusion.3), channel_id=1, source_target_pairs={{0,16},{16,0},{1,17},{17,1},{2,18},{18,2},{3,19},{19,3},{4,20},{20... | collective-permute-start | bytes 147464 | tf_op jit(solution)/shard_map/ppermute | solution.py:357
  157.0 0.7 copy-start.12
Sparse Core Ops, SparseCore 0:
  9.8 86.3 all-gather.1

commit v3 on v2

--- a/solution.py
+++ b/solution.py
@@ -62,28 +62,38 @@
     pitch, span = 2 * SLOTS, 2 * SPAN
     arrived = fetch(None, mine_ref, None, w_ref, sem, 0)
     stage_shifts(x_ref, s_ref)
-    out_ref[...] = jnp.zeros_like(out_ref)
-    for triple in range(9):
-        arrived(triple)
-        depth, down = triple // 3, triple % 3
+
+    def windows(depth, down, lanes):
+        return s_ref[depth, down * pitch : down * pitch + span, lanes]
+
+    for depth in range(3):
+        for down in range(3):
+            arrived(3 * depth + down)
+        taps = range(9 * depth, 9 * depth + 9)
+
+        def add(term, depth=depth):
+            out_ref[...] = term if depth == 0 else out_ref[...] + term
 
         @pl.when(core_ref[0] == 0)
         def _():
-            window = s_ref[depth, down * pitch : down * pitch + span, :]
-            matrix = w_ref[3 * triple : 3 * triple + 3].reshape(3 * C, C)
-            out_ref[...] += jnp.dot(window, matrix, preferred_element_type=F32)
+            window = jnp.concatenate(
+                [windows(depth, down, slice(0, 3 * C)) for down in range(3)], axis=1
+            )
+            matrix = w_ref[9 * depth : 9 * depth + 9].reshape(9 * C, C)
+            add(jnp.dot(window, matrix, preferred_element_type=F32))
 
         @pl.when(core_ref[0] != 0)
         def _():
-            start = (2 - down) * pitch
-            total = out_ref[...]
-            for across in range(3):
-                lane = (2 - across) * C
-                window = s_ref[2 - depth, start : start + span, lane : lane + C]
-                total += lax.dot_general(
-                    window, w_ref[3 * triple + across], NT, preferred_element_type=F32
-                )
-            out_ref[...] = total
+            window = jnp.concatenate(
+                [
+                    windows(2 - depth, 2 - down, slice((2 - across) * C, (3 - across) * C))
+                    for down in range(3)
+                    for across in range(3)
+                ],
+                axis=1,
+            )
+            matrix = jnp.concatenate([w_ref[tap] for tap in taps], axis=1)
+            add(lax.dot_general(window, matrix, NT, preferred_element_type=F32))
 
 
 def pair_conv(core, x, mine):
@@ -106,29 +116,25 @@
     )(core, x, mine)
 
 
-def back_kernel(depths, core_ref, *refs):
-    count = len(depths)
-    frame_refs, (mine_ref, other_ref), rest = refs[:count], refs[count : count + 2], refs[count + 2 :]
-    if count == 2:
-        start_ref, grad_ref, mixed_ref, gain_ref, out_ref, s_ref, wide_ref, tile_ref, w_ref, sem = rest
-    else:
-        out_ref, s_ref, wide_ref, tile_ref, w_ref, sem = rest
-    arrived = fetch(core_ref[0], mine_ref, other_ref, w_ref, sem, 3 * depths[0])
+def window_of(frame_ref, place, s_ref, wide_ref, tile_ref):
+    wide_ref[...] = frame_ref[...].astype(F32)
+    for shift in range(3):
+        for r in range(ROWS):
+            tile_ref[shift, 8 + r * 8 : 16 + r * 8, :] = wide_ref[
+                r * 10 + shift : r * 10 + shift + 8, :
+            ]
+        for down in range(3):
+            s_ref[place, down, :, shift * C : (shift + 1) * C] = tile_ref[
+                shift, down * 8 : down * 8 + TILE, :
+            ].astype(BF16)
+
+
+def back_taps(frame_refs, arrived, s_ref, wide_ref, tile_ref, w_ref, total):
     tile_ref[:, :8, :] = jnp.zeros((3, 8, C), F32)
     tile_ref[:, 8 + TILE :, :] = jnp.zeros((3, 8, C), F32)
     for place, frame_ref in enumerate(frame_refs):
-        wide_ref[...] = frame_ref[...].astype(F32)
-        for shift in range(3):
-            for r in range(ROWS):
-                tile_ref[shift, 8 + r * 8 : 16 + r * 8, :] = wide_ref[
-                    r * 10 + shift : r * 10 + shift + 8, :
-                ]
-            for down in range(3):
-                s_ref[place, down, :, shift * C : (shift + 1) * C] = tile_ref[
-                    shift, down * 8 : down * 8 + TILE, :
-                ].astype(BF16)
-    total = start_ref[...] if count == 2 else jnp.zeros((TILE, C), F32)
-    for triple in range(3 * count):
+        window_of(frame_ref, place, s_ref, wide_ref, tile_ref)
+    for triple in range(3 * len(frame_refs)):
         arrived(triple)
         place, down = triple // 3, triple % 3
         for across in range(3):
@@ -137,57 +143,81 @@
             total += lax.dot_general(
                 window, w_ref[3 * triple + across], NT, preferred_element_type=F32
             )
-    if count == 2:
-        mixed = mixed_ref[...].astype(F32)
-        gain = gain_ref[...]
-        slope = silu_slope(mixed * norm_factor(mixed) * gain)
-        total = grad_ref[...].astype(F32) + norm_backward(mixed, gain, total * slope)
-    out_ref[...] = total.astype(out_ref.dtype)
-
-
-def back_conv(depths, core, frames, weights, rest=()):
-    count = len(depths)
-    vmem, remain = pl.BlockSpec(memory_space=pltpu.VMEM), pl.BlockSpec(memory_space=pl.ANY)
+    return total
+
+
+def own_kernel(core_ref, frame_ref, mine_ref, other_ref, out_ref, s_ref, wide_ref, tile_ref, w_ref, sem):
+    arrived = fetch(core_ref[0], mine_ref, other_ref, w_ref, sem, 6)
+    zero = jnp.zeros((TILE, C), F32)
+    out_ref[...] = back_taps([frame_ref], arrived, s_ref, wide_ref, tile_ref, w_ref, zero)
+
+
+def back_scratch(count):
+    return [
+        pltpu.VMEM((count, 3, TILE, 3 * C), BF16),
+        pltpu.VMEM((ROWS * 10, C), F32),
+        pltpu.VMEM((3, TILE + 16, C), F32),
+        pltpu.VMEM((9 * count, C, C), BF16),
+        pltpu.SemaphoreType.DMA((3 * count,)),
+    ]
+
+
+def back_own(core, frame, mine, other):
+    smem, vmem = pl.BlockSpec(memory_space=pltpu.SMEM), pl.BlockSpec(memory_space=pltpu.VMEM)
+    remain = pl.BlockSpec(memory_space=pl.ANY)
     return pl.pallas_call(
-        lambda *refs: back_kernel(depths, *refs),
-        out_shape=jax.ShapeDtypeStruct((TILE, C), BF16 if rest else F32),
-        in_specs=[pl.BlockSpec(memory_space=pltpu.SMEM)]
-        + [vmem] * count
-        + [remain] * 2
-        + [vmem] * len(rest),
+        own_kernel,
+        out_shape=jax.ShapeDtypeStruct((TILE, C), F32),
+        in_specs=[smem, vmem, remain, remain],
         out_specs=vmem,
-        scratch_shapes=[
-            pltpu.VMEM((count, 3, TILE, 3 * C), BF16),
-            pltpu.VMEM((ROWS * 10, C), F32),
-            pltpu.VMEM((3, TILE + 16, C), F32),
-            pltpu.VMEM((9 * count, C, C), BF16),
-            pltpu.SemaphoreType.DMA((3 * count,)),
-        ],
+        scratch_shapes=back_scratch(1),
         compiler_params=pltpu.CompilerParams(vmem_limit_bytes=VMEM),
         cost_estimate=pl.CostEstimate(
-            flops=2 * 9 * count * TILE * C * C, bytes_accessed=9 * count * C * C * 2, transcendentals=0
+            flops=2 * 9 * TILE * C * C, bytes_accessed=9 * C * C * 2, transcendentals=0
         ),
-        name="back_conv",
-    )(core, *frames, *weights, *rest)
+        name="back_own",
+    )(core, frame, mine, other)
 
 
 CHUNK = 512
 
 
-def attend_back_kernel(
-    col_ref, gm_ref, prob_ref, keys_ref, values_ref, qk_ref, w_out_ref, w_value_ref, w_query_ref,
-    out_ref, gp_ref, sum_ref, mix_ref, right_ref,
+def back_kernel(
+    core_ref, col_ref, late_ref, soon_ref, mine_ref, other_ref, start_ref, grad_ref, mixed_ref, gain_ref,
+    qk_ref, w_out_ref, w_value_ref, w_query_ref, prob_from, keys_from, values_from,
+    gm_ref, out_ref,
+    s_ref, wide_ref, tile_ref, w_ref, sem, prob_ref, keys_ref, values_ref, in_sem,
+    gp_ref, sum_ref, mix_ref, right_ref,
 ):
+    arrived = fetch(core_ref[0], mine_ref, other_ref, w_ref, sem, 0)
+    pairs = ((values_from, values_ref), (prob_from, prob_ref), (keys_from, keys_ref))
+    inputs = [
+        pltpu.make_async_copy(source, target, in_sem.at[i])
+        for i, (source, target) in enumerate(pairs)
+    ]
+    for copy in inputs:
+        copy.start()
+    total = back_taps(
+        [late_ref, soon_ref], arrived, s_ref, wide_ref, tile_ref, w_ref, start_ref[...]
+    )
+    mixed = mixed_ref[...].astype(F32)
+    gain = gain_ref[...]
+    slope = silu_slope(mixed * norm_factor(mixed) * gain)
+    total = grad_ref[...].astype(F32) + norm_backward(mixed, gain, total * slope)
+    g_mixed = total.astype(BF16)
+    gm_ref[...] = g_mixed
+
     positions = keys_ref.shape[0]
     count = positions // CHUNK
     inverse_root = 1.0 / math.sqrt(C)
-    g_context = lax.dot_general(
-        gm_ref[...], w_out_ref[...], NT, preferred_element_type=F32
-    ).astype(BF16)
+    g_context = lax.dot_general(g_mixed, w_out_ref[...], NT, preferred_element_type=F32)
+    g_context = g_context.astype(BF16)
     right_ref[:TILE, :] = qk_ref[...]
     right_ref[TILE:, :] = lax.dot_general(
         g_context, w_value_ref[...], NT, preferred_element_type=F32
     ).astype(BF16)
+    for copy in inputs:
+        copy.wait()
     delta = jnp.zeros((1, TILE), F32)
     for c in range(count):
         part = pl.ds(c * CHUNK, CHUNK)
@@ -215,14 +245,24 @@
     out_ref[...] = sum_ref[...].astype(BF16)
 
 
-def attend_back(col, gm, prob, keys, values, qk, w_out, w_value, w_query):
-    positions = keys.shape[0]
+def back_rest(core, col, frames, weights, conv_rest, small, large):
+    positions = large[1].shape[0]
+    smem, vmem = pl.BlockSpec(memory_space=pltpu.SMEM), pl.BlockSpec(memory_space=pltpu.VMEM)
+    remain = pl.BlockSpec(memory_space=pl.ANY)
     return pl.pallas_call(
-        attend_back_kernel,
-        out_shape=jax.ShapeDtypeStruct((positions, C), BF16),
-        in_specs=[pl.BlockSpec(memory_space=pltpu.SMEM)] + [pl.BlockSpec(memory_space=pltpu.VMEM)] * 8,
-        out_specs=pl.BlockSpec(memory_space=pltpu.VMEM),
-        scratch_shapes=[
+        back_kernel,
+        out_shape=(
+            jax.ShapeDtypeStruct((TILE, C), BF16),
+            jax.ShapeDtypeStruct((positions, C), BF16),
+        ),
+        in_specs=[smem] * 2 + [vmem] * 2 + [remain] * 2 + [vmem] * 8 + [remain] * 3,
+        out_specs=(vmem, vmem),
+        scratch_shapes=back_scratch(2)
+        + [
+            pltpu.VMEM((positions, TILE), F32),
+            pltpu.VMEM((positions, C), BF16),
+            pltpu.VMEM((positions, C), BF16),
+            pltpu.SemaphoreType.DMA((3,)),
             pltpu.VMEM((positions, TILE), F32),
             pltpu.VMEM((positions, C), F32),
             pltpu.VMEM((CHUNK, 2 * TILE), BF16),
@@ -230,10 +270,12 @@
         ],
         compiler_params=pltpu.CompilerParams(vmem_limit_bytes=VMEM),
         cost_estimate=pl.CostEstimate(
-            flops=10 * positions * TILE * C, bytes_accessed=8 * positions * C, transcendentals=0
+            flops=2 * 18 * TILE * C * C + 10 * positions * TILE * C,
+            bytes_accessed=18 * C * C * 2 + 8 * positions * C,
+            transcendentals=0,
         ),
-        name="attend_back",
-    )(col, gm, prob, keys, values, qk, w_out, w_value, w_query)
+        name="back_rest",
+    )(core, col, *frames, *weights, *conv_rest, *small, *large)
 
 
 def shards(
@@ -337,29 +379,31 @@
     other = lax.ppermute(mine, "tm", swap_core)
     sums = pair_conv(core_arg, both, mine).reshape(ROWS, 2, SLOTS, C)
     kept = sums[:, 0].reshape(SPAN, C)
-    given = lax.ppermute(sums[:, 1].reshape(SPAN, C), "tm", swap_core)
-    conv_one = jnp.where(core == 0, kept, given).astype(BF16)
-    g_act_two = jnp.where(core == 0, given, kept)
+    given = lax.ppermute(sums[:, 1].reshape(SPAN, C).astype(BF16), "tm", swap_core)
+    conv_one = jnp.where(core == 0, kept.astype(BF16), given)
+    g_act_two = jnp.where(core == 0, given.astype(F32), kept)
     wide_conv = conv_one.astype(F32)
     pre_two = wide_conv * norm_factor(wide_conv) * gain_two
     g_conv = norm_backward(wide_conv, gain_two, g_act_two * silu_slope(pre_two))
     g_conv = jnp.where(inside, g_conv, 0.0).astype(BF16)
     g_conv = g_conv.reshape(ROWS, SLOTS, C)[:, 1:11].reshape(ROWS * 10, C)
     later = [moved(g_conv, -2), moved(g_conv, -1)]
-    weights = (mine, other)
-    own_part = back_conv((2,), core_arg, [g_conv], weights)
-    rest = (own_part, own_columns(grad), own_columns(mixed), gain_one.reshape(1, C))
-    g_mixed = back_conv((0, 1), core_arg, later, weights, rest)
+    own_part = back_own(core_arg, g_conv, mine, other)
+    g_mixed, partial = back_rest(
+        core_arg,
+        col_arg,
+        later,
+        (mine, other),
+        (own_part, own_columns(grad), own_columns(mixed), gain_one.reshape(1, C)),
+        (query_key, w_out, w_value, w_query),
+        (own_prob, keys, values),
+    )
 
     halves = g_mixed.reshape(2, 8, 8, C)
     stay = lax.dynamic_index_in_dim(halves, row, 0, keepdims=False)
     leave = lax.dynamic_index_in_dim(halves, 1 - row, 0, keepdims=False)
     come = lax.ppermute(leave, "row", swap_row)
     g_tile = jnp.stack([jnp.where(row == 0, stay, come), jnp.where(row == 0, come, stay)])
-    partial = attend_back(
-        col_arg, g_mixed, own_prob, keys, values, query_key, w_out, w_value, w_query
-    )
-    partial, g_tile = lax.optimization_barrier((partial, g_tile))
     parts = lax.all_to_all(partial.reshape(-1, 64, C), ("row", "col"), 0, 0, tiled=True)
     g_normed = jnp.sum(parts.reshape(2, cols, 64, C).astype(F32), axis=1).reshape(latent.shape)
 

time: 166 us -> 163 us (0.982)
  blocking collectives: 26.4 us -> 0 us
  waiting for transfers between devices: 44 us -> 64.5 us
  starting transfers between devices: 36.5 us -> 43.3 us
  Pallas kernels: 20.3 us -> 18 us
    all_to_all x1 -> x0, blocking collectives: 26.4 us -> none  [shards(): lax.all_to_all(partial.reshape(-1, 64, C), ('row', 'col'), 0, 0, tiled=True)]
    ppermute x1, waiting for transfers between devices: 0.01 us -> 16.1 us  [shards(): come = lax.ppermute(leave, 'row', swap_row)]
    all_to_all x0 -> x1, starting transfers between devices: none -> 5.28 us  [shards(): lax.all_to_all(partial.reshape(-1, 64, C), ('row', 'col'), 0, 0, tiled=True)]
    all_to_all x0 -> x1, waiting for transfers between devices: none -> 2.33 us  [shards(): lax.all_to_all(partial.reshape(-1, 64, C), ('row', 'col'), 0, 0, tiled=True)]
    ppermute x1, waiting for transfers between devices: 2.48 us -> 4.33 us  [shards(): lax.ppermute(sums[:, 1].reshape(SPAN, C).astype(BF16), 'tm', swap_core)]
    pallas_call x3 -> x2, Pallas kernels: 10.8 us -> 10.1 us  [the longest x1 7.52 us: back_rest(): pl.pallas_call(back_kernel, out_shape=(jax.ShapeDtypeStruct((TILE, C), BF...]
  transfers between devices with their start and end apart: 15 -> 16, of which waited for: 7 -> 9; matrix products, arithmetic and copies ran while one was open for 11% -> 11% of each run, Pallas kernels for 10% -> 6%
where the time goes in v3:
time: 163 us
  waiting for transfers between devices  64.5 us (40%)
  starting transfers between devices  43.3 us (27%)
  Pallas kernels  18 us (11%)
  between operations  14 us (9%)
  other arithmetic  10.3 us (6%)
  matrix products  8.98 us (6%)
  local copies, waits for them, and re-layouts  3.6 us (2%)
    ppermute x6, starting transfers between devices, moved(): return lax.ppermute(value, time_row, pairs)  20.8 us
    ppermute x1, waiting for transfers between devices, shards(): got = lax.ppermute(give, 'row', swap_row)  17.9 us
    ppermute x1, waiting for transfers between devices, shards(): come = lax.ppermute(leave, 'row', swap_row)  16.1 us
    all_gather x1, waiting for transfers between devices, shards(): lax.all_gather(jnp.where(core == 0, kernel_one, kernel_two), 'col', axis=...  13.3 us
    all_to_all x1, starting transfers between devices, shards(): frame = lax.all_to_all(spread, ('row', 'col'), 0, 0, tiled=True)  9.35 us
    pallas_call x1, Pallas kernels, pair_conv(): pl.pallas_call(pair_kernel, out_shape=jax.ShapeDtypeStruct((2 * SPAN, C),...  7.88 us
    pallas_call x1, Pallas kernels, back_rest(): pl.pallas_call(back_kernel, out_shape=(jax.ShapeDtypeStruct((TILE, C), BF...  7.52 us
    ppermute x6, waiting for transfers between devices, moved(): return lax.ppermute(value, time_row, pairs)  5.39 us
  transfers between devices with their start and end apart: 16, of which 9 were waited for; matrix products, arithmetic and copies ran while one was open for 11% of the time, Pallas kernels for 6%

profile of v3, /device:TPU:1, one launch (start us, length us, event | category | flops | bytes accessed | tf_op | source)
XLA Modules:
  0.0 162.7 jit_solution(7674486207294035221)
XLA Ops:
  6.5 2.0 %broadcast_select_fusion.1 = bf16[3,3,3,24,384]{4,3,2,1,0:T(8,128)(2,1)} fusion(bf16[3,3,3,24,384]{4,3,2,1,0:T(8,128)(2,1)} %param.20, bf16[3,3,3,24,384]{4,3,2,1,0:T(8,128)(2,1)} %param.21, pred[]{:T(512)S(6)} %eq.5), kind=kLoop, calls=%fused_computation.36 | loop fusion | flops 248832 | bytes 1492993 | tf_op jit(solution)/shard_map/jit(_where)/select_n | solution.py:309
  8.5 0.0 all-gather.2.cloned.1.call-update
  8.6 1.5 broadcast_in_dim.54
  10.0 9.4 %all-to-all-start = ((bf16[32,64,384]{2,1,0:T(8,128)(2,1)}), bf16[32,64,384]{2,1,0:T(8,128)(2,1)S(1)}, u32[]{:S(2)}, u32[]{:S(2)}) async-start(bf16[32,64,384]{2,1,0:T(8,128)(2,1)} %bitcast.111), calls=%async_computation | async-start | bytes 3145728 | tf_op jit(solution)/shard_map/all_to_all | solution.py:313
  19.4 1.3 collective-permute-start.2
  20.8 17.9 %collective-permute-done.2 = bf16[8,8,384]{2,1,0:T(8,128)(2,1)S(1)} collective-permute-done((bf16[8,8,384]{2,1,0:T(8,128)(2,1)S(1)}, bf16[8,8,384]{2,1,0:T(8,128)(2,1)S(1)}, u32[]{:S(2)}, u32[]{:S(2)}) %collective-permute-start.2) | collective-permute-done | bytes 49184 | tf_op jit(solution)/shard_map/ppermute | solution.py:360
  38.6 0.1 fusion.46
  38.7 3.0 %collective-permute-start.3 = (bf16[16,2,384]{2,1,0:T(2,128)(2,1)S(1)}, bf16[16,2,384]{2,1,0:T(2,128)(2,1)S(1)}, u32[]{:S(2)}, u32[]{:S(2)}) collective-permute-start(bf16[16,2,384]{2,1,0:T(2,128)(2,1)S(1)} %get-tuple-element.32), channel_id=1, source_target_pairs={{0,1},{1,2},{2,3},{3,4},{4,5},{5,6},{6,7},{7,8},{8,9},{9,10},{10,1... | collective-permute-start | bytes 73736 | tf_op jit(solution)/shard_map/ppermute | solution.py:366
  41.8 1.3 collective-permute-start.4
  43.1 0.1 pad.29.clone
  43.2 3.8 %collective-permute-done.4 = bf16[16,2,384]{2,1,0:T(2,128)(2,1)S(1)} collective-permute-done((bf16[16,2,384]{2,1,0:T(2,128)(2,1)S(1)}, bf16[16,2,384]{2,1,0:T(2,128)(2,1)S(1)}, u32[]{:S(2)}, u32[]{:S(2)}) %collective-permute-start.4) | collective-permute-done | bytes 24608 | tf_op jit(solution)/shard_map/ppermute | solution.py:368
  46.9 0.8 maximum_maximum_fusion
  47.8 4.7 %collective-permute-start.6 = (bf16[256,384]{1,0:T(8,128)(2,1)}, bf16[256,384]{1,0:T(8,128)(2,1)}, u32[]{:S(2)}, u32[]{:S(2)}) collective-permute-start(bf16[256,384]{1,0:T(8,128)(2,1)} %bitcast.16), channel_id=1, source_target_pairs={{32,0},{48,16},{64,32},{80,48},{96,64},{112,80},{128,96},{144,112}... | collective-permute-start | bytes 589832 | tf_op jit(solution)/shard_map/ppermute | solution.py:306
  52.4 1.9 %collective-permute-start.5 = (bf16[256,384]{1,0:T(8,128)(2,1)}, bf16[256,384]{1,0:T(8,128)(2,1)}, u32[]{:S(2)}, u32[]{:S(2)}) collective-permute-start(bf16[256,384]{1,0:T(8,128)(2,1)} %bitcast.16), channel_id=1, source_target_pairs={{16,0},{32,16},{48,32},{64,48},{80,64},{96,80},{112,96},{128,112},... | collective-permute-start | bytes 589832 | tf_op jit(solution)/shard_map/ppermute | solution.py:306
  54.3 0.8 fusion.64
  55.2 0.4 multiply_reduce_fusion
  55.6 0.1 rsqrt.54
  55.7 0.2 multiply_reduce_fusion.1
  56.0 0.1 rsqrt.56
  56.0 0.1 maximum_convert_fusion
  56.2 0.1 fusion.36
  56.3 0.3 convolution_convert_fusion.3
  56.6 0.4 fusion.1
  57.0 1.1 convolution_convert_fusion.1.keys_from
  58.2 0.7 fusion.50
  58.9 1.4 copy-done.6
  60.3 0.4 fusion.2
  60.7 2.3 %convolution_convert_fusion.values_from = bf16[2048,384]{1,0:T(8,128)(2,1)} fusion(bf16[2048,384]{1,0:T(8,128)(2,1)S(1)} %fusion.1, bf16[384,384]{1,0:T(8,128)(2,1)S(1)} %copy-done.1), kind=kOutput, calls=%fused_computation.5 | convolution fusion | flops 604766208 | bytes 3440640 | tf_op jit(solution)/shard_map/dot_general | solution.py:330
  63.0 3.7 %fusion.10 = (f32[256]{0:T(256)S(1)}, bf16[256,384]{1,0:T(8,128)(2,1)}) fusion(f32[256,384]{1,0:T(8,128)S(1)} %bitcast.115, bf16[384,384]{1,0:T(8,128)(2,1)S(1)} %copy-done.3, bf16[2048,384]{1,0:T(8,128)(2,1)} %convolution_convert_fusion.values_from, f32[2048,256]{1,0:T(8,128)} %copy-done.6, f32[256]{0:T(256)S(1)} %fusion.2, f32[256]{0:T(256)S(1)} %get-tuple-element.38), kind=kOutput, calls=%fused_computation.39 | convolution fusion | flops 480313088 | bytes 4557824 | tf_op jit(solution)/shard_map/dot_general | solution.py:339
  66.7 1.2 fusion.18
  67.9 3.4 %collective-permute-start.1 = (bf16[256,384]{1,0:T(8,128)(2,1)S(1)}, bf16[256,384]{1,0:T(8,128)(2,1)S(1)}, u32[]{:S(2)}, u32[]{:S(2)}) collective-permute-start(bf16[256,384]{1,0:T(8,128)(2,1)S(1)} %fusion.18), channel_id=1, source_target_pairs={{0,16},{16,32},{32,48},{48,64},{64,80},{80,96},{96,112},{112,128},... | collective-permute-start | bytes 589832 | tf_op jit(solution)/shard_map/ppermute | solution.py:306
  71.3 5.3 %collective-permute-start = (bf16[256,384]{1,0:T(8,128)(2,1)S(1)}, bf16[256,384]{1,0:T(8,128)(2,1)S(1)}, u32[]{:S(2)}, u32[]{:S(2)}) collective-permute-start(bf16[256,384]{1,0:T(8,128)(2,1)S(1)} %fusion.18), channel_id=1, source_target_pairs={{0,32},{16,48},{32,64},{48,80},{64,96},{80,112},{96,128},{112,144}... | collective-permute-start | bytes 589832 | tf_op jit(solution)/shard_map/ppermute | solution.py:306
  76.6 0.6 fusion.51
  77.2 2.0 %collective-permute-done = bf16[256,384]{1,0:T(8,128)(2,1)S(1)} collective-permute-done((bf16[256,384]{1,0:T(8,128)(2,1)S(1)}, bf16[256,384]{1,0:T(8,128)(2,1)S(1)}, u32[]{:S(2)}, u32[]{:S(2)}) %collective-permute-start) | collective-permute-done | bytes 196640 | tf_op jit(solution)/shard_map/ppermute | solution.py:306
  79.2 1.3 select_bitcast_fusion
  80.5 0.1 collective-permute-start.7
  80.6 0.2 convolution_convert_fusion.4.qk_ref
  80.8 0.3 fusion.8
  81.1 0.1 fusion.7.prob_from
  81.3 1.4 collective-permute-done.7
  82.7 0.2 pad_maximum_fusion
  82.8 0.1 copy.13
  83.0 13.3 %all-gather.2.cloned.1.call-done = bf16[3,3,3,384,384]{4,3,2,1,0:T(8,128)(2,1)} async-done(((bf16[3,3,3,24,384]{4,3,2,1,0:T(8,128)(2,1)}), bf16[3,3,3,384,384]{4,3,2,1,0:T(8,128)(2,1)}) %all-gather.2.cloned.1.call-update) | async-done | bytes 7962640 | tf_op jit(solution)/shard_map/all_gather | solution.py:308
  96.3 0.7 collective-permute-start.11
  97.0 7.9 %pair_conv.1 = f32[512,384]{1,0:T(8,128)S(1)} custom-call(s32[1]{0:T(128)} %bitcast.core_ref, bf16[3,576,384]{2,1,0:T(8,128)(2,1)S(1)} %bitcast.101, bf16[27,384,384]{2,1,0:T(8,128)(2,1)} %bitcast.107), custom_call_target="tpu_custom_call" | custom-call | flops 4076863488 | bytes 7962624 | tf_op jit(solution)/shard_map/pair_conv/pallas_call | solution.py:101
  104.9 0.1 collective-permute-start.8
  105.1 4.3 %collective-permute-done.8 = bf16[256,384]{1,0:T(8,128)(2,1)S(1)} collective-permute-done((bf16[256,384]{1,0:T(8,128)(2,1)S(1)}, bf16[256,384]{1,0:T(8,128)(2,1)S(1)}, u32[]{:S(2)}, u32[]{:S(2)}) %collective-permute-start.8) | collective-permute-done | bytes 196640 | tf_op jit(solution)/shard_map/ppermute | solution.py:382
  109.4 0.1 fusion.19
  109.6 0.4 fusion.34
  110.0 0.2 fusion.33
  110.2 0.1 slice.46
  110.3 0.1 reshape.184.frame_ref
  110.3 3.4 %collective-permute-start.10 = (bf16[160,384]{1,0:T(8,128)(2,1)S(1)}, bf16[160,384]{1,0:T(8,128)(2,1)S(1)}, u32[]{:S(2)}, u32[]{:S(2)}) collective-permute-start(bf16[160,384]{1,0:T(8,128)(2,1)S(1)} %reshape.184.frame_ref), channel_id=1, source_target_pairs={{16,0},{32,16},{48,32},{64,48},{80,64},{96,80},{112,96},{128,112},... | collective-permute-start | bytes 368648 | tf_op jit(solution)/shard_map/ppermute | solution.py:306
  113.8 2.1 %collective-permute-start.9 = (bf16[160,384]{1,0:T(8,128)(2,1)S(1)}, bf16[160,384]{1,0:T(8,128)(2,1)S(1)}, u32[]{:S(2)}, u32[]{:S(2)}) collective-permute-start(bf16[160,384]{1,0:T(8,128)(2,1)S(1)} %reshape.184.frame_ref), channel_id=1, source_target_pairs={{32,0},{48,16},{64,32},{80,48},{96,64},{112,80},{128,96},{144,112}... | collective-permute-start | bytes 368648 | tf_op jit(solution)/shard_map/ppermute | solution.py:306
  116.0 2.6 %back_own.1.start_ref = f32[128,384]{1,0:T(8,128)S(1)} custom-call(s32[1]{0:T(128)} %bitcast.core_ref, bf16[160,384]{1,0:T(8,128)(2,1)S(1)} %reshape.184.frame_ref, bf16[27,384,384]{2,1,0:T(8,128)(2,1)} %bitcast.108, bf16[27,384,384]{2,1,0:T(8,128)(2,1)} %collective-permute-done.11.other_ref), custom_call_target="tpu_custom_call" | custom-call | flops 339738624 | bytes 2654208 | tf_op jit(solution)/shard_map/back_own/pallas_call | solution.py:168
  118.6 3.4 %collective-permute-done.9.late_ref = bf16[160,384]{1,0:T(8,128)(2,1)S(1)} collective-permute-done((bf16[160,384]{1,0:T(8,128)(2,1)S(1)}, bf16[160,384]{1,0:T(8,128)(2,1)S(1)}, u32[]{:S(2)}, u32[]{:S(2)}) %collective-permute-start.9) | collective-permute-done | bytes 122912 | tf_op jit(solution)/shard_map/ppermute | solution.py:306
  122.0 7.5 %back_rest.1 = (bf16[128,384]{1,0:T(8,128)(2,1)S(1)}, bf16[2048,384]{1,0:T(8,128)(2,1)}) custom-call(s32[1]{0:T(128)} %bitcast.core_ref, s32[1]{0:T(128)} %bitcast.1.col_ref, bf16[160,384]{1,0:T(8,128)(2,1)S(1)} %collective-permute-done.9.late_ref, bf16[160,384]{1,0:T(8,128)(2,1)S(1)} %collective-permute-done.10.soon_ref, bf16[27,384,384]{2,1,0:T(8,128)(2,1)} %bitcast.109, ...), custom_call_target="tpu_custom_call" | custom-call | flops 1686110208 | bytes 11599872 | tf_op jit(solution)/shard_map/back_rest/pallas_call | solution.py:252
  129.5 5.3 %all-to-all-start.1 = ((bf16[32,64,384]{2,1,0:T(8,128)(2,1)}), bf16[32,64,384]{2,1,0:T(8,128)(2,1)S(1)}, u32[]{:S(2)}, u32[]{:S(2)}) async-start(bf16[32,64,384]{2,1,0:T(8,128)(2,1)} %bitcast.114), calls=%async_computation.1 | async-start | bytes 3145728 | tf_op jit(solution)/shard_map/all_to_all | solution.py:407
  134.9 1.3 collective-permute-start.12
  136.2 16.1 %collective-permute-done.12 = bf16[8,8,384]{2,1,0:T(8,128)(2,1)S(1)} collective-permute-done((bf16[8,8,384]{2,1,0:T(8,128)(2,1)S(1)}, bf16[8,8,384]{2,1,0:T(8,128)(2,1)S(1)}, u32[]{:S(2)}, u32[]{:S(2)}) %collective-permute-start.12) | collective-permute-done | bytes 49184 | tf_op jit(solution)/shard_map/ppermute | solution.py:405
  152.3 2.3 %all-to-all-done.1 = bf16[32,64,384]{2,1,0:T(8,128)(2,1)S(1)} async-done(((bf16[32,64,384]{2,1,0:T(8,128)(2,1)}), bf16[32,64,384]{2,1,0:T(8,128)(2,1)S(1)}, u32[]{:S(2)}, u32[]{:S(2)}) %all-to-all-start.1) | async-done | bytes 1572896 | tf_op jit(solution)/shard_map/all_to_all | solution.py:407
  154.7 0.2 convert_reduce_fusion
  154.9 0.1 fusion.37
  155.0 0.8 fusion.40
  (58 shorter events, 0.4 us)
Async XLA Ops:
  6.5 50.5 %copy-start = (bf16[384,384]{1,0:T(8,128)(2,1)S(1)}, bf16[384,384]{1,0:T(8,128)(2,1)}, u32[]{:S(2)}) copy-start(bf16[384,384]{1,0:T(8,128)(2,1)} %param.15) | copy-start | bytes 884740
  6.5 2.0 %copy-start.7 = (bf16[2,8,8,384]{3,2,1,0:T(8,128)(2,1)S(1)}, bf16[2,8,8,384]{3,2,1,0:T(8,128)(2,1)}, u32[]{:S(2)}) copy-start(bf16[2,8,8,384]{3,2,1,0:T(8,128)(2,1)} %param.11) | copy-start | bytes 294916
  6.5 89.7 %all-gather.2.cloned.1.call-start = ((), (), s32[]{:S(2)}) async-start(), calls=%async_computation.2 | async-start | bytes 8460288 | tf_op jit(solution)/shard_map/all_gather | solution.py:308
  10.0 9.4 %copy-start.11 = (bf16[2,8,8,384]{3,2,1,0:T(8,128)(2,1)S(1)}, bf16[2,8,8,384]{3,2,1,0:T(8,128)(2,1)}, u32[]{:S(2)}) copy-start(bf16[2,8,8,384]{3,2,1,0:T(8,128)(2,1)} %param.12) | copy-start | bytes 294916
  10.0 45.1 %all-to-all-start = ((bf16[32,64,384]{2,1,0:T(8,128)(2,1)}), bf16[32,64,384]{2,1,0:T(8,128)(2,1)S(1)}, u32[]{:S(2)}, u32[]{:S(2)}) async-start(bf16[32,64,384]{2,1,0:T(8,128)(2,1)} %bitcast.111), calls=%async_computation | async-start | bytes 3145728 | tf_op jit(solution)/shard_map/all_to_all | solution.py:313
  19.4 19.2 %collective-permute-start.2 = (bf16[8,8,384]{2,1,0:T(8,128)(2,1)S(1)}, bf16[8,8,384]{2,1,0:T(8,128)(2,1)S(1)}, u32[]{:S(2)}, u32[]{:S(2)}) collective-permute-start(bf16[8,8,384]{2,1,0:T(8,128)(2,1)S(1)} %dynamic-slice_bitcast_fusion.4), channel_id=1, source_target_pairs={{0,16},{16,0},{1,17},{17,1},{2,18},{18,2},{3,19},{19,3},{4,20},{20... | collective-permute-start | bytes 147464 | tf_op jit(solution)/shard_map/ppermute | solution.py:360
  38.7 4.5 %collective-permute-start.3 = (bf16[16,2,384]{2,1,0:T(2,128)(2,1)S(1)}, bf16[16,2,384]{2,1,0:T(2,128)(2,1)S(1)}, u32[]{:S(2)}, u32[]{:S(2)}) collective-permute-start(bf16[16,2,384]{2,1,0:T(2,128)(2,1)S(1)} %get-tuple-element.32), channel_id=1, source_target_pairs={{0,1},{1,2},{2,3},{3,4},{4,5},{5,6},{6,7},{7,8},{8,9},{9,10},{10,1... | collective-permute-start | bytes 73736 | tf_op jit(solution)/shard_map/ppermute | solution.py:366
  41.8 5.2 %collective-permute-start.4 = (bf16[16,2,384]{2,1,0:T(2,128)(2,1)S(1)}, bf16[16,2,384]{2,1,0:T(2,128)(2,1)S(1)}, u32[]{:S(2)}, u32[]{:S(2)}) collective-permute-start(bf16[16,2,384]{2,1,0:T(2,128)(2,1)S(1)} %get-tuple-element.33), channel_id=1, source_target_pairs={{1,0},{2,1},{3,2},{4,3},{5,4},{6,5},{7,6},{8,7},{9,8},{10,9},{11,1... | collective-permute-start | bytes 73736 | tf_op jit(solution)/shard_map/ppermute | solution.py:368
  47.8 29.4 %collective-permute-start.6 = (bf16[256,384]{1,0:T(8,128)(2,1)}, bf16[256,384]{1,0:T(8,128)(2,1)}, u32[]{:S(2)}, u32[]{:S(2)}) collective-permute-start(bf16[256,384]{1,0:T(8,128)(2,1)} %bitcast.16), channel_id=1, source_target_pairs={{32,0},{48,16},{64,32},{80,48},{96,64},{112,80},{128,96},{144,112}... | collective-permute-start | bytes 589832 | tf_op jit(solution)/shard_map/ppermute | solution.py:306
  52.4 24.8 %collective-permute-start.5 = (bf16[256,384]{1,0:T(8,128)(2,1)}, bf16[256,384]{1,0:T(8,128)(2,1)}, u32[]{:S(2)}, u32[]{:S(2)}) collective-permute-start(bf16[256,384]{1,0:T(8,128)(2,1)} %bitcast.16), channel_id=1, source_target_pairs={{16,0},{32,16},{48,32},{64,48},{80,64},{96,80},{112,96},{128,112},... | collective-permute-start | bytes 589832 | tf_op jit(solution)/shard_map/ppermute | solution.py:306
  55.2 1.0 copy-start.12
  55.2 1.1 copy-start.2
  58.2 18.4 %copy-start.5 = (bf16[2048,384]{1,0:T(8,128)(2,1)}, bf16[2048,384]{1,0:T(8,128)(2,1)S(1)}, u32[]{:S(2)}) copy-start(bf16[2048,384]{1,0:T(8,128)(2,1)S(1)} %convolution_convert_fusion.1.keys_from) | copy-start | bytes 4718596
  58.9 1.4 copy-start.6
  58.9 1.8 %copy-start.1 = (bf16[384,384]{1,0:T(8,128)(2,1)S(1)}, bf16[384,384]{1,0:T(8,128)(2,1)}, u32[]{:S(2)}) copy-start(bf16[384,384]{1,0:T(8,128)(2,1)} %w_value_ref.1) | copy-start | bytes 884740
  60.7 2.3 %copy-start.3 = (bf16[384,384]{1,0:T(8,128)(2,1)S(1)}, bf16[384,384]{1,0:T(8,128)(2,1)}, u32[]{:S(2)}) copy-start(bf16[384,384]{1,0:T(8,128)(2,1)} %w_out_ref.1) | copy-start | bytes 884740
  63.0 3.7 %copy-start.13 = (f32[384]{0:T(512)S(1)}, f32[384]{0:T(512)}, u32[]{:S(2)}) copy-start(f32[384]{0:T(512)} %param.18) | copy-start | bytes 4612
  66.7 12.5 %copy-start.9 = (bf16[1,16,16,384]{3,2,1,0:T(8,128)(2,1)S(1)}, bf16[1,16,16,384]{3,2,1,0:T(8,128)(2,1)}, u32[]{:S(2)}) copy-start(bf16[1,16,16,384]{3,2,1,0:T(8,128)(2,1)} %fusion.64) | copy-start | bytes 589828
  67.9 9.3 %collective-permute-start.1 = (bf16[256,384]{1,0:T(8,128)(2,1)S(1)}, bf16[256,384]{1,0:T(8,128)(2,1)S(1)}, u32[]{:S(2)}, u32[]{:S(2)}) collective-permute-start(bf16[256,384]{1,0:T(8,128)(2,1)S(1)} %fusion.18), channel_id=1, source_target_pairs={{0,16},{16,32},{32,48},{48,64},{64,80},{80,96},{96,112},{112,128},... | collective-permute-start | bytes 589832 | tf_op jit(solution)/shard_map/ppermute | solution.py:306
  71.3 7.9 %collective-permute-start = (bf16[256,384]{1,0:T(8,128)(2,1)S(1)}, bf16[256,384]{1,0:T(8,128)(2,1)S(1)}, u32[]{:S(2)}, u32[]{:S(2)}) collective-permute-start(bf16[256,384]{1,0:T(8,128)(2,1)S(1)} %fusion.18), channel_id=1, source_target_pairs={{0,32},{16,48},{32,64},{48,80},{64,96},{80,112},{96,128},{112,144}... | collective-permute-start | bytes 589832 | tf_op jit(solution)/shard_map/ppermute | solution.py:306
  80.5 2.2 %collective-permute-start.7 = (bf16[3,18,16,384]{3,2,1,0:T(8,128)(2,1)S(1)}, bf16[3,18,16,384]{3,2,1,0:T(8,128)(2,1)S(1)}, u32[]{:S(2)}, u32[]{:S(2)}) collective-permute-start(bf16[3,18,16,384]{3,2,1,0:T(8,128)(2,1)S(1)} %get-tuple-element.27), channel_id=1, source_target_pairs={{0,32},{32,0},{64,96},{96,64},{128,160},{160,128},{192,224},{224,1... | collective-permute-start | bytes 1990664 | tf_op jit(solution)/shard_map/ppermute | solution.py:376
  96.3 19.7 %collective-permute-start.11 = (bf16[27,384,384]{2,1,0:T(8,128)(2,1)}, bf16[27,384,384]{2,1,0:T(8,128)(2,1)}, u32[]{:S(2)}, u32[]{:S(2)}) collective-permute-start(bf16[27,384,384]{2,1,0:T(8,128)(2,1)} %bitcast.106), channel_id=1, source_target_pairs={{0,32},{32,0},{64,96},{96,64},{128,160},{160,128},{192,224},{224,1... | collective-permute-start | bytes 23887880 | tf_op jit(solution)/shard_map/ppermute | solution.py:379
  104.8 4.7 %copy-start.14 = (f32[384]{0:T(512)S(1)}, f32[384]{0:T(512)}, u32[]{:S(2)}) copy-start(f32[384]{0:T(512)} %param.19) | copy-start | bytes 4612
  104.9 4.5 %collective-permute-start.8 = (bf16[256,384]{1,0:T(8,128)(2,1)S(1)}, bf16[256,384]{1,0:T(8,128)(2,1)S(1)}, u32[]{:S(2)}, u32[]{:S(2)}) collective-permute-start(bf16[256,384]{1,0:T(8,128)(2,1)S(1)} %bitcast.121), channel_id=1, source_target_pairs={{0,32},{32,0},{64,96},{96,64},{128,160},{160,128},{192,224},{224,1... | collective-permute-start | bytes 589832 | tf_op jit(solution)/shard_map/ppermute | solution.py:382
  105.1 10.9 %copy-start.10 = (bf16[256,384]{1,0:T(8,128)(2,1)S(1)}, bf16[256,384]{1,0:T(8,128)(2,1)}, u32[]{:S(2)}) copy-start(bf16[256,384]{1,0:T(8,128)(2,1)} %get-tuple-element.41) | copy-start | bytes 589828
  110.3 8.3 %collective-permute-start.10 = (bf16[160,384]{1,0:T(8,128)(2,1)S(1)}, bf16[160,384]{1,0:T(8,128)(2,1)S(1)}, u32[]{:S(2)}, u32[]{:S(2)}) collective-permute-start(bf16[160,384]{1,0:T(8,128)(2,1)S(1)} %reshape.184.frame_ref), channel_id=1, source_target_pairs={{16,0},{32,16},{48,32},{64,48},{80,64},{96,80},{112,96},{128,112},... | collective-permute-start | bytes 368648 | tf_op jit(solution)/shard_map/ppermute | solution.py:306
  113.8 8.2 %collective-permute-start.9 = (bf16[160,384]{1,0:T(8,128)(2,1)S(1)}, bf16[160,384]{1,0:T(8,128)(2,1)S(1)}, u32[]{:S(2)}, u32[]{:S(2)}) collective-permute-start(bf16[160,384]{1,0:T(8,128)(2,1)S(1)} %reshape.184.frame_ref), channel_id=1, source_target_pairs={{32,0},{48,16},{64,32},{80,48},{96,64},{112,80},{128,96},{144,112}... | collective-permute-start | bytes 368648 | tf_op jit(solution)/shard_map/ppermute | solution.py:306
  116.0 6.0 %copy-start.4 = (bf16[384,384]{1,0:T(8,128)(2,1)S(1)}, bf16[384,384]{1,0:T(8,128)(2,1)}, u32[]{:S(2)}) copy-start(bf16[384,384]{1,0:T(8,128)(2,1)} %w_out_ref.1) | copy-start | bytes 884740
  129.5 25.1 %all-to-all-start.1 = ((bf16[32,64,384]{2,1,0:T(8,128)(2,1)}), bf16[32,64,384]{2,1,0:T(8,128)(2,1)S(1)}, u32[]{:S(2)}, u32[]{:S(2)}) async-start(bf16[32,64,384]{2,1,0:T(8,128)(2,1)} %bitcast.114), calls=%async_computation.1 | async-start | bytes 3145728 | tf_op jit(solution)/shard_map/all_to_all | solution.py:407
  134.8 20.1 %copy-start.8 = (bf16[2,8,8,384]{3,2,1,0:T(8,128)(2,1)S(1)}, bf16[2,8,8,384]{3,2,1,0:T(8,128)(2,1)}, u32[]{:S(2)}) copy-start(bf16[2,8,8,384]{3,2,1,0:T(8,128)(2,1)} %param.11) | copy-start | bytes 294916
  134.9 17.4 %collective-permute-start.12 = (bf16[8,8,384]{2,1,0:T(8,128)(2,1)S(1)}, bf16[8,8,384]{2,1,0:T(8,128)(2,1)S(1)}, u32[]{:S(2)}, u32[]{:S(2)}) collective-permute-start(bf16[8,8,384]{2,1,0:T(8,128)(2,1)S(1)} %dynamic-slice_bitcast_fusion.3), channel_id=1, source_target_pairs={{0,16},{16,0},{1,17},{17,1},{2,18},{18,2},{3,19},{19,3},{4,20},{20... | collective-permute-start | bytes 147464 | tf_op jit(solution)/shard_map/ppermute | solution.py:405
Sparse Core Ops, SparseCore 0:
  9.8 86.3 all-gather.1

commit v4 on v3

--- a/solution.py
+++ b/solution.py
@@ -32,13 +32,12 @@
     return sig * (1.0 + pre * (1.0 - sig))
 
 
-def stage_shifts(x_ref, s_ref):
+def stage_shifts(x_ref, s_ref, frame):
     length = x_ref.shape[1]
-    for frame in range(3):
-        wide = x_ref[frame].astype(F32)
-        s_ref[frame, :, :C] = pltpu.roll(wide, 1, 0).astype(BF16)
-        s_ref[frame, :, C : 2 * C] = x_ref[frame]
-        s_ref[frame, :, 2 * C :] = pltpu.roll(wide, length - 1, 0).astype(BF16)
+    wide = x_ref[frame].astype(F32)
+    s_ref[frame, :, :C] = pltpu.roll(wide, 1, 0).astype(BF16)
+    s_ref[frame, :, C : 2 * C] = x_ref[frame]
+    s_ref[frame, :, 2 * C :] = pltpu.roll(wide, length - 1, 0).astype(BF16)
 
 
 def fetch(core, mine_ref, other_ref, w_ref, sem, begin):
@@ -61,39 +60,41 @@
 def pair_kernel(core_ref, x_ref, mine_ref, out_ref, s_ref, w_ref, sem):
     pitch, span = 2 * SLOTS, 2 * SPAN
     arrived = fetch(None, mine_ref, None, w_ref, sem, 0)
-    stage_shifts(x_ref, s_ref)
 
     def windows(depth, down, lanes):
         return s_ref[depth, down * pitch : down * pitch + span, lanes]
 
-    for depth in range(3):
-        for down in range(3):
-            arrived(3 * depth + down)
-        taps = range(9 * depth, 9 * depth + 9)
-
-        def add(term, depth=depth):
+    def causal(depth):
+        window = jnp.concatenate(
+            [windows(depth, down, slice(0, 3 * C)) for down in range(3)], axis=1
+        )
+        matrix = w_ref[9 * depth : 9 * depth + 9].reshape(9 * C, C)
+        return jnp.dot(window, matrix, preferred_element_type=F32)
+
+    def transposed(depth):
+        window = jnp.concatenate(
+            [
+                windows(2 - depth, 2 - down, slice((2 - across) * C, (3 - across) * C))
+                for down in range(3)
+                for across in range(3)
+            ],
+            axis=1,
+        )
+        matrix = jnp.concatenate([w_ref[9 * depth + tap] for tap in range(9)], axis=1)
+        return lax.dot_general(window, matrix, NT, preferred_element_type=F32)
+
+    def work(order, part):
+        stage_shifts(x_ref, s_ref, order[0])
+        for depth in range(3):
+            for down in range(3):
+                arrived(3 * depth + down)
+            if depth < 2:
+                stage_shifts(x_ref, s_ref, order[depth + 1])
+            term = part(depth)
             out_ref[...] = term if depth == 0 else out_ref[...] + term
 
-        @pl.when(core_ref[0] == 0)
-        def _():
-            window = jnp.concatenate(
-                [windows(depth, down, slice(0, 3 * C)) for down in range(3)], axis=1
-            )
-            matrix = w_ref[9 * depth : 9 * depth + 9].reshape(9 * C, C)
-            add(jnp.dot(window, matrix, preferred_element_type=F32))
-
-        @pl.when(core_ref[0] != 0)
-        def _():
-            window = jnp.concatenate(
-                [
-                    windows(2 - depth, 2 - down, slice((2 - across) * C, (3 - across) * C))
-                    for down in range(3)
-                    for across in range(3)
-                ],
-                axis=1,
-            )
-            matrix = jnp.concatenate([w_ref[tap] for tap in taps], axis=1)
-            add(lax.dot_general(window, matrix, NT, preferred_element_type=F32))
+    pl.when(core_ref[0] == 0)(lambda: work((0, 1, 2), causal))
+    pl.when(core_ref[0] != 0)(lambda: work((2, 1, 0), transposed))
 
 
 def pair_conv(core, x, mine):
@@ -239,10 +240,13 @@
     low = (g_query - high.astype(F32)).astype(BF16)
     local = lax.dot_general(high, w_query_ref[...], NT, preferred_element_type=F32)
     local += lax.dot_general(low, w_query_ref[...], NT, preferred_element_type=F32)
+    start = pl.multiple_of(col_ref[0] * TILE, TILE)
+    sum_ref[pl.ds(start, TILE), :] += local
+    tiles = positions // TILE
     for half in range(2):
-        start = pl.multiple_of(half * (positions // 2) + col_ref[0] * 64, 64)
-        sum_ref[pl.ds(start, 64), :] += local[half * 64 : half * 64 + 64]
-    out_ref[...] = sum_ref[...].astype(BF16)
+        for tile in range(tiles):
+            there, here = (half * tiles + tile) * 64, tile * TILE + half * 64
+            out_ref[there : there + 64, :] = sum_ref[here : here + 64, :].astype(BF16)
 
 
 def back_rest(core, col, frames, weights, conv_rest, small, large):
@@ -309,10 +313,21 @@
         jnp.where(core == 0, kernel_one, kernel_two), "col", axis=3, tiled=True
     ).reshape(27, C, C)
 
-    spread = jnp.broadcast_to(latent.reshape(2, 1, 64, C), (2, cols, 64, C)).reshape(-1, 64, C)
-    frame = lax.all_to_all(spread, ("row", "col"), 0, 0, tiled=True)
-    tiles = frame.reshape(2, cols, 8, 8, C)
-    pick = lambda index: lax.dynamic_index_in_dim(tiles, index, 1, keepdims=False)
+    keep = lax.dynamic_index_in_dim(latent, row, 0, keepdims=False)
+    give = lax.dynamic_index_in_dim(latent, 1 - row, 0, keepdims=False)
+    got = lax.ppermute(give, "row", swap_row)
+    tile = jnp.concatenate([jnp.where(row == 0, keep, got), jnp.where(row == 0, got, keep)], axis=0)
+    side = 4
+    along_x = [[side * y + x for x in range(side)] for y in range(side)]
+    along_y = [[side * y + x for y in range(side)] for x in range(side)]
+
+    def shared(value, members):
+        spread = jnp.broadcast_to(value[None], (side,) + value.shape)
+        return lax.all_to_all(spread, "col", 0, 0, tiled=True, axis_index_groups=members)
+
+    frame = shared(shared(tile.reshape(TILE, C), along_x), along_y)
+    tiles = frame.reshape(cols, 2, 8, 8, C)
+    pick = lambda index: lax.dynamic_index_in_dim(tiles, index, 0, keepdims=False)
     before, own, after = (
         pick(jnp.maximum(col - 1, 0)),
         pick(col),

time: 163 us -> 158 us (0.969)
  waiting for transfers between devices: 64.5 us -> 47.3 us
  blocking collectives: 0 us -> 10 us
  starting transfers between devices: 43.3 us -> 45.2 us
    ppermute x1 -> x2, waiting for transfers between devices: 17.9 us -> 3.36 us  [shards(): got = lax.ppermute(give, 'row', swap_row)]
    all_to_all x0 -> x1, blocking collectives: none -> 10 us  [shared(): lax.all_to_all(spread, 'col', 0, 0, tiled=True, axis_index_groups=members)]
    all_gather x1, waiting for transfers between devices: 13.3 us -> 7.69 us  [shards(): lax.all_gather(jnp.where(core == 0, kernel_one, kernel_two), 'col', axis=...]
    all_to_all x1, starting transfers between devices: 9.35 us -> 4.31 us  [shared(): lax.all_to_all(spread, 'col', 0, 0, tiled=True, axis_index_groups=members)]
    ppermute x6, starting transfers between devices: 20.8 us -> 25.7 us  [moved(): return lax.ppermute(value, time_row, pairs)]
    all_to_all x1, waiting for transfers between devices: 0.01 us -> 3.55 us  [shared(): lax.all_to_all(spread, 'col', 0, 0, tiled=True, axis_index_groups=members)]
    ppermute x1 -> x2, starting transfers between devices: 1.32 us -> 4.1 us  [shards(): got = lax.ppermute(give, 'row', swap_row)]
  transfers between devices with their start and end apart: 16 -> 17, of which waited for: 9 -> 11; matrix products, arithmetic and copies ran while one was open for 11% -> 12% of each run, Pallas kernels for 6% -> 7%
where the time goes in v4:
time: 158 us
  waiting for transfers between devices  47.3 us (30%)
  starting transfers between devices  45.2 us (29%)
  Pallas kernels  18.4 us (12%)
  between operations  13.9 us (9%)
  other arithmetic  10.3 us (7%)
  blocking collectives  10 us (6%)
  matrix products  9 us (6%)
  local copies, waits for them, and re-layouts  3.55 us (2%)
    ppermute x6, starting transfers between devices, moved(): return lax.ppermute(value, time_row, pairs)  25.7 us
    ppermute x1, waiting for transfers between devices, shards(): come = lax.ppermute(leave, 'row', swap_row)  16.1 us
    all_to_all x1, blocking collectives, shared(): lax.all_to_all(spread, 'col', 0, 0, tiled=True, axis_index_groups=members)  10 us
    pallas_call x1, Pallas kernels, pair_conv(): pl.pallas_call(pair_kernel, out_shape=jax.ShapeDtypeStruct((2 * SPAN, C),...  8.3 us
    all_gather x1, waiting for transfers between devices, shards(): lax.all_gather(jnp.where(core == 0, kernel_one, kernel_two), 'col', axis=...  7.69 us
    pallas_call x1, Pallas kernels, back_rest(): pl.pallas_call(back_kernel, out_shape=(jax.ShapeDtypeStruct((TILE, C), BF...  7.5 us
    ppermute x6, waiting for transfers between devices, moved(): return lax.ppermute(value, time_row, pairs)  5.39 us
    all_to_all x1, starting transfers between devices, shards(): lax.all_to_all(partial.reshape(-1, 64, C), ('row', 'col'), 0, 0, tiled=True)  5.27 us
  transfers between devices with their start and end apart: 17, of which 11 were waited for; matrix products, arithmetic and copies ran while one was open for 12% of the time, Pallas kernels for 7%

profile of v4, /device:TPU:1, one launch (start us, length us, event | category | flops | bytes accessed | tf_op | source)
XLA Modules:
  0.0 157.8 jit_solution(17235886670786554739)
XLA Ops:
  6.5 2.0 %broadcast_select_fusion.1 = bf16[3,3,3,24,384]{4,3,2,1,0:T(8,128)(2,1)} fusion(bf16[3,3,3,24,384]{4,3,2,1,0:T(8,128)(2,1)} %param.20, bf16[3,3,3,24,384]{4,3,2,1,0:T(8,128)(2,1)} %param.21, pred[]{:T(512)S(6)} %eq.5), kind=kLoop, calls=%fused_computation.36 | loop fusion | flops 248832 | bytes 1492993 | tf_op jit(solution)/shard_map/jit(_where)/select_n | solution.py:313
  8.6 2.6 %collective-permute-start = (bf16[8,8,384]{2,1,0:T(8,128)(2,1)S(1)}, bf16[8,8,384]{2,1,0:T(8,128)(2,1)S(1)}, u32[]{:S(2)}, u32[]{:S(2)}) collective-permute-start(bf16[8,8,384]{2,1,0:T(8,128)(2,1)S(1)} %dynamic-slice_bitcast_fusion.5), channel_id=1, source_target_pairs={{0,16},{16,0},{1,17},{17,1},{2,18},{18,2},{3,19},{19,3},{4,20},{20... | collective-permute-start | bytes 147464 | tf_op jit(solution)/shard_map/ppermute | solution.py:318
  11.1 1.5 collective-permute-done
  12.7 10.0 %all_to_all.15 = bf16[4,128,384]{2,1,0:T(8,128)(2,1)S(1)} all-to-all(bf16[4,128,384]{2,1,0:T(8,128)(2,1)S(1)} %broadcast_in_dim.33), channel_id=1, replica_groups={{0,1,2,3},{4,5,6,7},{8,9,10,11},{12,13,14,15},{16,17,18,19},{20,21,22,2..., dimensions={0} | all-to-all | bytes 786432 | tf_op jit(solution)/shard_map/all_to_all | solution.py:326
  22.7 1.5 broadcast_in_dim.34
  24.2 4.3 %all-to-all-start.1 = ((bf16[4,4,128,384]{3,2,1,0:T(8,128)(2,1)}), bf16[4,4,128,384]{3,2,1,0:T(8,128)(2,1)S(1)}, u32[]{:S(2)}, u32[]{:S(2)}) async-start(bf16[4,4,128,384]{3,2,1,0:T(8,128)(2,1)} %broadcast_in_dim.34), calls=%async_computation.1 | async-start | bytes 3145728 | tf_op jit(solution)/shard_map/all_to_all | solution.py:326
  28.5 1.5 collective-permute-start.3
  30.1 1.9 %collective-permute-done.3 = bf16[8,8,384]{2,1,0:T(8,128)(2,1)S(1)} collective-permute-done((bf16[8,8,384]{2,1,0:T(8,128)(2,1)S(1)}, bf16[8,8,384]{2,1,0:T(8,128)(2,1)S(1)}, u32[]{:S(2)}, u32[]{:S(2)}) %collective-permute-start.3) | collective-permute-done | bytes 49184 | tf_op jit(solution)/shard_map/ppermute | solution.py:375
  32.0 0.1 fusion.46
  32.1 2.2 %collective-permute-start.4 = (bf16[16,2,384]{2,1,0:T(2,128)(2,1)S(1)}, bf16[16,2,384]{2,1,0:T(2,128)(2,1)S(1)}, u32[]{:S(2)}, u32[]{:S(2)}) collective-permute-start(bf16[16,2,384]{2,1,0:T(2,128)(2,1)S(1)} %get-tuple-element.34), channel_id=1, source_target_pairs={{0,1},{1,2},{2,3},{3,4},{4,5},{5,6},{6,7},{7,8},{8,9},{9,10},{10,1... | collective-permute-start | bytes 73736 | tf_op jit(solution)/shard_map/ppermute | solution.py:381
  34.3 1.3 collective-permute-start.5
  35.6 0.1 pad.29.clone
  35.7 3.6 %collective-permute-done.5 = bf16[16,2,384]{2,1,0:T(2,128)(2,1)S(1)} collective-permute-done((bf16[16,2,384]{2,1,0:T(2,128)(2,1)S(1)}, bf16[16,2,384]{2,1,0:T(2,128)(2,1)S(1)}, u32[]{:S(2)}, u32[]{:S(2)}) %collective-permute-start.5) | collective-permute-done | bytes 24608 | tf_op jit(solution)/shard_map/ppermute | solution.py:383
  39.3 0.8 maximum_maximum_fusion
  40.1 7.0 %collective-permute-start.7 = (bf16[256,384]{1,0:T(8,128)(2,1)}, bf16[256,384]{1,0:T(8,128)(2,1)}, u32[]{:S(2)}, u32[]{:S(2)}) collective-permute-start(bf16[256,384]{1,0:T(8,128)(2,1)} %bitcast.18), channel_id=1, source_target_pairs={{32,0},{48,16},{64,32},{80,48},{96,64},{112,80},{128,96},{144,112}... | collective-permute-start | bytes 589832 | tf_op jit(solution)/shard_map/ppermute | solution.py:310
  47.1 2.8 %collective-permute-start.6 = (bf16[256,384]{1,0:T(8,128)(2,1)}, bf16[256,384]{1,0:T(8,128)(2,1)}, u32[]{:S(2)}, u32[]{:S(2)}) collective-permute-start(bf16[256,384]{1,0:T(8,128)(2,1)} %bitcast.18), channel_id=1, source_target_pairs={{16,0},{32,16},{48,32},{64,48},{80,64},{96,80},{112,96},{128,112},... | collective-permute-start | bytes 589832 | tf_op jit(solution)/shard_map/ppermute | solution.py:310
  49.9 0.8 fusion.64
  50.7 3.5 %all-to-all-done.1 = bf16[4,4,128,384]{3,2,1,0:T(8,128)(2,1)S(1)} async-done(((bf16[4,4,128,384]{3,2,1,0:T(8,128)(2,1)}), bf16[4,4,128,384]{3,2,1,0:T(8,128)(2,1)S(1)}, u32[]{:S(2)}, u32[]{:S(2)}) %all-to-all-start.1) | async-done | bytes 1572896 | tf_op jit(solution)/shard_map/all_to_all | solution.py:326
  54.4 0.2 multiply_reduce_fusion.1
  54.6 0.1 rsqrt.56
  54.7 0.4 multiply_reduce_fusion
  55.1 0.1 maximum_convert_fusion
  55.2 0.1 fusion.36
  55.3 0.3 convolution_convert_fusion.3
  55.6 0.4 fusion.1
  56.1 1.1 convolution_convert_fusion.1.keys_from
  57.2 0.7 fusion.50
  58.0 1.4 copy-done.6
  59.3 0.4 fusion.2
  59.7 2.3 %convolution_convert_fusion.values_from = bf16[2048,384]{1,0:T(8,128)(2,1)} fusion(bf16[2048,384]{1,0:T(8,128)(2,1)S(1)} %fusion.1, bf16[384,384]{1,0:T(8,128)(2,1)S(1)} %copy-done.1), kind=kOutput, calls=%fused_computation.5 | convolution fusion | flops 604766208 | bytes 3440640 | tf_op jit(solution)/shard_map/dot_general | solution.py:345
  62.0 3.7 %fusion.10 = (f32[256]{0:T(256)S(1)}, bf16[256,384]{1,0:T(8,128)(2,1)}) fusion(f32[256,384]{1,0:T(8,128)S(1)} %bitcast.120, bf16[384,384]{1,0:T(8,128)(2,1)S(1)} %copy-done.3, bf16[2048,384]{1,0:T(8,128)(2,1)} %convolution_convert_fusion.values_from, f32[2048,256]{1,0:T(8,128)} %copy-done.6, f32[256]{0:T(256)S(1)} %fusion.2, f32[256]{0:T(256)S(1)} %get-tuple-element.40), kind=kOutput, calls=%fused_computation.39 | convolution fusion | flops 480313088 | bytes 4557824 | tf_op jit(solution)/shard_map/dot_general | solution.py:354
  65.8 1.2 fusion.18
  67.0 3.0 %collective-permute-start.2 = (bf16[256,384]{1,0:T(8,128)(2,1)S(1)}, bf16[256,384]{1,0:T(8,128)(2,1)S(1)}, u32[]{:S(2)}, u32[]{:S(2)}) collective-permute-start(bf16[256,384]{1,0:T(8,128)(2,1)S(1)} %fusion.18), channel_id=1, source_target_pairs={{0,16},{16,32},{32,48},{48,64},{64,80},{80,96},{96,112},{112,128},... | collective-permute-start | bytes 589832 | tf_op jit(solution)/shard_map/ppermute | solution.py:310
  70.0 7.3 %collective-permute-start.1 = (bf16[256,384]{1,0:T(8,128)(2,1)S(1)}, bf16[256,384]{1,0:T(8,128)(2,1)S(1)}, u32[]{:S(2)}, u32[]{:S(2)}) collective-permute-start(bf16[256,384]{1,0:T(8,128)(2,1)S(1)} %fusion.18), channel_id=1, source_target_pairs={{0,32},{16,48},{32,64},{48,80},{64,96},{80,112},{96,128},{112,144}... | collective-permute-start | bytes 589832 | tf_op jit(solution)/shard_map/ppermute | solution.py:310
  77.3 0.6 fusion.51
  77.9 2.0 %collective-permute-done.1 = bf16[256,384]{1,0:T(8,128)(2,1)S(1)} collective-permute-done((bf16[256,384]{1,0:T(8,128)(2,1)S(1)}, bf16[256,384]{1,0:T(8,128)(2,1)S(1)}, u32[]{:S(2)}, u32[]{:S(2)}) %collective-permute-start.1) | collective-permute-done | bytes 196640 | tf_op jit(solution)/shard_map/ppermute | solution.py:310
  79.9 1.2 select_bitcast_fusion
  81.2 0.1 collective-permute-start.8
  81.3 0.2 convolution_convert_fusion.4.qk_ref
  81.5 0.3 fusion.8
  81.8 0.1 fusion.7.prob_from
  82.0 1.4 collective-permute-done.8
  83.4 0.2 pad_maximum_fusion
  83.5 0.1 copy.13
  83.7 7.7 %all-gather.2.cloned.1.call-done = bf16[3,3,3,384,384]{4,3,2,1,0:T(8,128)(2,1)} async-done(((bf16[3,3,3,24,384]{4,3,2,1,0:T(8,128)(2,1)}), bf16[3,3,3,384,384]{4,3,2,1,0:T(8,128)(2,1)}) %all-gather.2.cloned.1.call-update) | async-done | bytes 7962640 | tf_op jit(solution)/shard_map/all_gather | solution.py:312
  91.4 0.7 collective-permute-start.12
  92.0 8.3 %pair_conv.1 = f32[512,384]{1,0:T(8,128)S(1)} custom-call(s32[1]{0:T(128)} %bitcast.core_ref, bf16[3,576,384]{2,1,0:T(8,128)(2,1)S(1)} %bitcast.107, bf16[27,384,384]{2,1,0:T(8,128)(2,1)} %bitcast.113), custom_call_target="tpu_custom_call" | custom-call | flops 4076863488 | bytes 7962624 | tf_op jit(solution)/shard_map/pair_conv/pallas_call | solution.py:102
  100.4 0.2 collective-permute-start.9
  100.7 3.8 %collective-permute-done.9 = bf16[256,384]{1,0:T(8,128)(2,1)S(1)} collective-permute-done((bf16[256,384]{1,0:T(8,128)(2,1)S(1)}, bf16[256,384]{1,0:T(8,128)(2,1)S(1)}, u32[]{:S(2)}, u32[]{:S(2)}) %collective-permute-start.9) | collective-permute-done | bytes 196640 | tf_op jit(solution)/shard_map/ppermute | solution.py:397
  104.5 0.1 fusion.19
  104.7 0.4 fusion.34
  105.1 0.2 fusion.33
  105.4 3.4 %collective-permute-start.11 = (bf16[160,384]{1,0:T(8,128)(2,1)S(1)}, bf16[160,384]{1,0:T(8,128)(2,1)S(1)}, u32[]{:S(2)}, u32[]{:S(2)}) collective-permute-start(bf16[160,384]{1,0:T(8,128)(2,1)S(1)} %reshape.180.frame_ref), channel_id=1, source_target_pairs={{16,0},{32,16},{48,32},{64,48},{80,64},{96,80},{112,96},{128,112},... | collective-permute-start | bytes 368648 | tf_op jit(solution)/shard_map/ppermute | solution.py:310
  108.9 2.1 %collective-permute-start.10 = (bf16[160,384]{1,0:T(8,128)(2,1)S(1)}, bf16[160,384]{1,0:T(8,128)(2,1)S(1)}, u32[]{:S(2)}, u32[]{:S(2)}) collective-permute-start(bf16[160,384]{1,0:T(8,128)(2,1)S(1)} %reshape.180.frame_ref), channel_id=1, source_target_pairs={{32,0},{48,16},{64,32},{80,48},{96,64},{112,80},{128,96},{144,112}... | collective-permute-start | bytes 368648 | tf_op jit(solution)/shard_map/ppermute | solution.py:310
  111.1 2.6 %back_own.1.start_ref = f32[128,384]{1,0:T(8,128)S(1)} custom-call(s32[1]{0:T(128)} %bitcast.core_ref, bf16[160,384]{1,0:T(8,128)(2,1)S(1)} %reshape.180.frame_ref, bf16[27,384,384]{2,1,0:T(8,128)(2,1)} %bitcast.114, bf16[27,384,384]{2,1,0:T(8,128)(2,1)} %collective-permute-done.12.other_ref), custom_call_target="tpu_custom_call" | custom-call | flops 339738624 | bytes 2654208 | tf_op jit(solution)/shard_map/back_own/pallas_call | solution.py:169
  113.7 3.4 %collective-permute-done.10.late_ref = bf16[160,384]{1,0:T(8,128)(2,1)S(1)} collective-permute-done((bf16[160,384]{1,0:T(8,128)(2,1)S(1)}, bf16[160,384]{1,0:T(8,128)(2,1)S(1)}, u32[]{:S(2)}, u32[]{:S(2)}) %collective-permute-start.10) | collective-permute-done | bytes 122912 | tf_op jit(solution)/shard_map/ppermute | solution.py:310
  117.1 7.5 %back_rest.1 = (bf16[128,384]{1,0:T(8,128)(2,1)S(1)}, bf16[2048,384]{1,0:T(8,128)(2,1)}) custom-call(s32[1]{0:T(128)} %bitcast.core_ref, s32[1]{0:T(128)} %bitcast.1.col_ref, bf16[160,384]{1,0:T(8,128)(2,1)S(1)} %collective-permute-done.10.late_ref, bf16[160,384]{1,0:T(8,128)(2,1)S(1)} %collective-permute-done.11.soon_ref, bf16[27,384,384]{2,1,0:T(8,128)(2,1)} %bitcast.115, ...), custom_call_target="tpu_custom_call" | custom-call | flops 1686110208 | bytes 11599872 | tf_op jit(solution)/shard_map/back_rest/pallas_call | solution.py:256
  124.6 5.3 %all-to-all-start.2 = ((bf16[32,64,384]{2,1,0:T(8,128)(2,1)}), bf16[32,64,384]{2,1,0:T(8,128)(2,1)S(1)}, u32[]{:S(2)}, u32[]{:S(2)}) async-start(bf16[32,64,384]{2,1,0:T(8,128)(2,1)} %bitcast.119), calls=%async_computation.2 | async-start | bytes 3145728 | tf_op jit(solution)/shard_map/all_to_all | solution.py:422
  129.9 1.3 collective-permute-start.13
  131.2 16.1 %collective-permute-done.13 = bf16[8,8,384]{2,1,0:T(8,128)(2,1)S(1)} collective-permute-done((bf16[8,8,384]{2,1,0:T(8,128)(2,1)S(1)}, bf16[8,8,384]{2,1,0:T(8,128)(2,1)S(1)}, u32[]{:S(2)}, u32[]{:S(2)}) %collective-permute-start.13) | collective-permute-done | bytes 49184 | tf_op jit(solution)/shard_map/ppermute | solution.py:420
  147.4 2.3 %all-to-all-done.2 = bf16[32,64,384]{2,1,0:T(8,128)(2,1)S(1)} async-done(((bf16[32,64,384]{2,1,0:T(8,128)(2,1)}), bf16[32,64,384]{2,1,0:T(8,128)(2,1)S(1)}, u32[]{:S(2)}, u32[]{:S(2)}) %all-to-all-start.2) | async-done | bytes 1572896 | tf_op jit(solution)/shard_map/all_to_all | solution.py:422
  149.7 0.2 convert_reduce_fusion
  150.0 0.1 fusion.37
  150.1 0.8 fusion.40
  (64 shorter events, 0.6 us)
Async XLA Ops:
  6.5 49.5 %copy-start = (bf16[384,384]{1,0:T(8,128)(2,1)S(1)}, bf16[384,384]{1,0:T(8,128)(2,1)}, u32[]{:S(2)}) copy-start(bf16[384,384]{1,0:T(8,128)(2,1)} %param.15) | copy-start | bytes 884740
  6.5 2.0 %copy-start.7 = (bf16[2,8,8,384]{3,2,1,0:T(8,128)(2,1)S(1)}, bf16[2,8,8,384]{3,2,1,0:T(8,128)(2,1)}, u32[]{:S(2)}) copy-start(bf16[2,8,8,384]{3,2,1,0:T(8,128)(2,1)} %param.11) | copy-start | bytes 294916
  6.5 84.8 %all-gather.2.cloned.1.call-start = ((), (), s32[]{:S(2)}) async-start(), calls=%async_computation.3 | async-start | bytes 8460288 | tf_op jit(solution)/shard_map/all_gather | solution.py:312
  8.6 4.0 %collective-permute-start = (bf16[8,8,384]{2,1,0:T(8,128)(2,1)S(1)}, bf16[8,8,384]{2,1,0:T(8,128)(2,1)S(1)}, u32[]{:S(2)}, u32[]{:S(2)}) collective-permute-start(bf16[8,8,384]{2,1,0:T(8,128)(2,1)S(1)} %dynamic-slice_bitcast_fusion.5), channel_id=1, source_target_pairs={{0,16},{16,0},{1,17},{17,1},{2,18},{18,2},{3,19},{19,3},{4,20},{20... | collective-permute-start | bytes 147464 | tf_op jit(solution)/shard_map/ppermute | solution.py:318
  24.2 4.3 %copy-start.11 = (bf16[2,8,8,384]{3,2,1,0:T(8,128)(2,1)S(1)}, bf16[2,8,8,384]{3,2,1,0:T(8,128)(2,1)}, u32[]{:S(2)}) copy-start(bf16[2,8,8,384]{3,2,1,0:T(8,128)(2,1)} %param.12) | copy-start | bytes 294916
  24.2 30.0 %all-to-all-start.1 = ((bf16[4,4,128,384]{3,2,1,0:T(8,128)(2,1)}), bf16[4,4,128,384]{3,2,1,0:T(8,128)(2,1)S(1)}, u32[]{:S(2)}, u32[]{:S(2)}) async-start(bf16[4,4,128,384]{3,2,1,0:T(8,128)(2,1)} %broadcast_in_dim.34), calls=%async_computation.1 | async-start | bytes 3145728 | tf_op jit(solution)/shard_map/all_to_all | solution.py:326
  28.5 3.4 %collective-permute-start.3 = (bf16[8,8,384]{2,1,0:T(8,128)(2,1)S(1)}, bf16[8,8,384]{2,1,0:T(8,128)(2,1)S(1)}, u32[]{:S(2)}, u32[]{:S(2)}) collective-permute-start(bf16[8,8,384]{2,1,0:T(8,128)(2,1)S(1)} %dynamic-slice_bitcast_fusion.4), channel_id=1, source_target_pairs={{0,16},{16,0},{1,17},{17,1},{2,18},{18,2},{3,19},{19,3},{4,20},{20... | collective-permute-start | bytes 147464 | tf_op jit(solution)/shard_map/ppermute | solution.py:375
  32.1 3.6 %collective-permute-start.4 = (bf16[16,2,384]{2,1,0:T(2,128)(2,1)S(1)}, bf16[16,2,384]{2,1,0:T(2,128)(2,1)S(1)}, u32[]{:S(2)}, u32[]{:S(2)}) collective-permute-start(bf16[16,2,384]{2,1,0:T(2,128)(2,1)S(1)} %get-tuple-element.34), channel_id=1, source_target_pairs={{0,1},{1,2},{2,3},{3,4},{4,5},{5,6},{6,7},{7,8},{8,9},{9,10},{10,1... | collective-permute-start | bytes 73736 | tf_op jit(solution)/shard_map/ppermute | solution.py:381
  34.3 5.0 %collective-permute-start.5 = (bf16[16,2,384]{2,1,0:T(2,128)(2,1)S(1)}, bf16[16,2,384]{2,1,0:T(2,128)(2,1)S(1)}, u32[]{:S(2)}, u32[]{:S(2)}) collective-permute-start(bf16[16,2,384]{2,1,0:T(2,128)(2,1)S(1)} %get-tuple-element.35), channel_id=1, source_target_pairs={{1,0},{2,1},{3,2},{4,3},{5,4},{6,5},{7,6},{8,7},{9,8},{10,9},{11,1... | collective-permute-start | bytes 73736 | tf_op jit(solution)/shard_map/ppermute | solution.py:383
  40.1 37.8 %collective-permute-start.7 = (bf16[256,384]{1,0:T(8,128)(2,1)}, bf16[256,384]{1,0:T(8,128)(2,1)}, u32[]{:S(2)}, u32[]{:S(2)}) collective-permute-start(bf16[256,384]{1,0:T(8,128)(2,1)} %bitcast.18), channel_id=1, source_target_pairs={{32,0},{48,16},{64,32},{80,48},{96,64},{112,80},{128,96},{144,112}... | collective-permute-start | bytes 589832 | tf_op jit(solution)/shard_map/ppermute | solution.py:310
  47.1 30.8 %collective-permute-start.6 = (bf16[256,384]{1,0:T(8,128)(2,1)}, bf16[256,384]{1,0:T(8,128)(2,1)}, u32[]{:S(2)}, u32[]{:S(2)}) collective-permute-start(bf16[256,384]{1,0:T(8,128)(2,1)} %bitcast.18), channel_id=1, source_target_pairs={{16,0},{32,16},{48,32},{64,48},{80,64},{96,80},{112,96},{128,112},... | collective-permute-start | bytes 589832 | tf_op jit(solution)/shard_map/ppermute | solution.py:310
  50.7 4.5 %copy-start.12 = (f32[384]{0:T(512)S(1)}, f32[384]{0:T(512)}, u32[]{:S(2)}) copy-start(f32[384]{0:T(512)} %param.13) | copy-start | bytes 4612
  54.3 1.0 copy-start.2
  57.2 20.1 %copy-start.5 = (bf16[2048,384]{1,0:T(8,128)(2,1)}, bf16[2048,384]{1,0:T(8,128)(2,1)S(1)}, u32[]{:S(2)}) copy-start(bf16[2048,384]{1,0:T(8,128)(2,1)S(1)} %convolution_convert_fusion.1.keys_from) | copy-start | bytes 4718596
  57.9 1.4 copy-start.6
  58.0 1.7 %copy-start.1 = (bf16[384,384]{1,0:T(8,128)(2,1)S(1)}, bf16[384,384]{1,0:T(8,128)(2,1)}, u32[]{:S(2)}) copy-start(bf16[384,384]{1,0:T(8,128)(2,1)} %w_value_ref.1) | copy-start | bytes 884740
  59.7 2.3 %copy-start.3 = (bf16[384,384]{1,0:T(8,128)(2,1)S(1)}, bf16[384,384]{1,0:T(8,128)(2,1)}, u32[]{:S(2)}) copy-start(bf16[384,384]{1,0:T(8,128)(2,1)} %w_out_ref.1) | copy-start | bytes 884740
  62.0 3.8 %copy-start.13 = (f32[384]{0:T(512)S(1)}, f32[384]{0:T(512)}, u32[]{:S(2)}) copy-start(f32[384]{0:T(512)} %param.18) | copy-start | bytes 4612
  65.8 14.2 %copy-start.9 = (bf16[1,16,16,384]{3,2,1,0:T(8,128)(2,1)S(1)}, bf16[1,16,16,384]{3,2,1,0:T(8,128)(2,1)}, u32[]{:S(2)}) copy-start(bf16[1,16,16,384]{3,2,1,0:T(8,128)(2,1)} %fusion.64) | copy-start | bytes 589828
  67.0 10.9 %collective-permute-start.2 = (bf16[256,384]{1,0:T(8,128)(2,1)S(1)}, bf16[256,384]{1,0:T(8,128)(2,1)S(1)}, u32[]{:S(2)}, u32[]{:S(2)}) collective-permute-start(bf16[256,384]{1,0:T(8,128)(2,1)S(1)} %fusion.18), channel_id=1, source_target_pairs={{0,16},{16,32},{32,48},{48,64},{64,80},{80,96},{96,112},{112,128},... | collective-permute-start | bytes 589832 | tf_op jit(solution)/shard_map/ppermute | solution.py:310
  70.0 9.9 %collective-permute-start.1 = (bf16[256,384]{1,0:T(8,128)(2,1)S(1)}, bf16[256,384]{1,0:T(8,128)(2,1)S(1)}, u32[]{:S(2)}, u32[]{:S(2)}) collective-permute-start(bf16[256,384]{1,0:T(8,128)(2,1)S(1)} %fusion.18), channel_id=1, source_target_pairs={{0,32},{16,48},{32,64},{48,80},{64,96},{80,112},{96,128},{112,144}... | collective-permute-start | bytes 589832 | tf_op jit(solution)/shard_map/ppermute | solution.py:310
  81.2 2.2 %collective-permute-start.8 = (bf16[3,18,16,384]{3,2,1,0:T(8,128)(2,1)S(1)}, bf16[3,18,16,384]{3,2,1,0:T(8,128)(2,1)S(1)}, u32[]{:S(2)}, u32[]{:S(2)}) collective-permute-start(bf16[3,18,16,384]{3,2,1,0:T(8,128)(2,1)S(1)} %get-tuple-element.27), channel_id=1, source_target_pairs={{0,32},{32,0},{64,96},{96,64},{128,160},{160,128},{192,224},{224,1... | collective-permute-start | bytes 1990664 | tf_op jit(solution)/shard_map/ppermute | solution.py:391
  91.4 19.7 %collective-permute-start.12 = (bf16[27,384,384]{2,1,0:T(8,128)(2,1)}, bf16[27,384,384]{2,1,0:T(8,128)(2,1)}, u32[]{:S(2)}, u32[]{:S(2)}) collective-permute-start(bf16[27,384,384]{2,1,0:T(8,128)(2,1)} %bitcast.112), channel_id=1, source_target_pairs={{0,32},{32,0},{64,96},{96,64},{128,160},{160,128},{192,224},{224,1... | collective-permute-start | bytes 23887880 | tf_op jit(solution)/shard_map/ppermute | solution.py:394
  100.3 4.3 %copy-start.14 = (f32[384]{0:T(512)S(1)}, f32[384]{0:T(512)}, u32[]{:S(2)}) copy-start(f32[384]{0:T(512)} %param.19) | copy-start | bytes 4612
  100.4 4.1 %collective-permute-start.9 = (bf16[256,384]{1,0:T(8,128)(2,1)S(1)}, bf16[256,384]{1,0:T(8,128)(2,1)S(1)}, u32[]{:S(2)}, u32[]{:S(2)}) collective-permute-start(bf16[256,384]{1,0:T(8,128)(2,1)S(1)} %bitcast.125), channel_id=1, source_target_pairs={{0,32},{32,0},{64,96},{96,64},{128,160},{160,128},{192,224},{224,1... | collective-permute-start | bytes 589832 | tf_op jit(solution)/shard_map/ppermute | solution.py:397
  100.7 10.4 %copy-start.10 = (bf16[256,384]{1,0:T(8,128)(2,1)S(1)}, bf16[256,384]{1,0:T(8,128)(2,1)}, u32[]{:S(2)}) copy-start(bf16[256,384]{1,0:T(8,128)(2,1)} %get-tuple-element.43) | copy-start | bytes 589828
  105.4 8.3 %collective-permute-start.11 = (bf16[160,384]{1,0:T(8,128)(2,1)S(1)}, bf16[160,384]{1,0:T(8,128)(2,1)S(1)}, u32[]{:S(2)}, u32[]{:S(2)}) collective-permute-start(bf16[160,384]{1,0:T(8,128)(2,1)S(1)} %reshape.180.frame_ref), channel_id=1, source_target_pairs={{16,0},{32,16},{48,32},{64,48},{80,64},{96,80},{112,96},{128,112},... | collective-permute-start | bytes 368648 | tf_op jit(solution)/shard_map/ppermute | solution.py:310
  108.9 8.2 %collective-permute-start.10 = (bf16[160,384]{1,0:T(8,128)(2,1)S(1)}, bf16[160,384]{1,0:T(8,128)(2,1)S(1)}, u32[]{:S(2)}, u32[]{:S(2)}) collective-permute-start(bf16[160,384]{1,0:T(8,128)(2,1)S(1)} %reshape.180.frame_ref), channel_id=1, source_target_pairs={{32,0},{48,16},{64,32},{80,48},{96,64},{112,80},{128,96},{144,112}... | collective-permute-start | bytes 368648 | tf_op jit(solution)/shard_map/ppermute | solution.py:310
  111.1 6.0 %copy-start.4 = (bf16[384,384]{1,0:T(8,128)(2,1)S(1)}, bf16[384,384]{1,0:T(8,128)(2,1)}, u32[]{:S(2)}) copy-start(bf16[384,384]{1,0:T(8,128)(2,1)} %w_out_ref.1) | copy-start | bytes 884740
  124.6 25.1 %all-to-all-start.2 = ((bf16[32,64,384]{2,1,0:T(8,128)(2,1)}), bf16[32,64,384]{2,1,0:T(8,128)(2,1)S(1)}, u32[]{:S(2)}, u32[]{:S(2)}) async-start(bf16[32,64,384]{2,1,0:T(8,128)(2,1)} %bitcast.119), calls=%async_computation.2 | async-start | bytes 3145728 | tf_op jit(solution)/shard_map/all_to_all | solution.py:422
  129.9 20.1 %copy-start.8 = (bf16[2,8,8,384]{3,2,1,0:T(8,128)(2,1)S(1)}, bf16[2,8,8,384]{3,2,1,0:T(8,128)(2,1)}, u32[]{:S(2)}) copy-start(bf16[2,8,8,384]{3,2,1,0:T(8,128)(2,1)} %param.11) | copy-start | bytes 294916
  129.9 17.5 %collective-permute-start.13 = (bf16[8,8,384]{2,1,0:T(8,128)(2,1)S(1)}, bf16[8,8,384]{2,1,0:T(8,128)(2,1)S(1)}, u32[]{:S(2)}, u32[]{:S(2)}) collective-permute-start(bf16[8,8,384]{2,1,0:T(8,128)(2,1)S(1)} %dynamic-slice_bitcast_fusion.3), channel_id=1, source_target_pairs={{0,16},{16,0},{1,17},{17,1},{2,18},{18,2},{3,19},{19,3},{4,20},{20... | collective-permute-start | bytes 147464 | tf_op jit(solution)/shard_map/ppermute | solution.py:420
Sparse Core Ops, SparseCore 0:
  9.8 81.4 all-gather.1

commit v5 on v3

--- a/solution.py
+++ b/solution.py
@@ -66,20 +66,22 @@
     def windows(depth, down, lanes):
         return s_ref[depth, down * pitch : down * pitch + span, lanes]
 
-    for depth in range(3):
-        for down in range(3):
-            arrived(3 * depth + down)
-        taps = range(9 * depth, 9 * depth + 9)
-
-        def add(term, depth=depth):
-            out_ref[...] = term if depth == 0 else out_ref[...] + term
+    for group in ((0,), (1, 2), (3, 4, 5), (6, 7, 8)):
+        for triple in group:
+            arrived(triple)
+        depth, first = group[0] // 3, group[0] == 0
+        downs = [triple % 3 for triple in group]
+        taps = range(3 * group[0], 3 * group[-1] + 3)
+
+        def add(term, first=first):
+            out_ref[...] = term if first else out_ref[...] + term
 
         @pl.when(core_ref[0] == 0)
         def _():
             window = jnp.concatenate(
-                [windows(depth, down, slice(0, 3 * C)) for down in range(3)], axis=1
+                [windows(depth, down, slice(0, 3 * C)) for down in downs], axis=1
             )
-            matrix = w_ref[9 * depth : 9 * depth + 9].reshape(9 * C, C)
+            matrix = w_ref[taps[0] : taps[-1] + 1].reshape(len(taps) * C, C)
             add(jnp.dot(window, matrix, preferred_element_type=F32))
 
         @pl.when(core_ref[0] != 0)
@@ -87,7 +89,7 @@
             window = jnp.concatenate(
                 [
                     windows(2 - depth, 2 - down, slice((2 - across) * C, (3 - across) * C))
-                    for down in range(3)
+                    for down in downs
                     for across in range(3)
                 ],
                 axis=1,
@@ -179,7 +181,7 @@
     )(core, frame, mine, other)
 
 
-CHUNK = 512
+CHUNK = 2048
 
 
 def back_kernel(
@@ -187,7 +189,7 @@
     qk_ref, w_out_ref, w_value_ref, w_query_ref, prob_from, keys_from, values_from,
     gm_ref, out_ref,
     s_ref, wide_ref, tile_ref, w_ref, sem, prob_ref, keys_ref, values_ref, in_sem,
-    gp_ref, sum_ref, mix_ref, right_ref,
+    gp_ref, mix_ref, right_ref,
 ):
     arrived = fetch(core_ref[0], mine_ref, other_ref, w_ref, sem, 0)
     pairs = ((values_from, values_ref), (prob_from, prob_ref), (keys_from, keys_ref))
@@ -231,7 +233,11 @@
         g_score = (prob * (gp_ref[part, :] - delta) * inverse_root).astype(BF16)
         mix_ref[:, :TILE] = g_score
         mix_ref[:, TILE:] = prob.astype(BF16)
-        sum_ref[part, :] = jnp.dot(mix_ref[...], right_ref[...], preferred_element_type=F32)
+        sums = jnp.dot(mix_ref[...], right_ref[...], preferred_element_type=F32).astype(BF16)
+        for piece in range(CHUNK // 64):
+            tile, half = c * CHUNK // TILE + piece // 2, piece % 2
+            there = half * (positions // 2) + tile * 64
+            out_ref[there : there + 64, :] = sums[piece * 64 : piece * 64 + 64]
         g_query += lax.dot_general(
             g_score, keys_ref[part, :], (((0,), (0,)), ((), ())), preferred_element_type=F32
         )
@@ -239,10 +245,14 @@
     low = (g_query - high.astype(F32)).astype(BF16)
     local = lax.dot_general(high, w_query_ref[...], NT, preferred_element_type=F32)
     local += lax.dot_general(low, w_query_ref[...], NT, preferred_element_type=F32)
+    own = pl.ds(pl.multiple_of(col_ref[0] * TILE, TILE), TILE)
+    prob = prob_ref[own, :]
+    mix_ref[:TILE, :TILE] = (prob * (gp_ref[own, :] - delta) * inverse_root).astype(BF16)
+    mix_ref[:TILE, TILE:] = prob.astype(BF16)
+    local += jnp.dot(mix_ref[:TILE, :], right_ref[...], preferred_element_type=F32)
     for half in range(2):
-        start = pl.multiple_of(half * (positions // 2) + col_ref[0] * 64, 64)
-        sum_ref[pl.ds(start, 64), :] += local[half * 64 : half * 64 + 64]
-    out_ref[...] = sum_ref[...].astype(BF16)
+        there = pl.multiple_of(half * (positions // 2) + col_ref[0] * 64, 64)
+        out_ref[pl.ds(there, 64), :] = local[half * 64 : half * 64 + 64].astype(BF16)
 
 
 def back_rest(core, col, frames, weights, conv_rest, small, large):
@@ -264,7 +274,6 @@
             pltpu.VMEM((positions, C), BF16),
             pltpu.SemaphoreType.DMA((3,)),
             pltpu.VMEM((positions, TILE), F32),
-            pltpu.VMEM((positions, C), F32),
             pltpu.VMEM((CHUNK, 2 * TILE), BF16),
             pltpu.VMEM((2 * TILE, C), BF16),
         ],
@@ -309,10 +318,21 @@
         jnp.where(core == 0, kernel_one, kernel_two), "col", axis=3, tiled=True
     ).reshape(27, C, C)
 
-    spread = jnp.broadcast_to(latent.reshape(2, 1, 64, C), (2, cols, 64, C)).reshape(-1, 64, C)
-    frame = lax.all_to_all(spread, ("row", "col"), 0, 0, tiled=True)
-    tiles = frame.reshape(2, cols, 8, 8, C)
-    pick = lambda index: lax.dynamic_index_in_dim(tiles, index, 1, keepdims=False)
+    keep = lax.dynamic_index_in_dim(latent, row, 0, keepdims=False)
+    give = lax.dynamic_index_in_dim(latent, 1 - row, 0, keepdims=False)
+    got = lax.ppermute(give, "row", swap_row)
+    tile = jnp.concatenate([jnp.where(row == 0, keep, got), jnp.where(row == 0, got, keep)], axis=0)
+    side = 4
+    along_x = [[side * y + x for x in range(side)] for y in range(side)]
+    along_y = [[side * y + x for y in range(side)] for x in range(side)]
+
+    def shared(value, members):
+        spread = jnp.broadcast_to(value[None], (side,) + value.shape)
+        return lax.all_to_all(spread, "col", 0, 0, tiled=True, axis_index_groups=members)
+
+    frame = shared(shared(tile.reshape(TILE, C), along_x), along_y)
+    tiles = frame.reshape(cols, 2, 8, 8, C)
+    pick = lambda index: lax.dynamic_index_in_dim(tiles, index, 0, keepdims=False)
     before, own, after = (
         pick(jnp.maximum(col - 1, 0)),
         pick(col),

time: 163 us -> 158 us (0.969)
  waiting for transfers between devices: 64.5 us -> 48.1 us
  blocking collectives: 0 us -> 10 us
  starting transfers between devices: 43.3 us -> 45.1 us
    ppermute x1 -> x2, waiting for transfers between devices: 17.9 us -> 3.36 us  [shards(): got = lax.ppermute(give, 'row', swap_row)]
    all_to_all x0 -> x1, blocking collectives: none -> 10 us  [shared(): lax.all_to_all(spread, 'col', 0, 0, tiled=True, axis_index_groups=members)]
    all_gather x1, waiting for transfers between devices: 13.3 us -> 7.69 us  [shards(): lax.all_gather(jnp.where(core == 0, kernel_one, kernel_two), 'col', axis=...]
    all_to_all x1, starting transfers between devices: 9.35 us -> 4.31 us  [shared(): lax.all_to_all(spread, 'col', 0, 0, tiled=True, axis_index_groups=members)]
    ppermute x6, starting transfers between devices: 20.8 us -> 25.7 us  [moved(): return lax.ppermute(value, time_row, pairs)]
    all_to_all x1, waiting for transfers between devices: 0.01 us -> 3.55 us  [shared(): lax.all_to_all(spread, 'col', 0, 0, tiled=True, axis_index_groups=members)]
    ppermute x1 -> x2, starting transfers between devices: 1.32 us -> 4.1 us  [shards(): got = lax.ppermute(give, 'row', swap_row)]
  transfers between devices with their start and end apart: 16 -> 17, of which waited for: 9 -> 11; matrix products, arithmetic and copies ran while one was open for 11% -> 12% of each run, Pallas kernels for 6% -> 6%
where the time goes in v5:
time: 158 us
  waiting for transfers between devices  48.1 us (30%)
  starting transfers between devices  45.1 us (29%)
  Pallas kernels  17.5 us (11%)
  between operations  14 us (9%)
  other arithmetic  10.3 us (7%)
  blocking collectives  10 us (6%)
  matrix products  9 us (6%)
  local copies, waits for them, and re-layouts  3.55 us (2%)
    ppermute x6, starting transfers between devices, moved(): return lax.ppermute(value, time_row, pairs)  25.7 us
    ppermute x1, waiting for transfers between devices, shards(): come = lax.ppermute(leave, 'row', swap_row)  16.1 us
    all_to_all x1, blocking collectives, shared(): lax.all_to_all(spread, 'col', 0, 0, tiled=True, axis_index_groups=members)  10 us
    all_gather x1, waiting for transfers between devices, shards(): lax.all_gather(jnp.where(core == 0, kernel_one, kernel_two), 'col', axis=...  7.69 us
    pallas_call x1, Pallas kernels, pair_conv(): pl.pallas_call(pair_kernel, out_shape=jax.ShapeDtypeStruct((2 * SPAN, C),...  7.56 us
    pallas_call x1, Pallas kernels, back_rest(): pl.pallas_call(back_kernel, out_shape=(jax.ShapeDtypeStruct((TILE, C), BF...  7.29 us
    ppermute x6, waiting for transfers between devices, moved(): return lax.ppermute(value, time_row, pairs)  5.39 us
    all_to_all x1, starting transfers between devices, shards(): lax.all_to_all(partial.reshape(-1, 64, C), ('row', 'col'), 0, 0, tiled=True)  5.27 us
  transfers between devices with their start and end apart: 17, of which 11 were waited for; matrix products, arithmetic and copies ran while one was open for 12% of the time, Pallas kernels for 6%

profile of v5, /device:TPU:1, one launch (start us, length us, event | category | flops | bytes accessed | tf_op | source)
XLA Modules:
  0.0 157.5 jit_solution(13768087492523716079)
XLA Ops:
  6.5 2.0 %broadcast_select_fusion.1 = bf16[3,3,3,24,384]{4,3,2,1,0:T(8,128)(2,1)} fusion(bf16[3,3,3,24,384]{4,3,2,1,0:T(8,128)(2,1)} %param.20, bf16[3,3,3,24,384]{4,3,2,1,0:T(8,128)(2,1)} %param.21, pred[]{:T(512)S(6)} %eq.5), kind=kLoop, calls=%fused_computation.36 | loop fusion | flops 248832 | bytes 1492993 | tf_op jit(solution)/shard_map/jit(_where)/select_n | solution.py:318
  8.6 2.6 %collective-permute-start = (bf16[8,8,384]{2,1,0:T(8,128)(2,1)S(1)}, bf16[8,8,384]{2,1,0:T(8,128)(2,1)S(1)}, u32[]{:S(2)}, u32[]{:S(2)}) collective-permute-start(bf16[8,8,384]{2,1,0:T(8,128)(2,1)S(1)} %dynamic-slice_bitcast_fusion.5), channel_id=1, source_target_pairs={{0,16},{16,0},{1,17},{17,1},{2,18},{18,2},{3,19},{19,3},{4,20},{20... | collective-permute-start | bytes 147464 | tf_op jit(solution)/shard_map/ppermute | solution.py:323
  11.1 1.5 collective-permute-done
  12.7 10.0 %all_to_all.15 = bf16[4,128,384]{2,1,0:T(8,128)(2,1)S(1)} all-to-all(bf16[4,128,384]{2,1,0:T(8,128)(2,1)S(1)} %broadcast_in_dim.33), channel_id=1, replica_groups={{0,1,2,3},{4,5,6,7},{8,9,10,11},{12,13,14,15},{16,17,18,19},{20,21,22,2..., dimensions={0} | all-to-all | bytes 786432 | tf_op jit(solution)/shard_map/all_to_all | solution.py:331
  22.7 1.5 broadcast_in_dim.34
  24.2 4.3 %all-to-all-start.1 = ((bf16[4,4,128,384]{3,2,1,0:T(8,128)(2,1)}), bf16[4,4,128,384]{3,2,1,0:T(8,128)(2,1)S(1)}, u32[]{:S(2)}, u32[]{:S(2)}) async-start(bf16[4,4,128,384]{3,2,1,0:T(8,128)(2,1)} %broadcast_in_dim.34), calls=%async_computation.1 | async-start | bytes 3145728 | tf_op jit(solution)/shard_map/all_to_all | solution.py:331
  28.5 1.5 collective-permute-start.3
  30.1 1.9 %collective-permute-done.3 = bf16[8,8,384]{2,1,0:T(8,128)(2,1)S(1)} collective-permute-done((bf16[8,8,384]{2,1,0:T(8,128)(2,1)S(1)}, bf16[8,8,384]{2,1,0:T(8,128)(2,1)S(1)}, u32[]{:S(2)}, u32[]{:S(2)}) %collective-permute-start.3) | collective-permute-done | bytes 49184 | tf_op jit(solution)/shard_map/ppermute | solution.py:380
  32.0 0.1 fusion.46
  32.1 2.2 %collective-permute-start.4 = (bf16[16,2,384]{2,1,0:T(2,128)(2,1)S(1)}, bf16[16,2,384]{2,1,0:T(2,128)(2,1)S(1)}, u32[]{:S(2)}, u32[]{:S(2)}) collective-permute-start(bf16[16,2,384]{2,1,0:T(2,128)(2,1)S(1)} %get-tuple-element.34), channel_id=1, source_target_pairs={{0,1},{1,2},{2,3},{3,4},{4,5},{5,6},{6,7},{7,8},{8,9},{9,10},{10,1... | collective-permute-start | bytes 73736 | tf_op jit(solution)/shard_map/ppermute | solution.py:386
  34.3 1.3 collective-permute-start.5
  35.6 0.1 pad.29.clone
  35.7 3.6 %collective-permute-done.5 = bf16[16,2,384]{2,1,0:T(2,128)(2,1)S(1)} collective-permute-done((bf16[16,2,384]{2,1,0:T(2,128)(2,1)S(1)}, bf16[16,2,384]{2,1,0:T(2,128)(2,1)S(1)}, u32[]{:S(2)}, u32[]{:S(2)}) %collective-permute-start.5) | collective-permute-done | bytes 24608 | tf_op jit(solution)/shard_map/ppermute | solution.py:388
  39.3 0.8 maximum_maximum_fusion
  40.1 7.0 %collective-permute-start.7 = (bf16[256,384]{1,0:T(8,128)(2,1)}, bf16[256,384]{1,0:T(8,128)(2,1)}, u32[]{:S(2)}, u32[]{:S(2)}) collective-permute-start(bf16[256,384]{1,0:T(8,128)(2,1)} %bitcast.18), channel_id=1, source_target_pairs={{32,0},{48,16},{64,32},{80,48},{96,64},{112,80},{128,96},{144,112}... | collective-permute-start | bytes 589832 | tf_op jit(solution)/shard_map/ppermute | solution.py:315
  47.1 2.8 %collective-permute-start.6 = (bf16[256,384]{1,0:T(8,128)(2,1)}, bf16[256,384]{1,0:T(8,128)(2,1)}, u32[]{:S(2)}, u32[]{:S(2)}) collective-permute-start(bf16[256,384]{1,0:T(8,128)(2,1)} %bitcast.18), channel_id=1, source_target_pairs={{16,0},{32,16},{48,32},{64,48},{80,64},{96,80},{112,96},{128,112},... | collective-permute-start | bytes 589832 | tf_op jit(solution)/shard_map/ppermute | solution.py:315
  49.9 0.8 fusion.64
  50.7 3.5 %all-to-all-done.1 = bf16[4,4,128,384]{3,2,1,0:T(8,128)(2,1)S(1)} async-done(((bf16[4,4,128,384]{3,2,1,0:T(8,128)(2,1)}), bf16[4,4,128,384]{3,2,1,0:T(8,128)(2,1)S(1)}, u32[]{:S(2)}, u32[]{:S(2)}) %all-to-all-start.1) | async-done | bytes 1572896 | tf_op jit(solution)/shard_map/all_to_all | solution.py:331
  54.4 0.2 multiply_reduce_fusion.1
  54.6 0.1 rsqrt.56
  54.7 0.4 multiply_reduce_fusion
  55.1 0.1 maximum_convert_fusion
  55.2 0.1 fusion.36
  55.3 0.3 convolution_convert_fusion.3
  55.6 0.4 fusion.1
  56.1 1.1 convolution_convert_fusion.1.keys_from
  57.2 0.7 fusion.50
  58.0 1.4 copy-done.6
  59.3 0.4 fusion.2
  59.7 2.3 %convolution_convert_fusion.values_from = bf16[2048,384]{1,0:T(8,128)(2,1)} fusion(bf16[2048,384]{1,0:T(8,128)(2,1)S(1)} %fusion.1, bf16[384,384]{1,0:T(8,128)(2,1)S(1)} %copy-done.1), kind=kOutput, calls=%fused_computation.5 | convolution fusion | flops 604766208 | bytes 3440640 | tf_op jit(solution)/shard_map/dot_general | solution.py:350
  62.0 3.7 %fusion.10 = (f32[256]{0:T(256)S(1)}, bf16[256,384]{1,0:T(8,128)(2,1)}) fusion(f32[256,384]{1,0:T(8,128)S(1)} %bitcast.120, bf16[384,384]{1,0:T(8,128)(2,1)S(1)} %copy-done.3, bf16[2048,384]{1,0:T(8,128)(2,1)} %convolution_convert_fusion.values_from, f32[2048,256]{1,0:T(8,128)} %copy-done.6, f32[256]{0:T(256)S(1)} %fusion.2, f32[256]{0:T(256)S(1)} %get-tuple-element.40), kind=kOutput, calls=%fused_computation.39 | convolution fusion | flops 480313088 | bytes 4557824 | tf_op jit(solution)/shard_map/dot_general | solution.py:359
  65.8 1.2 fusion.18
  67.0 3.0 %collective-permute-start.2 = (bf16[256,384]{1,0:T(8,128)(2,1)S(1)}, bf16[256,384]{1,0:T(8,128)(2,1)S(1)}, u32[]{:S(2)}, u32[]{:S(2)}) collective-permute-start(bf16[256,384]{1,0:T(8,128)(2,1)S(1)} %fusion.18), channel_id=1, source_target_pairs={{0,16},{16,32},{32,48},{48,64},{64,80},{80,96},{96,112},{112,128},... | collective-permute-start | bytes 589832 | tf_op jit(solution)/shard_map/ppermute | solution.py:315
  70.0 7.3 %collective-permute-start.1 = (bf16[256,384]{1,0:T(8,128)(2,1)S(1)}, bf16[256,384]{1,0:T(8,128)(2,1)S(1)}, u32[]{:S(2)}, u32[]{:S(2)}) collective-permute-start(bf16[256,384]{1,0:T(8,128)(2,1)S(1)} %fusion.18), channel_id=1, source_target_pairs={{0,32},{16,48},{32,64},{48,80},{64,96},{80,112},{96,128},{112,144}... | collective-permute-start | bytes 589832 | tf_op jit(solution)/shard_map/ppermute | solution.py:315
  77.3 0.6 fusion.51
  77.9 2.0 %collective-permute-done.1 = bf16[256,384]{1,0:T(8,128)(2,1)S(1)} collective-permute-done((bf16[256,384]{1,0:T(8,128)(2,1)S(1)}, bf16[256,384]{1,0:T(8,128)(2,1)S(1)}, u32[]{:S(2)}, u32[]{:S(2)}) %collective-permute-start.1) | collective-permute-done | bytes 196640 | tf_op jit(solution)/shard_map/ppermute | solution.py:315
  79.9 1.2 select_bitcast_fusion
  81.2 0.1 collective-permute-start.8
  81.3 0.2 convolution_convert_fusion.4.qk_ref
  81.5 0.3 fusion.8
  81.8 0.1 fusion.7.prob_from
  82.0 1.4 collective-permute-done.8
  83.4 0.2 pad_maximum_fusion
  83.5 0.1 copy.13
  83.7 7.7 %all-gather.2.cloned.1.call-done = bf16[3,3,3,384,384]{4,3,2,1,0:T(8,128)(2,1)} async-done(((bf16[3,3,3,24,384]{4,3,2,1,0:T(8,128)(2,1)}), bf16[3,3,3,384,384]{4,3,2,1,0:T(8,128)(2,1)}) %all-gather.2.cloned.1.call-update) | async-done | bytes 7962640 | tf_op jit(solution)/shard_map/all_gather | solution.py:317
  91.4 0.7 collective-permute-start.12
  92.0 7.6 %pair_conv.1 = f32[512,384]{1,0:T(8,128)S(1)} custom-call(s32[1]{0:T(128)} %bitcast.core_ref, bf16[3,576,384]{2,1,0:T(8,128)(2,1)S(1)} %bitcast.107, bf16[27,384,384]{2,1,0:T(8,128)(2,1)} %bitcast.113), custom_call_target="tpu_custom_call" | custom-call | flops 4076863488 | bytes 7962624 | tf_op jit(solution)/shard_map/pair_conv/pallas_call | solution.py:103
  99.7 0.1 collective-permute-start.9
  99.8 4.7 %collective-permute-done.9 = bf16[256,384]{1,0:T(8,128)(2,1)S(1)} collective-permute-done((bf16[256,384]{1,0:T(8,128)(2,1)S(1)}, bf16[256,384]{1,0:T(8,128)(2,1)S(1)}, u32[]{:S(2)}, u32[]{:S(2)}) %collective-permute-start.9) | collective-permute-done | bytes 196640 | tf_op jit(solution)/shard_map/ppermute | solution.py:402
  104.5 0.1 fusion.19
  104.7 0.4 fusion.34
  105.1 0.2 fusion.33
  105.4 3.4 %collective-permute-start.11 = (bf16[160,384]{1,0:T(8,128)(2,1)S(1)}, bf16[160,384]{1,0:T(8,128)(2,1)S(1)}, u32[]{:S(2)}, u32[]{:S(2)}) collective-permute-start(bf16[160,384]{1,0:T(8,128)(2,1)S(1)} %reshape.180.frame_ref), channel_id=1, source_target_pairs={{16,0},{32,16},{48,32},{64,48},{80,64},{96,80},{112,96},{128,112},... | collective-permute-start | bytes 368648 | tf_op jit(solution)/shard_map/ppermute | solution.py:315
  108.9 2.1 %collective-permute-start.10 = (bf16[160,384]{1,0:T(8,128)(2,1)S(1)}, bf16[160,384]{1,0:T(8,128)(2,1)S(1)}, u32[]{:S(2)}, u32[]{:S(2)}) collective-permute-start(bf16[160,384]{1,0:T(8,128)(2,1)S(1)} %reshape.180.frame_ref), channel_id=1, source_target_pairs={{32,0},{48,16},{64,32},{80,48},{96,64},{112,80},{128,96},{144,112}... | collective-permute-start | bytes 368648 | tf_op jit(solution)/shard_map/ppermute | solution.py:315
  111.1 2.6 %back_own.1.start_ref = f32[128,384]{1,0:T(8,128)S(1)} custom-call(s32[1]{0:T(128)} %bitcast.core_ref, bf16[160,384]{1,0:T(8,128)(2,1)S(1)} %reshape.180.frame_ref, bf16[27,384,384]{2,1,0:T(8,128)(2,1)} %bitcast.114, bf16[27,384,384]{2,1,0:T(8,128)(2,1)} %collective-permute-done.12.other_ref), custom_call_target="tpu_custom_call" | custom-call | flops 339738624 | bytes 2654208 | tf_op jit(solution)/shard_map/back_own/pallas_call | solution.py:170
  113.7 3.4 %collective-permute-done.10.late_ref = bf16[160,384]{1,0:T(8,128)(2,1)S(1)} collective-permute-done((bf16[160,384]{1,0:T(8,128)(2,1)S(1)}, bf16[160,384]{1,0:T(8,128)(2,1)S(1)}, u32[]{:S(2)}, u32[]{:S(2)}) %collective-permute-start.10) | collective-permute-done | bytes 122912 | tf_op jit(solution)/shard_map/ppermute | solution.py:315
  117.1 7.3 %back_rest.1 = (bf16[128,384]{1,0:T(8,128)(2,1)S(1)}, bf16[2048,384]{1,0:T(8,128)(2,1)}) custom-call(s32[1]{0:T(128)} %bitcast.core_ref, s32[1]{0:T(128)} %bitcast.1.col_ref, bf16[160,384]{1,0:T(8,128)(2,1)S(1)} %collective-permute-done.10.late_ref, bf16[160,384]{1,0:T(8,128)(2,1)S(1)} %collective-permute-done.11.soon_ref, bf16[27,384,384]{2,1,0:T(8,128)(2,1)} %bitcast.115, ...), custom_call_target="tpu_custom_call" | custom-call | flops 1686110208 | bytes 11599872 | tf_op jit(solution)/shard_map/back_rest/pallas_call | solution.py:262
  124.4 5.3 %all-to-all-start.2 = ((bf16[32,64,384]{2,1,0:T(8,128)(2,1)}), bf16[32,64,384]{2,1,0:T(8,128)(2,1)S(1)}, u32[]{:S(2)}, u32[]{:S(2)}) async-start(bf16[32,64,384]{2,1,0:T(8,128)(2,1)} %bitcast.119), calls=%async_computation.2 | async-start | bytes 3145728 | tf_op jit(solution)/shard_map/all_to_all | solution.py:427
  129.7 1.3 collective-permute-start.13
  131.0 16.1 %collective-permute-done.13 = bf16[8,8,384]{2,1,0:T(8,128)(2,1)S(1)} collective-permute-done((bf16[8,8,384]{2,1,0:T(8,128)(2,1)S(1)}, bf16[8,8,384]{2,1,0:T(8,128)(2,1)S(1)}, u32[]{:S(2)}, u32[]{:S(2)}) %collective-permute-start.13) | collective-permute-done | bytes 49184 | tf_op jit(solution)/shard_map/ppermute | solution.py:425
  147.2 2.3 %all-to-all-done.2 = bf16[32,64,384]{2,1,0:T(8,128)(2,1)S(1)} async-done(((bf16[32,64,384]{2,1,0:T(8,128)(2,1)}), bf16[32,64,384]{2,1,0:T(8,128)(2,1)S(1)}, u32[]{:S(2)}, u32[]{:S(2)}) %all-to-all-start.2) | async-done | bytes 1572896 | tf_op jit(solution)/shard_map/all_to_all | solution.py:427
  149.5 0.2 convert_reduce_fusion
  149.7 0.1 fusion.37
  149.9 0.8 fusion.40
  (64 shorter events, 0.6 us)
Async XLA Ops:
  6.5 49.5 %copy-start = (bf16[384,384]{1,0:T(8,128)(2,1)S(1)}, bf16[384,384]{1,0:T(8,128)(2,1)}, u32[]{:S(2)}) copy-start(bf16[384,384]{1,0:T(8,128)(2,1)} %param.15) | copy-start | bytes 884740
  6.5 2.0 %copy-start.7 = (bf16[2,8,8,384]{3,2,1,0:T(8,128)(2,1)S(1)}, bf16[2,8,8,384]{3,2,1,0:T(8,128)(2,1)}, u32[]{:S(2)}) copy-start(bf16[2,8,8,384]{3,2,1,0:T(8,128)(2,1)} %param.11) | copy-start | bytes 294916
  6.5 84.8 %all-gather.2.cloned.1.call-start = ((), (), s32[]{:S(2)}) async-start(), calls=%async_computation.3 | async-start | bytes 8460288 | tf_op jit(solution)/shard_map/all_gather | solution.py:317
  8.6 4.0 %collective-permute-start = (bf16[8,8,384]{2,1,0:T(8,128)(2,1)S(1)}, bf16[8,8,384]{2,1,0:T(8,128)(2,1)S(1)}, u32[]{:S(2)}, u32[]{:S(2)}) collective-permute-start(bf16[8,8,384]{2,1,0:T(8,128)(2,1)S(1)} %dynamic-slice_bitcast_fusion.5), channel_id=1, source_target_pairs={{0,16},{16,0},{1,17},{17,1},{2,18},{18,2},{3,19},{19,3},{4,20},{20... | collective-permute-start | bytes 147464 | tf_op jit(solution)/shard_map/ppermute | solution.py:323
  24.2 4.3 %copy-start.11 = (bf16[2,8,8,384]{3,2,1,0:T(8,128)(2,1)S(1)}, bf16[2,8,8,384]{3,2,1,0:T(8,128)(2,1)}, u32[]{:S(2)}) copy-start(bf16[2,8,8,384]{3,2,1,0:T(8,128)(2,1)} %param.12) | copy-start | bytes 294916
  24.2 30.0 %all-to-all-start.1 = ((bf16[4,4,128,384]{3,2,1,0:T(8,128)(2,1)}), bf16[4,4,128,384]{3,2,1,0:T(8,128)(2,1)S(1)}, u32[]{:S(2)}, u32[]{:S(2)}) async-start(bf16[4,4,128,384]{3,2,1,0:T(8,128)(2,1)} %broadcast_in_dim.34), calls=%async_computation.1 | async-start | bytes 3145728 | tf_op jit(solution)/shard_map/all_to_all | solution.py:331
  28.5 3.4 %collective-permute-start.3 = (bf16[8,8,384]{2,1,0:T(8,128)(2,1)S(1)}, bf16[8,8,384]{2,1,0:T(8,128)(2,1)S(1)}, u32[]{:S(2)}, u32[]{:S(2)}) collective-permute-start(bf16[8,8,384]{2,1,0:T(8,128)(2,1)S(1)} %dynamic-slice_bitcast_fusion.4), channel_id=1, source_target_pairs={{0,16},{16,0},{1,17},{17,1},{2,18},{18,2},{3,19},{19,3},{4,20},{20... | collective-permute-start | bytes 147464 | tf_op jit(solution)/shard_map/ppermute | solution.py:380
  32.1 3.6 %collective-permute-start.4 = (bf16[16,2,384]{2,1,0:T(2,128)(2,1)S(1)}, bf16[16,2,384]{2,1,0:T(2,128)(2,1)S(1)}, u32[]{:S(2)}, u32[]{:S(2)}) collective-permute-start(bf16[16,2,384]{2,1,0:T(2,128)(2,1)S(1)} %get-tuple-element.34), channel_id=1, source_target_pairs={{0,1},{1,2},{2,3},{3,4},{4,5},{5,6},{6,7},{7,8},{8,9},{9,10},{10,1... | collective-permute-start | bytes 73736 | tf_op jit(solution)/shard_map/ppermute | solution.py:386
  34.3 5.0 %collective-permute-start.5 = (bf16[16,2,384]{2,1,0:T(2,128)(2,1)S(1)}, bf16[16,2,384]{2,1,0:T(2,128)(2,1)S(1)}, u32[]{:S(2)}, u32[]{:S(2)}) collective-permute-start(bf16[16,2,384]{2,1,0:T(2,128)(2,1)S(1)} %get-tuple-element.35), channel_id=1, source_target_pairs={{1,0},{2,1},{3,2},{4,3},{5,4},{6,5},{7,6},{8,7},{9,8},{10,9},{11,1... | collective-permute-start | bytes 73736 | tf_op jit(solution)/shard_map/ppermute | solution.py:388
  40.1 37.8 %collective-permute-start.7 = (bf16[256,384]{1,0:T(8,128)(2,1)}, bf16[256,384]{1,0:T(8,128)(2,1)}, u32[]{:S(2)}, u32[]{:S(2)}) collective-permute-start(bf16[256,384]{1,0:T(8,128)(2,1)} %bitcast.18), channel_id=1, source_target_pairs={{32,0},{48,16},{64,32},{80,48},{96,64},{112,80},{128,96},{144,112}... | collective-permute-start | bytes 589832 | tf_op jit(solution)/shard_map/ppermute | solution.py:315
  47.1 30.8 %collective-permute-start.6 = (bf16[256,384]{1,0:T(8,128)(2,1)}, bf16[256,384]{1,0:T(8,128)(2,1)}, u32[]{:S(2)}, u32[]{:S(2)}) collective-permute-start(bf16[256,384]{1,0:T(8,128)(2,1)} %bitcast.18), channel_id=1, source_target_pairs={{16,0},{32,16},{48,32},{64,48},{80,64},{96,80},{112,96},{128,112},... | collective-permute-start | bytes 589832 | tf_op jit(solution)/shard_map/ppermute | solution.py:315
  50.7 4.5 %copy-start.12 = (f32[384]{0:T(512)S(1)}, f32[384]{0:T(512)}, u32[]{:S(2)}) copy-start(f32[384]{0:T(512)} %param.13) | copy-start | bytes 4612
  54.3 1.0 copy-start.2
  57.2 20.1 %copy-start.5 = (bf16[2048,384]{1,0:T(8,128)(2,1)}, bf16[2048,384]{1,0:T(8,128)(2,1)S(1)}, u32[]{:S(2)}) copy-start(bf16[2048,384]{1,0:T(8,128)(2,1)S(1)} %convolution_convert_fusion.1.keys_from) | copy-start | bytes 4718596
  57.9 1.4 copy-start.6
  58.0 1.7 %copy-start.1 = (bf16[384,384]{1,0:T(8,128)(2,1)S(1)}, bf16[384,384]{1,0:T(8,128)(2,1)}, u32[]{:S(2)}) copy-start(bf16[384,384]{1,0:T(8,128)(2,1)} %w_value_ref.1) | copy-start | bytes 884740
  59.7 2.3 %copy-start.3 = (bf16[384,384]{1,0:T(8,128)(2,1)S(1)}, bf16[384,384]{1,0:T(8,128)(2,1)}, u32[]{:S(2)}) copy-start(bf16[384,384]{1,0:T(8,128)(2,1)} %w_out_ref.1) | copy-start | bytes 884740
  62.0 3.8 %copy-start.13 = (f32[384]{0:T(512)S(1)}, f32[384]{0:T(512)}, u32[]{:S(2)}) copy-start(f32[384]{0:T(512)} %param.18) | copy-start | bytes 4612
  65.8 14.2 %copy-start.9 = (bf16[1,16,16,384]{3,2,1,0:T(8,128)(2,1)S(1)}, bf16[1,16,16,384]{3,2,1,0:T(8,128)(2,1)}, u32[]{:S(2)}) copy-start(bf16[1,16,16,384]{3,2,1,0:T(8,128)(2,1)} %fusion.64) | copy-start | bytes 589828
  67.0 10.9 %collective-permute-start.2 = (bf16[256,384]{1,0:T(8,128)(2,1)S(1)}, bf16[256,384]{1,0:T(8,128)(2,1)S(1)}, u32[]{:S(2)}, u32[]{:S(2)}) collective-permute-start(bf16[256,384]{1,0:T(8,128)(2,1)S(1)} %fusion.18), channel_id=1, source_target_pairs={{0,16},{16,32},{32,48},{48,64},{64,80},{80,96},{96,112},{112,128},... | collective-permute-start | bytes 589832 | tf_op jit(solution)/shard_map/ppermute | solution.py:315
  70.0 9.9 %collective-permute-start.1 = (bf16[256,384]{1,0:T(8,128)(2,1)S(1)}, bf16[256,384]{1,0:T(8,128)(2,1)S(1)}, u32[]{:S(2)}, u32[]{:S(2)}) collective-permute-start(bf16[256,384]{1,0:T(8,128)(2,1)S(1)} %fusion.18), channel_id=1, source_target_pairs={{0,32},{16,48},{32,64},{48,80},{64,96},{80,112},{96,128},{112,144}... | collective-permute-start | bytes 589832 | tf_op jit(solution)/shard_map/ppermute | solution.py:315
  81.2 2.2 %collective-permute-start.8 = (bf16[3,18,16,384]{3,2,1,0:T(8,128)(2,1)S(1)}, bf16[3,18,16,384]{3,2,1,0:T(8,128)(2,1)S(1)}, u32[]{:S(2)}, u32[]{:S(2)}) collective-permute-start(bf16[3,18,16,384]{3,2,1,0:T(8,128)(2,1)S(1)} %get-tuple-element.27), channel_id=1, source_target_pairs={{0,32},{32,0},{64,96},{96,64},{128,160},{160,128},{192,224},{224,1... | collective-permute-start | bytes 1990664 | tf_op jit(solution)/shard_map/ppermute | solution.py:396
  91.4 19.7 %collective-permute-start.12 = (bf16[27,384,384]{2,1,0:T(8,128)(2,1)}, bf16[27,384,384]{2,1,0:T(8,128)(2,1)}, u32[]{:S(2)}, u32[]{:S(2)}) collective-permute-start(bf16[27,384,384]{2,1,0:T(8,128)(2,1)} %bitcast.112), channel_id=1, source_target_pairs={{0,32},{32,0},{64,96},{96,64},{128,160},{160,128},{192,224},{224,1... | collective-permute-start | bytes 23887880 | tf_op jit(solution)/shard_map/ppermute | solution.py:399
  99.6 5.0 %copy-start.14 = (f32[384]{0:T(512)S(1)}, f32[384]{0:T(512)}, u32[]{:S(2)}) copy-start(f32[384]{0:T(512)} %param.19) | copy-start | bytes 4612
  99.7 4.8 %collective-permute-start.9 = (bf16[256,384]{1,0:T(8,128)(2,1)S(1)}, bf16[256,384]{1,0:T(8,128)(2,1)S(1)}, u32[]{:S(2)}, u32[]{:S(2)}) collective-permute-start(bf16[256,384]{1,0:T(8,128)(2,1)S(1)} %bitcast.125), channel_id=1, source_target_pairs={{0,32},{32,0},{64,96},{96,64},{128,160},{160,128},{192,224},{224,1... | collective-permute-start | bytes 589832 | tf_op jit(solution)/shard_map/ppermute | solution.py:402
  99.8 11.2 %copy-start.10 = (bf16[256,384]{1,0:T(8,128)(2,1)S(1)}, bf16[256,384]{1,0:T(8,128)(2,1)}, u32[]{:S(2)}) copy-start(bf16[256,384]{1,0:T(8,128)(2,1)} %get-tuple-element.43) | copy-start | bytes 589828
  105.4 8.3 %collective-permute-start.11 = (bf16[160,384]{1,0:T(8,128)(2,1)S(1)}, bf16[160,384]{1,0:T(8,128)(2,1)S(1)}, u32[]{:S(2)}, u32[]{:S(2)}) collective-permute-start(bf16[160,384]{1,0:T(8,128)(2,1)S(1)} %reshape.180.frame_ref), channel_id=1, source_target_pairs={{16,0},{32,16},{48,32},{64,48},{80,64},{96,80},{112,96},{128,112},... | collective-permute-start | bytes 368648 | tf_op jit(solution)/shard_map/ppermute | solution.py:315
  108.9 8.2 %collective-permute-start.10 = (bf16[160,384]{1,0:T(8,128)(2,1)S(1)}, bf16[160,384]{1,0:T(8,128)(2,1)S(1)}, u32[]{:S(2)}, u32[]{:S(2)}) collective-permute-start(bf16[160,384]{1,0:T(8,128)(2,1)S(1)} %reshape.180.frame_ref), channel_id=1, source_target_pairs={{32,0},{48,16},{64,32},{80,48},{96,64},{112,80},{128,96},{144,112}... | collective-permute-start | bytes 368648 | tf_op jit(solution)/shard_map/ppermute | solution.py:315
  111.1 6.0 %copy-start.4 = (bf16[384,384]{1,0:T(8,128)(2,1)S(1)}, bf16[384,384]{1,0:T(8,128)(2,1)}, u32[]{:S(2)}) copy-start(bf16[384,384]{1,0:T(8,128)(2,1)} %w_out_ref.1) | copy-start | bytes 884740
  124.4 25.1 %all-to-all-start.2 = ((bf16[32,64,384]{2,1,0:T(8,128)(2,1)}), bf16[32,64,384]{2,1,0:T(8,128)(2,1)S(1)}, u32[]{:S(2)}, u32[]{:S(2)}) async-start(bf16[32,64,384]{2,1,0:T(8,128)(2,1)} %bitcast.119), calls=%async_computation.2 | async-start | bytes 3145728 | tf_op jit(solution)/shard_map/all_to_all | solution.py:427
  129.7 20.1 %copy-start.8 = (bf16[2,8,8,384]{3,2,1,0:T(8,128)(2,1)S(1)}, bf16[2,8,8,384]{3,2,1,0:T(8,128)(2,1)}, u32[]{:S(2)}) copy-start(bf16[2,8,8,384]{3,2,1,0:T(8,128)(2,1)} %param.11) | copy-start | bytes 294916
  129.7 17.5 %collective-permute-start.13 = (bf16[8,8,384]{2,1,0:T(8,128)(2,1)S(1)}, bf16[8,8,384]{2,1,0:T(8,128)(2,1)S(1)}, u32[]{:S(2)}, u32[]{:S(2)}) collective-permute-start(bf16[8,8,384]{2,1,0:T(8,128)(2,1)S(1)} %dynamic-slice_bitcast_fusion.3), channel_id=1, source_target_pairs={{0,16},{16,0},{1,17},{17,1},{2,18},{18,2},{3,19},{19,3},{4,20},{20... | collective-permute-start | bytes 147464 | tf_op jit(solution)/shard_map/ppermute | solution.py:425
Sparse Core Ops, SparseCore 0:
  9.8 81.4 all-gather.1

commit v6 on v5

--- a/solution.py
+++ b/solution.py
@@ -218,14 +218,15 @@
     right_ref[TILE:, :] = lax.dot_general(
         g_context, w_value_ref[...], NT, preferred_element_type=F32
     ).astype(BF16)
-    for copy in inputs:
-        copy.wait()
+    inputs[0].wait()
+    inputs[1].wait()
     delta = jnp.zeros((1, TILE), F32)
     for c in range(count):
         part = pl.ds(c * CHUNK, CHUNK)
         g_prob = lax.dot_general(values_ref[part, :], g_context, NT, preferred_element_type=F32)
         gp_ref[part, :] = g_prob
         delta = delta + jnp.sum(prob_ref[part, :] * g_prob, axis=0, keepdims=True)
+    inputs[2].wait()
     g_query = jnp.zeros((TILE, C), F32)
     for c in range(count):
         part = pl.ds(c * CHUNK, CHUNK)

time: 158 us -> 158 us (level)
  no operation moved by 1% of the time
where the time goes in v6:
time: 158 us
  waiting for transfers between devices  48.1 us (30%)
  starting transfers between devices  45.1 us (29%)
  Pallas kernels  17.4 us (11%)
  between operations  14 us (9%)
  other arithmetic  10.3 us (7%)
  blocking collectives  10 us (6%)
  matrix products  9 us (6%)
  local copies, waits for them, and re-layouts  3.55 us (2%)
    ppermute x6, starting transfers between devices, moved(): return lax.ppermute(value, time_row, pairs)  25.7 us
    ppermute x1, waiting for transfers between devices, shards(): come = lax.ppermute(leave, 'row', swap_row)  16.1 us
    all_to_all x1, blocking collectives, shared(): lax.all_to_all(spread, 'col', 0, 0, tiled=True, axis_index_groups=members)  10 us
    all_gather x1, waiting for transfers between devices, shards(): lax.all_gather(jnp.where(core == 0, kernel_one, kernel_two), 'col', axis=...  7.69 us
    pallas_call x1, Pallas kernels, pair_conv(): pl.pallas_call(pair_kernel, out_shape=jax.ShapeDtypeStruct((2 * SPAN, C),...  7.56 us
    pallas_call x1, Pallas kernels, back_rest(): pl.pallas_call(back_kernel, out_shape=(jax.ShapeDtypeStruct((TILE, C), BF...  7.26 us
    ppermute x6, waiting for transfers between devices, moved(): return lax.ppermute(value, time_row, pairs)  5.39 us
    all_to_all x1, starting transfers between devices, shards(): lax.all_to_all(partial.reshape(-1, 64, C), ('row', 'col'), 0, 0, tiled=True)  5.28 us
  transfers between devices with their start and end apart: 17, of which 11 were waited for; matrix products, arithmetic and copies ran while one was open for 12% of the time, Pallas kernels for 6%

profile of v6, /device:TPU:1, one launch (start us, length us, event | category | flops | bytes accessed | tf_op | source)
XLA Modules:
  0.0 157.5 jit_solution(4269693186225033703)
XLA Ops:
  6.5 2.0 %broadcast_select_fusion.1 = bf16[3,3,3,24,384]{4,3,2,1,0:T(8,128)(2,1)} fusion(bf16[3,3,3,24,384]{4,3,2,1,0:T(8,128)(2,1)} %param.20, bf16[3,3,3,24,384]{4,3,2,1,0:T(8,128)(2,1)} %param.21, pred[]{:T(512)S(6)} %eq.5), kind=kLoop, calls=%fused_computation.36 | loop fusion | flops 248832 | bytes 1492993 | tf_op jit(solution)/shard_map/jit(_where)/select_n | solution.py:319
  8.6 2.6 %collective-permute-start = (bf16[8,8,384]{2,1,0:T(8,128)(2,1)S(1)}, bf16[8,8,384]{2,1,0:T(8,128)(2,1)S(1)}, u32[]{:S(2)}, u32[]{:S(2)}) collective-permute-start(bf16[8,8,384]{2,1,0:T(8,128)(2,1)S(1)} %dynamic-slice_bitcast_fusion.5), channel_id=1, source_target_pairs={{0,16},{16,0},{1,17},{17,1},{2,18},{18,2},{3,19},{19,3},{4,20},{20... | collective-permute-start | bytes 147464 | tf_op jit(solution)/shard_map/ppermute | solution.py:324
  11.1 1.5 collective-permute-done
  12.7 10.0 %all_to_all.15 = bf16[4,128,384]{2,1,0:T(8,128)(2,1)S(1)} all-to-all(bf16[4,128,384]{2,1,0:T(8,128)(2,1)S(1)} %broadcast_in_dim.33), channel_id=1, replica_groups={{0,1,2,3},{4,5,6,7},{8,9,10,11},{12,13,14,15},{16,17,18,19},{20,21,22,2..., dimensions={0} | all-to-all | bytes 786432 | tf_op jit(solution)/shard_map/all_to_all | solution.py:332
  22.7 1.5 broadcast_in_dim.34
  24.2 4.3 %all-to-all-start.1 = ((bf16[4,4,128,384]{3,2,1,0:T(8,128)(2,1)}), bf16[4,4,128,384]{3,2,1,0:T(8,128)(2,1)S(1)}, u32[]{:S(2)}, u32[]{:S(2)}) async-start(bf16[4,4,128,384]{3,2,1,0:T(8,128)(2,1)} %broadcast_in_dim.34), calls=%async_computation.1 | async-start | bytes 3145728 | tf_op jit(solution)/shard_map/all_to_all | solution.py:332
  28.5 1.5 collective-permute-start.3
  30.1 1.9 %collective-permute-done.3 = bf16[8,8,384]{2,1,0:T(8,128)(2,1)S(1)} collective-permute-done((bf16[8,8,384]{2,1,0:T(8,128)(2,1)S(1)}, bf16[8,8,384]{2,1,0:T(8,128)(2,1)S(1)}, u32[]{:S(2)}, u32[]{:S(2)}) %collective-permute-start.3) | collective-permute-done | bytes 49184 | tf_op jit(solution)/shard_map/ppermute | solution.py:381
  32.0 0.1 fusion.46
  32.1 2.2 %collective-permute-start.4 = (bf16[16,2,384]{2,1,0:T(2,128)(2,1)S(1)}, bf16[16,2,384]{2,1,0:T(2,128)(2,1)S(1)}, u32[]{:S(2)}, u32[]{:S(2)}) collective-permute-start(bf16[16,2,384]{2,1,0:T(2,128)(2,1)S(1)} %get-tuple-element.34), channel_id=1, source_target_pairs={{0,1},{1,2},{2,3},{3,4},{4,5},{5,6},{6,7},{7,8},{8,9},{9,10},{10,1... | collective-permute-start | bytes 73736 | tf_op jit(solution)/shard_map/ppermute | solution.py:387
  34.3 1.3 collective-permute-start.5
  35.6 0.1 pad.29.clone
  35.7 3.6 %collective-permute-done.5 = bf16[16,2,384]{2,1,0:T(2,128)(2,1)S(1)} collective-permute-done((bf16[16,2,384]{2,1,0:T(2,128)(2,1)S(1)}, bf16[16,2,384]{2,1,0:T(2,128)(2,1)S(1)}, u32[]{:S(2)}, u32[]{:S(2)}) %collective-permute-start.5) | collective-permute-done | bytes 24608 | tf_op jit(solution)/shard_map/ppermute | solution.py:389
  39.3 0.8 maximum_maximum_fusion
  40.1 7.0 %collective-permute-start.7 = (bf16[256,384]{1,0:T(8,128)(2,1)}, bf16[256,384]{1,0:T(8,128)(2,1)}, u32[]{:S(2)}, u32[]{:S(2)}) collective-permute-start(bf16[256,384]{1,0:T(8,128)(2,1)} %bitcast.18), channel_id=1, source_target_pairs={{32,0},{48,16},{64,32},{80,48},{96,64},{112,80},{128,96},{144,112}... | collective-permute-start | bytes 589832 | tf_op jit(solution)/shard_map/ppermute | solution.py:316
  47.1 2.8 %collective-permute-start.6 = (bf16[256,384]{1,0:T(8,128)(2,1)}, bf16[256,384]{1,0:T(8,128)(2,1)}, u32[]{:S(2)}, u32[]{:S(2)}) collective-permute-start(bf16[256,384]{1,0:T(8,128)(2,1)} %bitcast.18), channel_id=1, source_target_pairs={{16,0},{32,16},{48,32},{64,48},{80,64},{96,80},{112,96},{128,112},... | collective-permute-start | bytes 589832 | tf_op jit(solution)/shard_map/ppermute | solution.py:316
  49.9 0.8 fusion.64
  50.7 3.5 %all-to-all-done.1 = bf16[4,4,128,384]{3,2,1,0:T(8,128)(2,1)S(1)} async-done(((bf16[4,4,128,384]{3,2,1,0:T(8,128)(2,1)}), bf16[4,4,128,384]{3,2,1,0:T(8,128)(2,1)S(1)}, u32[]{:S(2)}, u32[]{:S(2)}) %all-to-all-start.1) | async-done | bytes 1572896 | tf_op jit(solution)/shard_map/all_to_all | solution.py:332
  54.4 0.2 multiply_reduce_fusion.1
  54.6 0.1 rsqrt.56
  54.7 0.4 multiply_reduce_fusion
  55.1 0.1 maximum_convert_fusion
  55.2 0.1 fusion.36
  55.3 0.3 convolution_convert_fusion.3
  55.6 0.4 fusion.1
  56.1 1.1 convolution_convert_fusion.1.keys_from
  57.2 0.7 fusion.50
  58.0 1.4 copy-done.6
  59.3 0.4 fusion.2
  59.7 2.3 %convolution_convert_fusion.values_from = bf16[2048,384]{1,0:T(8,128)(2,1)} fusion(bf16[2048,384]{1,0:T(8,128)(2,1)S(1)} %fusion.1, bf16[384,384]{1,0:T(8,128)(2,1)S(1)} %copy-done.1), kind=kOutput, calls=%fused_computation.5 | convolution fusion | flops 604766208 | bytes 3440640 | tf_op jit(solution)/shard_map/dot_general | solution.py:351
  62.0 3.7 %fusion.10 = (f32[256]{0:T(256)S(1)}, bf16[256,384]{1,0:T(8,128)(2,1)}) fusion(f32[256,384]{1,0:T(8,128)S(1)} %bitcast.120, bf16[384,384]{1,0:T(8,128)(2,1)S(1)} %copy-done.3, bf16[2048,384]{1,0:T(8,128)(2,1)} %convolution_convert_fusion.values_from, f32[2048,256]{1,0:T(8,128)} %copy-done.6, f32[256]{0:T(256)S(1)} %fusion.2, f32[256]{0:T(256)S(1)} %get-tuple-element.40), kind=kOutput, calls=%fused_computation.39 | convolution fusion | flops 480313088 | bytes 4557824 | tf_op jit(solution)/shard_map/dot_general | solution.py:360
  65.8 1.2 fusion.18
  67.0 3.0 %collective-permute-start.2 = (bf16[256,384]{1,0:T(8,128)(2,1)S(1)}, bf16[256,384]{1,0:T(8,128)(2,1)S(1)}, u32[]{:S(2)}, u32[]{:S(2)}) collective-permute-start(bf16[256,384]{1,0:T(8,128)(2,1)S(1)} %fusion.18), channel_id=1, source_target_pairs={{0,16},{16,32},{32,48},{48,64},{64,80},{80,96},{96,112},{112,128},... | collective-permute-start | bytes 589832 | tf_op jit(solution)/shard_map/ppermute | solution.py:316
  70.0 7.3 %collective-permute-start.1 = (bf16[256,384]{1,0:T(8,128)(2,1)S(1)}, bf16[256,384]{1,0:T(8,128)(2,1)S(1)}, u32[]{:S(2)}, u32[]{:S(2)}) collective-permute-start(bf16[256,384]{1,0:T(8,128)(2,1)S(1)} %fusion.18), channel_id=1, source_target_pairs={{0,32},{16,48},{32,64},{48,80},{64,96},{80,112},{96,128},{112,144}... | collective-permute-start | bytes 589832 | tf_op jit(solution)/shard_map/ppermute | solution.py:316
  77.3 0.6 fusion.51
  77.9 2.0 %collective-permute-done.1 = bf16[256,384]{1,0:T(8,128)(2,1)S(1)} collective-permute-done((bf16[256,384]{1,0:T(8,128)(2,1)S(1)}, bf16[256,384]{1,0:T(8,128)(2,1)S(1)}, u32[]{:S(2)}, u32[]{:S(2)}) %collective-permute-start.1) | collective-permute-done | bytes 196640 | tf_op jit(solution)/shard_map/ppermute | solution.py:316
  79.9 1.2 select_bitcast_fusion
  81.2 0.1 collective-permute-start.8
  81.3 0.2 convolution_convert_fusion.4.qk_ref
  81.5 0.3 fusion.8
  81.8 0.1 fusion.7.prob_from
  82.0 1.4 collective-permute-done.8
  83.4 0.2 pad_maximum_fusion
  83.5 0.1 copy.13
  83.7 7.7 %all-gather.2.cloned.1.call-done = bf16[3,3,3,384,384]{4,3,2,1,0:T(8,128)(2,1)} async-done(((bf16[3,3,3,24,384]{4,3,2,1,0:T(8,128)(2,1)}), bf16[3,3,3,384,384]{4,3,2,1,0:T(8,128)(2,1)}) %all-gather.2.cloned.1.call-update) | async-done | bytes 7962640 | tf_op jit(solution)/shard_map/all_gather | solution.py:318
  91.4 0.7 collective-permute-start.12
  92.0 7.6 %pair_conv.1 = f32[512,384]{1,0:T(8,128)S(1)} custom-call(s32[1]{0:T(128)} %bitcast.core_ref, bf16[3,576,384]{2,1,0:T(8,128)(2,1)S(1)} %bitcast.107, bf16[27,384,384]{2,1,0:T(8,128)(2,1)} %bitcast.113), custom_call_target="tpu_custom_call" | custom-call | flops 4076863488 | bytes 7962624 | tf_op jit(solution)/shard_map/pair_conv/pallas_call | solution.py:103
  99.7 0.1 collective-permute-start.9
  99.8 4.7 %collective-permute-done.9 = bf16[256,384]{1,0:T(8,128)(2,1)S(1)} collective-permute-done((bf16[256,384]{1,0:T(8,128)(2,1)S(1)}, bf16[256,384]{1,0:T(8,128)(2,1)S(1)}, u32[]{:S(2)}, u32[]{:S(2)}) %collective-permute-start.9) | collective-permute-done | bytes 196640 | tf_op jit(solution)/shard_map/ppermute | solution.py:403
  104.5 0.1 fusion.19
  104.7 0.4 fusion.34
  105.1 0.2 fusion.33
  105.4 3.4 %collective-permute-start.11 = (bf16[160,384]{1,0:T(8,128)(2,1)S(1)}, bf16[160,384]{1,0:T(8,128)(2,1)S(1)}, u32[]{:S(2)}, u32[]{:S(2)}) collective-permute-start(bf16[160,384]{1,0:T(8,128)(2,1)S(1)} %reshape.180.frame_ref), channel_id=1, source_target_pairs={{16,0},{32,16},{48,32},{64,48},{80,64},{96,80},{112,96},{128,112},... | collective-permute-start | bytes 368648 | tf_op jit(solution)/shard_map/ppermute | solution.py:316
  108.9 2.1 %collective-permute-start.10 = (bf16[160,384]{1,0:T(8,128)(2,1)S(1)}, bf16[160,384]{1,0:T(8,128)(2,1)S(1)}, u32[]{:S(2)}, u32[]{:S(2)}) collective-permute-start(bf16[160,384]{1,0:T(8,128)(2,1)S(1)} %reshape.180.frame_ref), channel_id=1, source_target_pairs={{32,0},{48,16},{64,32},{80,48},{96,64},{112,80},{128,96},{144,112}... | collective-permute-start | bytes 368648 | tf_op jit(solution)/shard_map/ppermute | solution.py:316
  111.1 2.6 %back_own.1.start_ref = f32[128,384]{1,0:T(8,128)S(1)} custom-call(s32[1]{0:T(128)} %bitcast.core_ref, bf16[160,384]{1,0:T(8,128)(2,1)S(1)} %reshape.180.frame_ref, bf16[27,384,384]{2,1,0:T(8,128)(2,1)} %bitcast.114, bf16[27,384,384]{2,1,0:T(8,128)(2,1)} %collective-permute-done.12.other_ref), custom_call_target="tpu_custom_call" | custom-call | flops 339738624 | bytes 2654208 | tf_op jit(solution)/shard_map/back_own/pallas_call | solution.py:170
  113.7 3.4 %collective-permute-done.10.late_ref = bf16[160,384]{1,0:T(8,128)(2,1)S(1)} collective-permute-done((bf16[160,384]{1,0:T(8,128)(2,1)S(1)}, bf16[160,384]{1,0:T(8,128)(2,1)S(1)}, u32[]{:S(2)}, u32[]{:S(2)}) %collective-permute-start.10) | collective-permute-done | bytes 122912 | tf_op jit(solution)/shard_map/ppermute | solution.py:316
  117.1 7.3 %back_rest.1 = (bf16[128,384]{1,0:T(8,128)(2,1)S(1)}, bf16[2048,384]{1,0:T(8,128)(2,1)}) custom-call(s32[1]{0:T(128)} %bitcast.core_ref, s32[1]{0:T(128)} %bitcast.1.col_ref, bf16[160,384]{1,0:T(8,128)(2,1)S(1)} %collective-permute-done.10.late_ref, bf16[160,384]{1,0:T(8,128)(2,1)S(1)} %collective-permute-done.11.soon_ref, bf16[27,384,384]{2,1,0:T(8,128)(2,1)} %bitcast.115, ...), custom_call_target="tpu_custom_call" | custom-call | flops 1686110208 | bytes 11599872 | tf_op jit(solution)/shard_map/back_rest/pallas_call | solution.py:263
  124.4 5.3 %all-to-all-start.2 = ((bf16[32,64,384]{2,1,0:T(8,128)(2,1)}), bf16[32,64,384]{2,1,0:T(8,128)(2,1)S(1)}, u32[]{:S(2)}, u32[]{:S(2)}) async-start(bf16[32,64,384]{2,1,0:T(8,128)(2,1)} %bitcast.119), calls=%async_computation.2 | async-start | bytes 3145728 | tf_op jit(solution)/shard_map/all_to_all | solution.py:428
  129.7 1.3 collective-permute-start.13
  131.0 16.1 %collective-permute-done.13 = bf16[8,8,384]{2,1,0:T(8,128)(2,1)S(1)} collective-permute-done((bf16[8,8,384]{2,1,0:T(8,128)(2,1)S(1)}, bf16[8,8,384]{2,1,0:T(8,128)(2,1)S(1)}, u32[]{:S(2)}, u32[]{:S(2)}) %collective-permute-start.13) | collective-permute-done | bytes 49184 | tf_op jit(solution)/shard_map/ppermute | solution.py:426
  147.1 2.3 %all-to-all-done.2 = bf16[32,64,384]{2,1,0:T(8,128)(2,1)S(1)} async-done(((bf16[32,64,384]{2,1,0:T(8,128)(2,1)}), bf16[32,64,384]{2,1,0:T(8,128)(2,1)S(1)}, u32[]{:S(2)}, u32[]{:S(2)}) %all-to-all-start.2) | async-done | bytes 1572896 | tf_op jit(solution)/shard_map/all_to_all | solution.py:428
  149.5 0.2 convert_reduce_fusion
  149.7 0.1 fusion.37
  149.8 0.8 fusion.40
  (64 shorter events, 0.6 us)
Async XLA Ops:
  6.5 49.5 %copy-start = (bf16[384,384]{1,0:T(8,128)(2,1)S(1)}, bf16[384,384]{1,0:T(8,128)(2,1)}, u32[]{:S(2)}) copy-start(bf16[384,384]{1,0:T(8,128)(2,1)} %param.15) | copy-start | bytes 884740
  6.5 2.0 %copy-start.7 = (bf16[2,8,8,384]{3,2,1,0:T(8,128)(2,1)S(1)}, bf16[2,8,8,384]{3,2,1,0:T(8,128)(2,1)}, u32[]{:S(2)}) copy-start(bf16[2,8,8,384]{3,2,1,0:T(8,128)(2,1)} %param.11) | copy-start | bytes 294916
  6.5 84.8 %all-gather.2.cloned.1.call-start = ((), (), s32[]{:S(2)}) async-start(), calls=%async_computation.3 | async-start | bytes 8460288 | tf_op jit(solution)/shard_map/all_gather | solution.py:318
  8.6 4.0 %collective-permute-start = (bf16[8,8,384]{2,1,0:T(8,128)(2,1)S(1)}, bf16[8,8,384]{2,1,0:T(8,128)(2,1)S(1)}, u32[]{:S(2)}, u32[]{:S(2)}) collective-permute-start(bf16[8,8,384]{2,1,0:T(8,128)(2,1)S(1)} %dynamic-slice_bitcast_fusion.5), channel_id=1, source_target_pairs={{0,16},{16,0},{1,17},{17,1},{2,18},{18,2},{3,19},{19,3},{4,20},{20... | collective-permute-start | bytes 147464 | tf_op jit(solution)/shard_map/ppermute | solution.py:324
  24.2 4.3 %copy-start.11 = (bf16[2,8,8,384]{3,2,1,0:T(8,128)(2,1)S(1)}, bf16[2,8,8,384]{3,2,1,0:T(8,128)(2,1)}, u32[]{:S(2)}) copy-start(bf16[2,8,8,384]{3,2,1,0:T(8,128)(2,1)} %param.12) | copy-start | bytes 294916
  24.2 30.0 %all-to-all-start.1 = ((bf16[4,4,128,384]{3,2,1,0:T(8,128)(2,1)}), bf16[4,4,128,384]{3,2,1,0:T(8,128)(2,1)S(1)}, u32[]{:S(2)}, u32[]{:S(2)}) async-start(bf16[4,4,128,384]{3,2,1,0:T(8,128)(2,1)} %broadcast_in_dim.34), calls=%async_computation.1 | async-start | bytes 3145728 | tf_op jit(solution)/shard_map/all_to_all | solution.py:332
  28.5 3.4 %collective-permute-start.3 = (bf16[8,8,384]{2,1,0:T(8,128)(2,1)S(1)}, bf16[8,8,384]{2,1,0:T(8,128)(2,1)S(1)}, u32[]{:S(2)}, u32[]{:S(2)}) collective-permute-start(bf16[8,8,384]{2,1,0:T(8,128)(2,1)S(1)} %dynamic-slice_bitcast_fusion.4), channel_id=1, source_target_pairs={{0,16},{16,0},{1,17},{17,1},{2,18},{18,2},{3,19},{19,3},{4,20},{20... | collective-permute-start | bytes 147464 | tf_op jit(solution)/shard_map/ppermute | solution.py:381
  32.1 3.6 %collective-permute-start.4 = (bf16[16,2,384]{2,1,0:T(2,128)(2,1)S(1)}, bf16[16,2,384]{2,1,0:T(2,128)(2,1)S(1)}, u32[]{:S(2)}, u32[]{:S(2)}) collective-permute-start(bf16[16,2,384]{2,1,0:T(2,128)(2,1)S(1)} %get-tuple-element.34), channel_id=1, source_target_pairs={{0,1},{1,2},{2,3},{3,4},{4,5},{5,6},{6,7},{7,8},{8,9},{9,10},{10,1... | collective-permute-start | bytes 73736 | tf_op jit(solution)/shard_map/ppermute | solution.py:387
  34.3 5.0 %collective-permute-start.5 = (bf16[16,2,384]{2,1,0:T(2,128)(2,1)S(1)}, bf16[16,2,384]{2,1,0:T(2,128)(2,1)S(1)}, u32[]{:S(2)}, u32[]{:S(2)}) collective-permute-start(bf16[16,2,384]{2,1,0:T(2,128)(2,1)S(1)} %get-tuple-element.35), channel_id=1, source_target_pairs={{1,0},{2,1},{3,2},{4,3},{5,4},{6,5},{7,6},{8,7},{9,8},{10,9},{11,1... | collective-permute-start | bytes 73736 | tf_op jit(solution)/shard_map/ppermute | solution.py:389
  40.1 37.8 %collective-permute-start.7 = (bf16[256,384]{1,0:T(8,128)(2,1)}, bf16[256,384]{1,0:T(8,128)(2,1)}, u32[]{:S(2)}, u32[]{:S(2)}) collective-permute-start(bf16[256,384]{1,0:T(8,128)(2,1)} %bitcast.18), channel_id=1, source_target_pairs={{32,0},{48,16},{64,32},{80,48},{96,64},{112,80},{128,96},{144,112}... | collective-permute-start | bytes 589832 | tf_op jit(solution)/shard_map/ppermute | solution.py:316
  47.1 30.8 %collective-permute-start.6 = (bf16[256,384]{1,0:T(8,128)(2,1)}, bf16[256,384]{1,0:T(8,128)(2,1)}, u32[]{:S(2)}, u32[]{:S(2)}) collective-permute-start(bf16[256,384]{1,0:T(8,128)(2,1)} %bitcast.18), channel_id=1, source_target_pairs={{16,0},{32,16},{48,32},{64,48},{80,64},{96,80},{112,96},{128,112},... | collective-permute-start | bytes 589832 | tf_op jit(solution)/shard_map/ppermute | solution.py:316
  50.7 4.5 %copy-start.12 = (f32[384]{0:T(512)S(1)}, f32[384]{0:T(512)}, u32[]{:S(2)}) copy-start(f32[384]{0:T(512)} %param.13) | copy-start | bytes 4612
  54.3 1.0 copy-start.2
  57.2 20.1 %copy-start.5 = (bf16[2048,384]{1,0:T(8,128)(2,1)}, bf16[2048,384]{1,0:T(8,128)(2,1)S(1)}, u32[]{:S(2)}) copy-start(bf16[2048,384]{1,0:T(8,128)(2,1)S(1)} %convolution_convert_fusion.1.keys_from) | copy-start | bytes 4718596
  57.9 1.4 copy-start.6
  58.0 1.7 %copy-start.1 = (bf16[384,384]{1,0:T(8,128)(2,1)S(1)}, bf16[384,384]{1,0:T(8,128)(2,1)}, u32[]{:S(2)}) copy-start(bf16[384,384]{1,0:T(8,128)(2,1)} %w_value_ref.1) | copy-start | bytes 884740
  59.7 2.3 %copy-start.3 = (bf16[384,384]{1,0:T(8,128)(2,1)S(1)}, bf16[384,384]{1,0:T(8,128)(2,1)}, u32[]{:S(2)}) copy-start(bf16[384,384]{1,0:T(8,128)(2,1)} %w_out_ref.1) | copy-start | bytes 884740
  62.0 3.8 %copy-start.13 = (f32[384]{0:T(512)S(1)}, f32[384]{0:T(512)}, u32[]{:S(2)}) copy-start(f32[384]{0:T(512)} %param.18) | copy-start | bytes 4612
  65.8 14.2 %copy-start.9 = (bf16[1,16,16,384]{3,2,1,0:T(8,128)(2,1)S(1)}, bf16[1,16,16,384]{3,2,1,0:T(8,128)(2,1)}, u32[]{:S(2)}) copy-start(bf16[1,16,16,384]{3,2,1,0:T(8,128)(2,1)} %fusion.64) | copy-start | bytes 589828
  67.0 10.9 %collective-permute-start.2 = (bf16[256,384]{1,0:T(8,128)(2,1)S(1)}, bf16[256,384]{1,0:T(8,128)(2,1)S(1)}, u32[]{:S(2)}, u32[]{:S(2)}) collective-permute-start(bf16[256,384]{1,0:T(8,128)(2,1)S(1)} %fusion.18), channel_id=1, source_target_pairs={{0,16},{16,32},{32,48},{48,64},{64,80},{80,96},{96,112},{112,128},... | collective-permute-start | bytes 589832 | tf_op jit(solution)/shard_map/ppermute | solution.py:316
  70.0 9.9 %collective-permute-start.1 = (bf16[256,384]{1,0:T(8,128)(2,1)S(1)}, bf16[256,384]{1,0:T(8,128)(2,1)S(1)}, u32[]{:S(2)}, u32[]{:S(2)}) collective-permute-start(bf16[256,384]{1,0:T(8,128)(2,1)S(1)} %fusion.18), channel_id=1, source_target_pairs={{0,32},{16,48},{32,64},{48,80},{64,96},{80,112},{96,128},{112,144}... | collective-permute-start | bytes 589832 | tf_op jit(solution)/shard_map/ppermute | solution.py:316
  81.2 2.2 %collective-permute-start.8 = (bf16[3,18,16,384]{3,2,1,0:T(8,128)(2,1)S(1)}, bf16[3,18,16,384]{3,2,1,0:T(8,128)(2,1)S(1)}, u32[]{:S(2)}, u32[]{:S(2)}) collective-permute-start(bf16[3,18,16,384]{3,2,1,0:T(8,128)(2,1)S(1)} %get-tuple-element.27), channel_id=1, source_target_pairs={{0,32},{32,0},{64,96},{96,64},{128,160},{160,128},{192,224},{224,1... | collective-permute-start | bytes 1990664 | tf_op jit(solution)/shard_map/ppermute | solution.py:397
  91.4 19.7 %collective-permute-start.12 = (bf16[27,384,384]{2,1,0:T(8,128)(2,1)}, bf16[27,384,384]{2,1,0:T(8,128)(2,1)}, u32[]{:S(2)}, u32[]{:S(2)}) collective-permute-start(bf16[27,384,384]{2,1,0:T(8,128)(2,1)} %bitcast.112), channel_id=1, source_target_pairs={{0,32},{32,0},{64,96},{96,64},{128,160},{160,128},{192,224},{224,1... | collective-permute-start | bytes 23887880 | tf_op jit(solution)/shard_map/ppermute | solution.py:400
  99.6 5.0 %copy-start.14 = (f32[384]{0:T(512)S(1)}, f32[384]{0:T(512)}, u32[]{:S(2)}) copy-start(f32[384]{0:T(512)} %param.19) | copy-start | bytes 4612
  99.7 4.8 %collective-permute-start.9 = (bf16[256,384]{1,0:T(8,128)(2,1)S(1)}, bf16[256,384]{1,0:T(8,128)(2,1)S(1)}, u32[]{:S(2)}, u32[]{:S(2)}) collective-permute-start(bf16[256,384]{1,0:T(8,128)(2,1)S(1)} %bitcast.125), channel_id=1, source_target_pairs={{0,32},{32,0},{64,96},{96,64},{128,160},{160,128},{192,224},{224,1... | collective-permute-start | bytes 589832 | tf_op jit(solution)/shard_map/ppermute | solution.py:403
  99.8 11.2 %copy-start.10 = (bf16[256,384]{1,0:T(8,128)(2,1)S(1)}, bf16[256,384]{1,0:T(8,128)(2,1)}, u32[]{:S(2)}) copy-start(bf16[256,384]{1,0:T(8,128)(2,1)} %get-tuple-element.43) | copy-start | bytes 589828
  105.4 8.3 %collective-permute-start.11 = (bf16[160,384]{1,0:T(8,128)(2,1)S(1)}, bf16[160,384]{1,0:T(8,128)(2,1)S(1)}, u32[]{:S(2)}, u32[]{:S(2)}) collective-permute-start(bf16[160,384]{1,0:T(8,128)(2,1)S(1)} %reshape.180.frame_ref), channel_id=1, source_target_pairs={{16,0},{32,16},{48,32},{64,48},{80,64},{96,80},{112,96},{128,112},... | collective-permute-start | bytes 368648 | tf_op jit(solution)/shard_map/ppermute | solution.py:316
  108.9 8.2 %collective-permute-start.10 = (bf16[160,384]{1,0:T(8,128)(2,1)S(1)}, bf16[160,384]{1,0:T(8,128)(2,1)S(1)}, u32[]{:S(2)}, u32[]{:S(2)}) collective-permute-start(bf16[160,384]{1,0:T(8,128)(2,1)S(1)} %reshape.180.frame_ref), channel_id=1, source_target_pairs={{32,0},{48,16},{64,32},{80,48},{96,64},{112,80},{128,96},{144,112}... | collective-permute-start | bytes 368648 | tf_op jit(solution)/shard_map/ppermute | solution.py:316
  111.1 6.0 %copy-start.4 = (bf16[384,384]{1,0:T(8,128)(2,1)S(1)}, bf16[384,384]{1,0:T(8,128)(2,1)}, u32[]{:S(2)}) copy-start(bf16[384,384]{1,0:T(8,128)(2,1)} %w_out_ref.1) | copy-start | bytes 884740
  124.4 25.1 %all-to-all-start.2 = ((bf16[32,64,384]{2,1,0:T(8,128)(2,1)}), bf16[32,64,384]{2,1,0:T(8,128)(2,1)S(1)}, u32[]{:S(2)}, u32[]{:S(2)}) async-start(bf16[32,64,384]{2,1,0:T(8,128)(2,1)} %bitcast.119), calls=%async_computation.2 | async-start | bytes 3145728 | tf_op jit(solution)/shard_map/all_to_all | solution.py:428
  129.6 20.1 %copy-start.8 = (bf16[2,8,8,384]{3,2,1,0:T(8,128)(2,1)S(1)}, bf16[2,8,8,384]{3,2,1,0:T(8,128)(2,1)}, u32[]{:S(2)}) copy-start(bf16[2,8,8,384]{3,2,1,0:T(8,128)(2,1)} %param.11) | copy-start | bytes 294916
  129.7 17.4 %collective-permute-start.13 = (bf16[8,8,384]{2,1,0:T(8,128)(2,1)S(1)}, bf16[8,8,384]{2,1,0:T(8,128)(2,1)S(1)}, u32[]{:S(2)}, u32[]{:S(2)}) collective-permute-start(bf16[8,8,384]{2,1,0:T(8,128)(2,1)S(1)} %dynamic-slice_bitcast_fusion.3), channel_id=1, source_target_pairs={{0,16},{16,0},{1,17},{17,1},{2,18},{18,2},{3,19},{19,3},{4,20},{20... | collective-permute-start | bytes 147464 | tf_op jit(solution)/shard_map/ppermute | solution.py:426
Sparse Core Ops, SparseCore 0:
  9.8 81.4 all-gather.1
